TPU v7x, 32 devices: a whole 2x2x4 slice. The times are simulated.
32 devices in a mesh: dp: 8 (over z, y), tensor: 4 (over x, core).
Axes of the slice: x: 2, y: 2, z: 4, core: 2. Of those that a mesh axis runs over, the one named last changes fastest.
Arguments:
- grad_query: bfloat16 [8, 1, 4096, 4608], P('dp', None, 'tensor'), may hold values from -33 to 33
- grad_key: bfloat16 [8, 1, 2048, 4608], P('dp', None, 'tensor'), may hold values from -33 to 33
- error_query: bfloat16 [8, 1, 4096, 4608], P('dp', None, 'tensor'), may hold values from -12 to 12
- error_key: bfloat16 [8, 1, 2048, 4608], P('dp', None, 'tensor'), may hold values from -12 to 12
- factor_query: bfloat16 [1, 4608, 64], replicated, may hold values from -0.09375 to 0.09375
- factor_key: bfloat16 [1, 4608, 64], replicated, may hold values from -0.09375 to 0.09375
Outputs:
- error_query_new: bfloat16 [8, 1, 4096, 4608], P('dp', None, 'tensor')
- error_key_new: bfloat16 [8, 1, 2048, 4608], P('dp', None, 'tensor')
- factor_query_new: bfloat16 [1, 4608, 64], replicated
- factor_key_new: bfloat16 [1, 4608, 64], replicated
All inputs are finite; a program needn't handle non-finite values.
Results may differ from a plain program's by a relative error of at most 0.0085.
Values may be sent and summed in bfloat16 or wider, within the bound.
No kernel may reach another device: no remote copies, remote signals or barrier semaphores. Data moves between devices by JAX's collectives and lax.ppermute only.
A program may use at most 128 MiB of HBM per device.

v0:
```python
import jax
import jax.numpy as jnp
from jax import lax
from jax.sharding import PartitionSpec as P


def merged_rows(grad, error):
    return (grad[0].astype(jnp.float32) + error[0].astype(jnp.float32)).astype(jnp.bfloat16)


def images(merged, factor):
    return jnp.einsum("lhd,ldr->lhr", merged, factor, preferred_element_type=jnp.float32)


def gram_of(field):
    return jnp.einsum("lhr,lhs->lrs", field, field, precision=lax.Precision.HIGHEST)


def orthonormal(field, gram):
    lower = jnp.linalg.cholesky(gram)
    solved = jax.scipy.linalg.solve_triangular(lower, jnp.swapaxes(field, 1, 2), lower=True)
    return jnp.swapaxes(solved, 1, 2).astype(jnp.bfloat16)


def projected(merged, basis):
    return jnp.einsum("lhd,lhr->ldr", merged, basis, preferred_element_type=jnp.float32)


def body(grad_query, grad_key, error_query, error_key, factor_query, factor_key):
    replicas = lax.axis_size("dp")
    merged_q = merged_rows(grad_query, error_query)
    merged_k = merged_rows(grad_key, error_key)
    image_q = images(merged_q, factor_query)
    image_k = images(merged_k, factor_key)
    image_q, image_k = lax.psum((image_q, image_k), "dp")
    gram_q, gram_k = lax.psum((gram_of(image_q), gram_of(image_k)), "tensor")
    basis_q = orthonormal(image_q, gram_q)
    basis_k = orthonormal(image_k, gram_k)
    summed_q, summed_k = lax.psum(
        (projected(merged_q, basis_q), projected(merged_k, basis_k)), ("dp", "tensor")
    )
    new_q = summed_q.astype(jnp.bfloat16)
    new_k = summed_k.astype(jnp.bfloat16)

    def refresh(merged, basis, factor):
        approx = jnp.einsum("lhr,ldr->lhd", basis, factor, preferred_element_type=jnp.float32)
        return (merged.astype(jnp.float32) - approx / replicas).astype(jnp.bfloat16)[None]

    return (refresh(merged_q, basis_q, new_q), refresh(merged_k, basis_k, new_k), new_q, new_k)


def solution(mesh):
    placed = (
        P("dp", None, "tensor", None),
        P("dp", None, "tensor", None),
        P("dp", None, "tensor", None),
        P("dp", None, "tensor", None),
        P(),
        P(),
    )
    return jax.shard_map(
        body,
        mesh=mesh,
        in_specs=placed,
        out_specs=(P("dp", None, "tensor", None), P("dp", None, "tensor", None), P(), P()),
        check_vma=False,
    )
```

profile of v0, /device:TPU:0, one launch (start us, length us, event | category | flops | bytes accessed | tf_op | source)
XLA Modules:
  0.0 246.4 jit_solution(16198099852077080777)
XLA Ops:
  7.2 0.0 copy-start
  7.2 0.0 copy-start.5
  7.2 0.0 all-reduce.6.cloned.1.call-start
  7.2 1.0 copy-done
  8.2 0.0 copy-start.1
  8.2 0.0 copy-start.2
  8.2 10.2 %convolution_bitcast_fusion.2 = f32[1,1024,64]{1,2,0:T(8,128)} fusion(bf16[1,4608,64]{1,2,0:T(8,128)(2,1)S(1)} %copy-done, bf16[1,1,1024,4608]{3,2,1,0:T(8,128)(2,1)} %param.9, bf16[1,1,1024,4608]{3,2,1,0:T(8,128)(2,1)} %param.7), kind=kOutput, calls=%fused_computation.10 | convolution fusion | flops 622854144 | bytes 19726336 | tf_op jit(solution)/shard_map/lhd,ldr->lhr/dot_general | solution.py:12
  18.4 0.0 copy-done.5
  18.4 0.0 copy-done.1
  18.4 0.0 copy-done.2
  18.5 2.2 convolution_bitcast_fusion.3
  20.7 0.0 all-reduce.6.cloned.1.call-update
  20.7 74.4 %all-reduce.6.cloned.1.call-done = (f32[1,1024,64]{1,2,0:T(8,128)}, f32[1,512,64]{1,2,0:T(8,128)}) async-done(((f32[1,1024,64]{1,2,0:T(8,128)}, f32[1,512,64]{1,2,0:T(8,128)}), (f32[1,1024,64]{1,2,0:T(8,128)}, f32[1,512,64]{1,2,0:T(8,128)})) %all-reduce.6.cloned.1.call-update) | async-done | bytes 393232 | tf_op jit(solution)/shard_map/psum | solution.py:35
  95.1 0.0 copy-start.4
  95.1 1.3 convolution_bitcast_fusion.4
  96.4 1.4 convolution_bitcast_fusion.5
  97.8 10.9 %all-reduce.2 = (f32[1,64,64]{1,2,0:T(8,128)S(1)}, f32[1,64,64]{1,2,0:T(8,128)S(1)}) all-reduce(f32[1,64,64]{1,2,0:T(8,128)S(1)} %convolution_bitcast_fusion.5, f32[1,64,64]{1,2,0:T(8,128)S(1)} %convolution_bitcast_fusion.4), channel_id=1, replica_groups=mesh['dp'=8,'tensor'=4] {'tensor'}, use_global_device_ids=true, to_apply=%region_1.0 | all-reduce | flops 8192 | bytes 65536 | tf_op jit(solution)/shard_map/psum | solution.py:36
  108.6 0.1 copy.11
  108.7 0.1 copy.13
  108.8 5.8 %custom-call.15 = f32[1,64,64]{2,1,0:T(8,128)S(1)} custom-call(f32[1,64,64]{2,1,0:T(8,128)S(1)} %get-tuple-element.11), custom_call_target="Cholesky" | custom-call | tf_op jit(solution)/shard_map/jit(cholesky)/cholesky | solution.py:20
  114.7 0.6 compare_reduce_fusion
  115.4 0.7 select_select_fusion
  116.0 4.9 %custom-call.12 = f32[1,64,64]{1,2,0:T(8,128)S(1)} custom-call(f32[1,64,64]{2,1,0:T(8,128)S(1)} %select_select_fusion), custom_call_target="InvertDiagBlocksLowerTriangular" | custom-call | tf_op jit(solution)/shard_map/jit(_solve_triangular)/triangular_solve | solution.py:21
  120.9 1.2 fusion.5
  122.2 5.2 %convolution_bitcast_fusion = f32[1,4608,64]{1,2,0:T(8,128)S(1)} fusion(bf16[512,64]{0,1:T(8,128)(2,1)S(1)} %fusion.5, bf16[1,1,512,4608]{3,2,1,0:T(8,128)(2,1)} %param.10, bf16[1,1,512,4608]{3,2,1,0:T(8,128)(2,1)} %param.8), kind=kOutput, calls=%fused_computation.7 | convolution fusion | flops 311427072 | bytes 10682368 | tf_op jit(solution)/shard_map/lhd,lhr->ldr/dot_general | solution.py:26
  127.3 5.9 %custom-call.14 = f32[1,64,64]{2,1,0:T(8,128)S(1)} custom-call(f32[1,64,64]{2,1,0:T(8,128)S(1)} %get-tuple-element.12), custom_call_target="Cholesky" | custom-call | tf_op jit(solution)/shard_map/jit(cholesky)/cholesky | solution.py:20
  133.2 0.6 compare_reduce_fusion.1
  133.9 0.7 select_select_fusion.1
  134.5 4.9 %custom-call.11 = f32[1,64,64]{1,2,0:T(8,128)S(1)} custom-call(f32[1,64,64]{2,1,0:T(8,128)S(1)} %select_select_fusion.1), custom_call_target="InvertDiagBlocksLowerTriangular" | custom-call | tf_op jit(solution)/shard_map/jit(_solve_triangular)/triangular_solve | solution.py:21
  139.4 0.0 copy-done.4
  139.4 0.4 fusion.4
  139.9 0.0 copy-start.3
  139.9 0.6 copy-done.3
  140.5 9.0 %convolution_bitcast_fusion.1 = f32[1,4608,64]{1,2,0:T(8,128)S(1)} fusion(bf16[1024,64]{0,1:T(8,128)(2,1)S(1)} %fusion.4, bf16[1,1,1024,4608]{3,2,1,0:T(8,128)(2,1)} %param.9, bf16[1,1,1024,4608]{3,2,1,0:T(8,128)(2,1)} %param.7), kind=kOutput, calls=%fused_computation.8 | convolution fusion | flops 622854144 | bytes 20185088 | tf_op jit(solution)/shard_map/lhd,lhr->ldr/dot_general | solution.py:26
  149.5 0.0 slice-start
  149.6 69.3 %all-reduce.7 = (bf16[1,4608,64]{1,2,0:T(8,128)(2,1)}, bf16[1,4608,64]{1,2,0:T(8,128)(2,1)}) all-reduce(f32[1,4608,64]{1,2,0:T(8,128)S(1)} %convolution_bitcast_fusion.1, f32[1,4608,64]{1,2,0:T(8,128)S(1)} %convolution_bitcast_fusion), channel_id=1, replica_groups=mesh['dp'=8,'tensor'=4] {'dp','tensor'}, use_global_device_ids=true, to_apply=%region_4.6 | all-reduce | flops 589824 | bytes 3538944 | tf_op jit(solution)/shard_map/psum | solution.py:39
  218.8 0.0 slice-start.1
  218.8 0.0 copy-start.6
  218.8 14.2 %fusion.1 = bf16[1,1,1024,4608]{3,2,1,0:T(8,128)(2,1)} fusion(bf16[1024,64]{0,1:T(8,128)(2,1)} %copy-done.3, bf16[1,4608,64]{1,2,0:T(8,128)(2,1)} %get-tuple-element.5, bf16[1,1,1024,4608]{3,2,1,0:T(8,128)(2,1)} %param.9, bf16[1,1,1024,4608]{3,2,1,0:T(8,128)(2,1)} %param.7), kind=kOutput, calls=%fused_computation.5 | convolution fusion | flops 641728512 | bytes 29032448 | tf_op jit(solution)/shard_map/lhr,ldr->lhd/dot_general | solution.py:46
  233.1 0.0 slice-done
  233.1 0.0 slice-done.1
  233.1 0.0 copy-done.6
  233.1 6.5 %fusion.2 = bf16[1,1,512,4608]{3,2,1,0:T(8,128)(2,1)} fusion(bf16[512,64]{0,1:T(8,128)(2,1)S(1)} %fusion.5, bf16[1,4608,64]{1,2,0:T(8,128)(2,1)S(1)} %copy-done.6, bf16[1,1,512,4608]{3,2,1,0:T(8,128)(2,1)S(1)} %bitcast.87, bf16[1,1,512,4608]{3,2,1,0:T(8,128)(2,1)} %param.8), kind=kOutput, calls=%fused_computation.6 | convolution fusion | flops 320864256 | bytes 14811136 | tf_op jit(solution)/shard_map/lhr,ldr->lhd/dot_general | solution.py:46
  (4 shorter events, 0.1 us)
Async XLA Ops:
  7.2 1.1 copy-start
  7.2 11.3 %copy-start.5 = (bf16[1,4608,64]{1,2,0:T(8,128)(2,1)S(1)}, bf16[1,4608,64]{1,2,0:T(8,128)(2,1)}, u32[]{:S(2)}) copy-start(bf16[1,4608,64]{1,2,0:T(8,128)(2,1)} %param.12) | copy-start | bytes 1769476
  7.2 87.9 %all-reduce.6.cloned.1.call-start = ((), (), s32[]{:S(2)}) async-start(), calls=%async_computation | async-start | bytes 786432 | tf_op jit(solution)/shard_map/psum | solution.py:35
  8.2 10.2 %copy-start.1 = (bf16[1,1,512,4608]{3,2,1,0:T(8,128)(2,1)S(1)}, bf16[1,1,512,4608]{3,2,1,0:T(8,128)(2,1)}, u32[]{:S(2)}) copy-start(bf16[1,1,512,4608]{3,2,1,0:T(8,128)(2,1)} %param.10) | copy-start | bytes 14155780
  8.2 10.2 %copy-start.2 = (bf16[1,1,512,4608]{3,2,1,0:T(8,128)(2,1)S(1)}, bf16[1,1,512,4608]{3,2,1,0:T(8,128)(2,1)}, u32[]{:S(2)}) copy-start(bf16[1,1,512,4608]{3,2,1,0:T(8,128)(2,1)} %param.8) | copy-start | bytes 14155780
  95.1 44.3 %copy-start.4 = (f32[1,1024,64]{1,2,0:T(8,128)S(1)}, f32[1,1024,64]{1,2,0:T(8,128)}, u32[]{:S(2)}) copy-start(f32[1,1024,64]{1,2,0:T(8,128)} %get-tuple-element.7) | copy-start | bytes 786436
  139.9 0.7 copy-start.3
  149.5 83.5 %slice-start = ((s8[4718592]{0:T(1024)(128)(4,1)}), s8[524288]{0:T(1024)(128)(4,1)S(1)}, s32[]{:S(2)}) async-start(s8[4718592]{0:T(1024)(128)(4,1)} %bitcast.86), calls=%async_computation.1 | async-start | bytes 1048576
  218.8 14.2 %slice-start.1 = ((s8[4718592]{0:T(1024)(128)(4,1)}), s8[4194304]{0:T(1024)(128)(4,1)S(1)}, s32[]{:S(2)}) async-start(s8[4718592]{0:T(1024)(128)(4,1)} %bitcast.86), calls=%async_computation.2 | async-start | bytes 8388608
  218.8 14.2 %copy-start.6 = (bf16[1,4608,64]{1,2,0:T(8,128)(2,1)S(1)}, bf16[1,4608,64]{1,2,0:T(8,128)(2,1)}, u32[]{:S(2)}) copy-start(bf16[1,4608,64]{1,2,0:T(8,128)(2,1)} %get-tuple-element.6) | copy-start | bytes 1769476
Sparse Core Ops, SparseCore 0:
  20.8 74.2 all-reduce.5
where the time goes:
time: 247 us; the launch traced here: 246 us
  blocking collectives  80.2 us (32%)
  waiting for transfers between devices  74.4 us (30%)
  matrix products  51.6 us (21%)
  other arithmetic  24.2 us (10%)
  between operations  14.2 us (6%)
    psum x1, waiting for transfers between devices, body(): image_q, image_k = lax.psum((image_q, image_k), 'dp')  74.4 us
    psum x1, blocking collectives, body(): lax.psum((projected(merged_q, basis_q), projected(merged_k, basis_k)), ('...  69.3 us
    dot_general x2, matrix products, refresh(): jnp.einsum('lhr,ldr->lhd', basis, factor, preferred_element_type=jnp.floa...  20.7 us
    dot_general x2, matrix products, projected(): jnp.einsum('lhd,lhr->ldr', merged, basis, preferred_element_type=jnp.floa...  14.2 us
    another operation x6, other arithmetic, orthonormal(): lower = jnp.linalg.cholesky(gram)  13 us
    dot_general x2, matrix products, images(): jnp.einsum('lhd,ldr->lhr', merged, factor, preferred_element_type=jnp.flo...  12.4 us
    another operation x4, other arithmetic, orthonormal(): jax.scipy.linalg.solve_triangular(lower, jnp.swapaxes(field, 1, 2), lower...  11.1 us
    psum x1, blocking collectives, body(): gram_q, gram_k = lax.psum((gram_of(image_q), gram_of(image_k)), 'tensor')  10.9 us
  transfers between devices with their start and end apart: 1, of which 1 were waited for; matrix products, arithmetic and copies ran while one was open for 0% of the time, Pallas kernels for 0%

commit v1 on v0

v1 whole, which is shorter than its diff:
```python
import functools

import jax
import jax.numpy as jnp
from jax import lax
from jax.experimental import pallas as pl
from jax.experimental.pallas import tpu as pltpu
from jax.sharding import PartitionSpec as P

F32, BF16 = jnp.float32, jnp.bfloat16
MIB = 1 << 20
EXACT = lax.Precision.HIGHEST
LANES = 128


def wide(a):
    return a.astype(F32)


def vmem(shape, dtype):
    return pltpu.VMEM(tuple(shape), dtype)


def whole():
    return pl.BlockSpec(memory_space=pltpu.VMEM)


def local(kernel, ins, outs, scratch=(), limit=8, flops=0, after=()):
    ins = [pltpu.with_memory_space_constraint(a, pltpu.VMEM) for a in ins]
    moved = sum(a.size * a.dtype.itemsize for a in ins)
    n_in, n_after = len(ins), len(after)

    def run(*refs):
        kernel(*refs[:n_in], *refs[n_in + n_after :])

    return pl.pallas_call(
        run,
        in_specs=[whole()] * n_in + [pl.BlockSpec(memory_space=pl.ANY)] * n_after,
        out_specs=[whole()] * len(outs),
        out_shape=list(outs),
        scratch_shapes=list(scratch),
        compiler_params=pltpu.CompilerParams(vmem_limit_bytes=limit * MIB),
        cost_estimate=pl.CostEstimate(flops=flops, bytes_accessed=moved, transcendentals=0),
    )(*ins, *after)


class Ring:
    def __init__(self, axis, total, stride, size):
        self.axis, self.total, self.stride, self.size = axis, total, stride, size
        self.pairwise = size & (size - 1) == 0

    def pos(self):
        return lax.rem(lax.div(lax.axis_index(self.axis), self.stride), self.size)

    def to(self, step):
        if self.pairwise:
            return lax.bitwise_xor(self.pos(), step)
        return lax.rem(self.pos() + step, self.size)

    def source(self, step):
        if self.pairwise:
            return lax.bitwise_xor(self.pos(), step)
        return lax.rem(self.pos() + (self.size - step), self.size)

    def send(self, x, step):
        pairs = []
        for src in range(self.total):
            p = (src // self.stride) % self.size
            q = p ^ step if self.pairwise else (p + step) % self.size
            pairs.append((src, src + (q - p) * self.stride))
        return lax.ppermute(x, self.axis, pairs)

    def scatter(self, parts):
        return [self.send(x, s + 1) for s, x in enumerate(parts)]

    def gather(self, x):
        return [self.send(x, s) for s in range(1, self.size)]


def rows_at(index, size, align):
    return pl.ds(pl.multiple_of(index * size, align), size)


def cut_into(held, base, share, ring, outs):
    size = share // ring.size
    for s, out in enumerate(outs):
        piece = held[pl.ds(pl.multiple_of(base + ring.to(s) * size, 8), size)]
        out[...] = piece.astype(out.dtype)


def image_kernel(rings, tile, depth, *refs):
    ins, outs, scratch = refs[:6], refs[6:-7], refs[-7:]
    grads, errors, factors = ins[0:2], ins[2:4], ins[4:6]
    merged, outs = outs[:2], outs[2:]
    arrived, flat_factors, natural, held, grad_sems, error_sems, factor_sems = scratch
    rank, d = flat_factors.shape[1:]
    tiles = [(m, i) for m in (0, 1) for i in range(grads[m].shape[0] // tile)]

    def copies(n):
        m, i = tiles[n]
        rows = pl.ds(i * tile, tile)
        return (
            pltpu.make_async_copy(grads[m].at[rows], merged[m].at[rows], grad_sems.at[n]),
            pltpu.make_async_copy(errors[m].at[rows], arrived.at[n], error_sems.at[n]),
        )

    def factor_copy(m):
        return pltpu.make_async_copy(factors[m], flat_factors.at[m], factor_sems.at[m])

    def start(n):
        for c in copies(n):
            c.start()

    factor_copy(0).start()
    for n in range(min(depth, len(tiles))):
        start(n)
        if n == 0:
            factor_copy(1).start()
    for m in range(2):
        factor_copy(m).wait()
        for t in range(0, d, LANES):
            natural[m, t : t + LANES] = wide(flat_factors[m, :, t : t + LANES]).T.astype(BF16)
    chunk = 512 if d % 512 == 0 else d
    for n, (m, i) in enumerate(tiles):
        for c in copies(n):
            c.wait()
        if n + depth < len(tiles):
            start(n + depth)
        rows = pl.ds(i * tile, tile)
        image = jnp.zeros((tile, rank), F32)
        for c in range(0, d, chunk):
            cols = pl.ds(c, chunk)
            x = (wide(merged[m][rows, cols]) + wide(arrived[n, :, cols])).astype(BF16)
            merged[m][rows, cols] = x
            image += jnp.dot(x, natural[m, cols], preferred_element_type=F32)
        held[n * rank : (n + 1) * rank] = image.T
    used = len(tiles) * rank
    if used < held.shape[0]:
        held[used:] = jnp.zeros((held.shape[0] - used, held.shape[1]), F32)
    share = held.shape[0] // len(rings)
    for r, ring in enumerate(rings):
        cut_into(held, r * share, share, ring, outs[: ring.size])
        outs = outs[ring.size :]


def images(rings, flat, grads, errors, factors):
    rows = [g.shape[0] for g in grads]
    d = grads[0].shape[1]
    rank = factors[0].shape[0]
    tile = LANES
    count = sum(rows) // tile
    ins = [pltpu.with_memory_space_constraint(a, pltpu.HBM) for a in (*grads, *errors, *factors)]
    outs = [vmem((r, d), BF16) for r in rows]
    for ring in rings:
        outs += [vmem((flat // len(rings) // ring.size, LANES), F32)] * ring.size
    got = pl.pallas_call(
        functools.partial(image_kernel, rings, tile, 4),
        in_specs=[pl.BlockSpec(memory_space=pltpu.HBM)] * len(ins),
        out_specs=[whole()] * len(outs),
        out_shape=outs,
        scratch_shapes=[
            vmem((count, tile, d), BF16),
            vmem((2, rank, d), BF16),
            vmem((2, d, rank), BF16),
            vmem((flat, LANES), F32),
            pltpu.SemaphoreType.DMA((count,)),
            pltpu.SemaphoreType.DMA((count,)),
            pltpu.SemaphoreType.DMA((2,)),
        ],
        compiler_params=pltpu.CompilerParams(vmem_limit_bytes=24 * MIB),
        cost_estimate=pl.CostEstimate(
            flops=2 * sum(rows) * d * 256, bytes_accessed=4 * sum(rows) * d, transcendentals=0
        ),
    )(*ins)
    merged, got = got[:2], list(got[2:])
    cuts = []
    for ring in rings:
        cuts.append((got[0], got[1 : ring.size]))
        got = got[ring.size :]
    return merged, cuts


def total_kernel(counts, *refs):
    ins, outs = list(refs[: sum(counts)]), refs[sum(counts) :]
    for count, out in zip(counts, outs):
        total = ins.pop(0)[...]
        for _ in range(count - 1):
            total = total + ins.pop(0)[...]
        out[...] = total


def assemble_kernel(rings, rank, rows, *refs):
    n_in = sum(r.size for r in rings)
    ins, (image_q, image_k, halves_q, halves_k, gram, held) = list(refs[:n_in]), refs[n_in:]
    share = held.shape[0] // len(rings)
    for r, ring in enumerate(rings):
        size = share // ring.size
        for s in range(ring.size):
            at = pl.multiple_of(r * share + ring.source(s) * size, 8)
            held[pl.ds(at, size)] = ins.pop(0)[...]
    n = 0
    for m, (image_out, halves) in enumerate(((image_q, halves_q), (image_k, halves_k))):
        count = rows[m] // LANES
        blocks = [held[(n + i) * rank : (n + i + 1) * rank] for i in range(count)]
        image = jnp.concatenate(blocks, axis=1) if count > 1 else blocks[0]
        n += count
        image_out[...] = image
        high = image.astype(BF16)
        halves[:rank] = high
        halves[rank:] = (image - wide(high)).astype(BF16)
        gram[:, m * rank : (m + 1) * rank] = lax.dot_general(
            image, image, (((1,), (1,)), ((), ())), precision=EXACT, preferred_element_type=F32
        )


def project_kernel(core, other, half, tile, halves_q, halves_k, merged_q, merged_k, out):
    rank = halves_q.shape[0] // 2
    d = merged_q.shape[1]
    first = (core.to(1) if other else core.pos()) * half
    for t in range(half // tile):
        start = first + t * tile

        def fill(start=start, t=t):
            cols = pl.ds(pl.multiple_of(start, tile), tile)
            both = []
            for halves, merged in ((halves_q, merged_q), (halves_k, merged_k)):
                p = jnp.dot(halves[...], merged[:, cols], preferred_element_type=F32)
                both.append(p[:rank] + p[rank:])
            p = jnp.concatenate(both, axis=0)
            out[t * tile : (t + 1) * tile] = p.T.astype(out.dtype)

        if 2 * half == d:
            fill()
        else:
            pl.when(start < d)(fill)

            @pl.when(start >= d)
            def _(t=t):
                out[t * tile : (t + 1) * tile] = jnp.zeros((tile, out.shape[1]), out.dtype)


def project(core, other, half, halves_q, halves_k, merged_q, merged_k):
    d = merged_q.shape[1]
    tile = 768 if half % 768 == 0 and d % 768 == 0 else LANES
    rows = merged_q.shape[0] + merged_k.shape[0]
    return local(
        functools.partial(project_kernel, core, other, half, tile),
        [halves_q, halves_k, merged_q, merged_k],
        [vmem((half, halves_q.shape[0]), BF16 if other else F32)],
        limit=16,
        flops=rows * d * 256,
    )[0]


def inverse_kernel(ring, *refs):
    grams, (out, held) = refs[:-2], refs[-2:]
    rank = out.shape[0] // 2
    for s, g in enumerate(grams):
        held[ring.source(s)] = g[...]
    lane = lax.broadcasted_iota(jnp.int32, (8, 2 * rank), 1)
    sub = lax.broadcasted_iota(jnp.int32, (8, 2 * rank), 0)
    both = held[0]
    for j in range(1, len(grams)):
        both += held[j]
    systems = []
    for m in range(2):
        gram = both[:, m * rank : (m + 1) * rank]
        gram = jnp.concatenate([gram, jnp.zeros((rank, rank), F32)], axis=1)
        systems.append(
            [
                jnp.where(lane == sub + (rank + 8 * i), 1.0, gram[8 * i : 8 * i + 8])
                for i in range(rank // 8)
            ]
        )
    for j in range(rank):
        i0, k = divmod(j, 8)
        for rows in systems:
            pivot = jnp.broadcast_to(rows[i0][k : k + 1, :], (8, 2 * rank))
            scaled = pivot * (1.0 / jnp.broadcast_to(pivot[:, j : j + 1], (8, 2 * rank)))
            for i in range(i0, rank // 8):
                updated = rows[i] - rows[i][:, j : j + 1] * scaled
                rows[i] = jnp.where(sub > k, updated, rows[i]) if i == i0 else updated
    for m, rows in enumerate(systems):
        for i, row in enumerate(rows):
            diagonal = jnp.where(lane == sub + 8 * i, row, 0.0).sum(axis=1, keepdims=True)
            right = row[:, rank:] / jnp.sqrt(diagonal)
            zero = jnp.zeros_like(right)
            pair = [right, zero] if m == 0 else [zero, right]
            out[m * rank + 8 * i : m * rank + 8 * i + 8] = jnp.concatenate(pair, axis=1)


def basis_kernel(scale, inverse, image_q, image_k, basis_q, basis_k):
    rank = image_q.shape[0]
    for m, (image, basis) in enumerate(((image_q, basis_q), (image_k, basis_k))):
        inv = inverse[m * rank : (m + 1) * rank, m * rank : (m + 1) * rank]
        b = jnp.dot(inv, image[...], precision=EXACT, preferred_element_type=F32)
        basis[...] = (wide(b.astype(BF16)) * scale).T.astype(BF16)


def split_kernel(jobs, *refs):
    n_in = sum(1 + j[0] for j in jobs)
    ins, outs = list(refs[:n_in]), list(refs[n_in : -len(jobs)])
    scratch = refs[-len(jobs) :]
    for (received, cuts), held in zip(jobs, scratch):
        total = ins.pop(0)[...]
        for _ in range(received):
            total = total + wide(ins.pop(0)[...])
        held[...] = total
        share = held.shape[0] // len(cuts)
        for r, ring in enumerate(cuts):
            cut_into(held, r * share, share, ring, outs[: ring.size])
            outs = outs[ring.size :]


def split(jobs, sent=BF16, after=()):
    ins, outs, scratch, plan = [], [], [], []
    for kept, received, cuts in jobs:
        ins += [kept] + list(received)
        plan.append((len(received), cuts))
        scratch.append(vmem(kept.shape, F32))
        for ring in cuts:
            shape = (kept.shape[0] // len(cuts) // ring.size, kept.shape[1])
            outs += [vmem(shape, F32)] + [vmem(shape, sent)] * (ring.size - 1)
    got = list(local(functools.partial(split_kernel, plan), ins, outs, scratch, limit=10, after=after))
    result = []
    for _, _, cuts in jobs:
        for ring in cuts:
            result.append((got[0], got[1 : ring.size]))
            got = got[ring.size :]
    return result


def split_two_kernel(received_a, received_b, ring, *refs):
    n_in = 2 + received_a + received_b
    ins, outs = refs[:n_in], refs[n_in:-2]
    held_a, held_b = refs[-2:]
    a = ins[0][...]
    for r in ins[1 : 1 + received_a]:
        a = a + wide(r[...])
    b = ins[1 + received_a][...]
    for r in ins[2 + received_a :]:
        b = b + wide(r[...])
    held_a[...] = a
    held_b[...] = b
    size = held_a.shape[0] // ring.size
    for s, out in enumerate(outs):
        at = rows_at(ring.to(s), size, 8)
        out[...] = jnp.concatenate([held_a[at], held_b[at]], axis=0).astype(out.dtype)


def finish_kernel(inverse, *refs):
    out = refs[-1]
    total = refs[0][...]
    for r in refs[1:-1]:
        total = total + wide(r[...])
    out[...] = lax.dot_general(
        total, inverse[...], (((1,), (1,)), ((), ())), precision=EXACT, preferred_element_type=F32
    ).astype(BF16)


def join_two_kernel(ring, *refs):
    parts, (out_a, out_b, held_a, held_b) = refs[:-4], refs[-4:]
    size = out_a.shape[0] // ring.size
    for s, r in enumerate(parts):
        both = wide(r[...])
        at = rows_at(ring.source(s), size, 8)
        held_a[at] = both[:size]
        held_b[at] = both[size:]
    out_a[...] = held_a[...].astype(BF16)
    out_b[...] = held_b[...].astype(BF16)


def join(rings, blocks):
    ins = [b for group in blocks for b in group]
    outs = [vmem((g[0].shape[0] * len(g), g[0].shape[1]), g[0].dtype) for g in blocks]
    return local(functools.partial(join_kernel, rings), ins, outs)


def join_kernel(rings, *refs):
    ins, outs = list(refs[: sum(r.size for r in rings)]), refs[sum(r.size for r in rings) :]
    for ring, out in zip(rings, outs):
        size = out.shape[0] // ring.size
        for s in range(ring.size):
            out[rows_at(ring.source(s), size, 8)] = ins.pop(0)[...]


def refresh_kernel(core, ring_a, ring_b, tiles_q, tile, *refs):
    n_pieces = 2 * (ring_a.size + ring_b.size)
    pieces = list(refs[:n_pieces])
    basis_q, basis_k, merged_q, merged_k, out_q, out_k, new_q, new_k, held, flat = refs[n_pieces:]
    rank, d = new_q.shape
    step = pl.program_id(0)
    half = held.shape[0] // 2

    @pl.when(step == 0)
    def _():
        for c in range(2):
            base = core.to(c) * half
            for ring in (ring_a, ring_b):
                size = half // 2 // ring.size
                for s in range(ring.size):
                    at = pl.multiple_of(base + ring.source(s) * size, 16)
                    held[pl.ds(at, size)] = pieces.pop(0)[...]
                base = base + half // 2
        for t in range(0, d, LANES):
            flat[:, t : t + LANES] = wide(held[t : t + LANES]).T.astype(BF16)
        new_q[...] = flat[:rank]
        new_k[...] = flat[rank:]

    chunk = 768 if d % 768 == 0 else d

    def update(at, merged, basis, factor, out):
        rows = rows_at(at, tile, tile)
        b = basis[rows]
        for c in range(0, d, chunk):
            approx = jnp.dot(b, factor[:, c : c + chunk], preferred_element_type=F32)
            out[:, c : c + chunk] = (wide(merged[rows, c : c + chunk]) - approx).astype(BF16)

    @pl.when(step < tiles_q)
    def _():
        update(step, merged_q, basis_q, flat.at[:rank], out_q)

    @pl.when(step >= tiles_q)
    def _():
        update(step - tiles_q, merged_k, basis_k, flat.at[rank:], out_k)


def refresh(core, ring_a, ring_b, padded, pieces, basis_q, basis_k, merged_q, merged_k):
    rank = basis_q.shape[1]
    rows_q, d = merged_q.shape
    rows_k = merged_k.shape[0]
    tile = 2 * LANES if rows_k % (2 * LANES) == 0 else LANES
    tiles_q, tiles_k = rows_q // tile, rows_k // tile
    ins = [*pieces, basis_q, basis_k, merged_q, merged_k]
    ins = [pltpu.with_memory_space_constraint(a, pltpu.VMEM) for a in ins]
    return pl.pallas_call(
        functools.partial(refresh_kernel, core, ring_a, ring_b, tiles_q, tile),
        grid=(tiles_q + tiles_k,),
        in_specs=[whole()] * len(ins),
        out_specs=[
            pl.BlockSpec((tile, d), lambda i: (jnp.minimum(i, tiles_q - 1), 0)),
            pl.BlockSpec((tile, d), lambda i: (jnp.maximum(i - tiles_q, 0), 0)),
            pl.BlockSpec((rank, d), lambda i: (0, 0)),
            pl.BlockSpec((rank, d), lambda i: (0, 0)),
        ],
        out_shape=[
            jax.ShapeDtypeStruct((rows_q, d), BF16),
            jax.ShapeDtypeStruct((rows_k, d), BF16),
            jax.ShapeDtypeStruct((rank, d), BF16),
            jax.ShapeDtypeStruct((rank, d), BF16),
        ],
        scratch_shapes=[vmem((padded, 2 * rank), BF16), vmem((2 * rank, d), BF16)],
        compiler_params=pltpu.CompilerParams(vmem_limit_bytes=24 * MIB),
        cost_estimate=pl.CostEstimate(
            flops=2 * (rows_q + rows_k) * d * 256, bytes_accessed=4 * (rows_q + rows_k) * d, transcendentals=0
        ),
    )(*ins)


def body(grad_query, grad_key, error_query, error_key, factor_query, factor_key):
    n_dp, n_t = lax.axis_size("dp"), lax.axis_size("tensor")
    n_z = 4 if n_dp % 4 == 0 else 2
    n_y = n_dp // n_z
    ring_y = Ring("dp", n_dp, 1, n_y)
    ring_z = Ring("dp", n_dp, n_y, n_z)
    core = Ring("tensor", n_t, 1, 2)
    ring_x = Ring("tensor", n_t, 2, n_t // 2)
    rows_q, d = grad_query.shape[2:]
    rows_k = grad_key.shape[2]
    rank = factor_query.shape[2]
    unit = 16 * n_dp * n_t
    padded = -(-d // unit) * unit
    half = padded // 2

    near, far = Ring("dp", n_dp, n_y, 2), Ring("dp", n_dp, 2 * n_y, n_z // 2)
    flat = -(-(rows_q + rows_k) // LANES * rank // (16 * n_dp)) * 16 * n_dp
    orders = [(ring_y, near, far), (near, far, ring_y)]
    (merged_q, merged_k), cuts = images(
        [o[0] for o in orders],
        flat,
        [grad_query[0, 0], grad_key[0, 0]],
        [error_query[0, 0], error_key[0, 0]],
        [factor_query[0].T, factor_key[0].T],
    )
    for level in range(1, 4):
        jobs = []
        for (kept, sent), order in zip(cuts, orders):
            got = order[level - 1].scatter(sent)
            jobs.append((kept, got, order[level : level + 1]))
        if level < 3:
            cuts = split(jobs, sent=F32)
    blocks = local(
        functools.partial(total_kernel, [1 + len(j[1]) for j in jobs]),
        [x for kept, got, _ in jobs for x in (kept, *got)],
        [vmem(kept.shape, F32) for kept, _, _ in jobs],
    )
    for level in (2, 1, 0):
        groups = [[b, *order[level].gather(b)] for b, order in zip(blocks, orders)]
        if level:
            blocks = join([order[level] for order in orders], groups)
    image_q, image_k, halves_q, halves_k, gram = local(
        functools.partial(assemble_kernel, [o[0] for o in orders], rank, (rows_q, rows_k)),
        [b for g in groups for b in g],
        [
            vmem((rank, rows_q), F32),
            vmem((rank, rows_k), F32),
            vmem((2 * rank, rows_q), BF16),
            vmem((2 * rank, rows_k), BF16),
            vmem((rank, 2 * rank), F32),
        ],
        [vmem((flat, LANES), F32)],
    )
    gram_pair = core.gather(gram)

    sent = project(core, True, half, halves_q, halves_k, merged_q, merged_k)
    got = core.scatter([sent])
    kept = project(core, False, half, halves_q, halves_k, merged_q, merged_k)
    gram = local(functools.partial(total_kernel, [2]), [gram, *gram_pair], [vmem(gram.shape, F32)])[0]
    grams = [gram, *ring_x.gather(gram)]
    (kept_a, sent_a), (kept_b, sent_b) = split([(kept, got, [ring_x, ring_y])])
    inverse = local(
        functools.partial(inverse_kernel, ring_x),
        grams,
        [vmem((2 * rank, 2 * rank), F32)],
        [vmem((len(grams), rank, 2 * rank), F32)],
        flops=1 << 32,
        after=[kept_a],
    )[0]
    got_a, got_b = ring_x.scatter(sent_a), ring_y.scatter(sent_b)
    (kept_a, sent_a), (kept_b, sent_b) = split(
        [(kept_a, got_a, [ring_y]), (kept_b, got_b, [ring_x])], after=[inverse]
    )
    got_a, got_b = ring_y.scatter(sent_a), ring_x.scatter(sent_b)
    piece = (2 * kept_a.shape[0] // n_z, 2 * rank)
    out = local(
        functools.partial(split_two_kernel, len(got_a), len(got_b), ring_z),
        [kept_a, *got_a, kept_b, *got_b],
        [vmem(piece, F32)] + [vmem(piece, BF16)] * (n_z - 1),
        [vmem(kept_a.shape, F32)] * 2,
    )
    got = ring_z.scatter(out[1:])
    own = local(finish_kernel, [inverse, out[0], *got], [vmem(piece, BF16)])[0]

    got = ring_z.gather(own)
    part = (kept_a.shape[0], 2 * rank)
    own_a, own_b = local(
        functools.partial(join_two_kernel, ring_z), [own, *got], [vmem(part, BF16)] * 2, [vmem(part, F32)] * 2
    )
    all_a, all_b = ring_y.gather(own_a), ring_x.gather(own_b)
    own_a, own_b = join([ring_y, ring_x], [[own_a, *all_a], [own_b, *all_b]])
    pieces = [own_a, *ring_x.gather(own_a), own_b, *ring_y.gather(own_b)]
    pieces += [core.send(p, 1) for p in pieces]
    basis_q, basis_k = local(
        functools.partial(basis_kernel, 1.0 / n_dp),
        [inverse, image_q, image_k],
        [vmem((rows_q, rank), BF16), vmem((rows_k, rank), BF16)],
    )
    error_q, error_k, new_q, new_k = refresh(
        core, ring_x, ring_y, padded, pieces, basis_q, basis_k, merged_q, merged_k
    )
    return error_q[None, None], error_k[None, None], new_q.T[None], new_k.T[None]


def solution(mesh):
    rows = P("dp", None, "tensor", None)
    return jax.shard_map(
        body,
        mesh=mesh,
        in_specs=(rows, rows, rows, rows, P(), P()),
        out_specs=(rows, rows, P(), P()),
        check_vma=False,
    )
```

time: 247 us -> 111 us (0.45)
  blocking collectives: 80.2 us -> 0 us
  matrix products: 51.6 us -> 0 us
  starting transfers between devices: 0.04 us -> 38.6 us
  waiting for transfers between devices: 74.4 us -> 38 us
  Pallas kernels: 0 us -> 33.3 us
  other arithmetic: 24.2 us -> 0 us
  between operations: 14.2 us -> 0.8 us
    psum x2 -> x0, blocking collectives: 80.2 us -> none  [the longest x1 69.3 us: body(): lax.psum((projected(merged_q, basis_q), projected(merged_k, basis_k)), ('...]
    psum x1 -> x0, waiting for transfers between devices: 74.4 us -> none  [body(): image_q, image_k = lax.psum((image_q, image_k), 'dp')]
    dot_general x8 -> x0, matrix products: 49.9 us -> none  [the longest x2 20.7 us: refresh(): jnp.einsum('lhr,ldr->lhd', basis, factor, preferred_element_type=jnp.floa...]
    ppermute x0 -> x33, starting transfers between devices: none -> 38.6 us  [send(): return lax.ppermute(x, self.axis, pairs)]
    ppermute x0 -> x33, waiting for transfers between devices: none -> 38 us  [send(): return lax.ppermute(x, self.axis, pairs)]
    pallas_call x0 -> x19, Pallas kernels: none -> 33.3 us  [the longest x17 13.2 us: local(): pl.pallas_call(run, in_specs=[whole()] * n_in + [pl.BlockSpec(memory_spac...]
    another operation x10 -> x0, other arithmetic: 24.1 us -> none  [the longest x6 13 us: orthonormal(): lower = jnp.linalg.cholesky(gram)]
  transfers between devices with their start and end apart: 1 -> 33, of which waited for: 1 -> 23; matrix products, arithmetic and copies ran while one was open for 0% -> 0% of each run, Pallas kernels for 0% -> 10%
where the time goes in v1:
time: 111 us
  starting transfers between devices  38.6 us (35%)
  waiting for transfers between devices  38 us (34%)
  Pallas kernels  33.3 us (30%)
    ppermute x33, starting transfers between devices, send(): return lax.ppermute(x, self.axis, pairs)  38.6 us
    ppermute x33, waiting for transfers between devices, send(): return lax.ppermute(x, self.axis, pairs)  38 us
    pallas_call x17, Pallas kernels, local(): pl.pallas_call(run, in_specs=[whole()] * n_in + [pl.BlockSpec(memory_spac...  13.2 us
    pallas_call x1, Pallas kernels, images(): pl.pallas_call(functools.partial(image_kernel, rings, tile, 4), in_specs=...  11.1 us
    pallas_call x1, Pallas kernels, refresh(): pl.pallas_call(functools.partial(refresh_kernel, core, ring_a, ring_b, ti...  8.96 us
  transfers between devices with their start and end apart: 33, of which 23 were waited for; matrix products, arithmetic and copies ran while one was open for 0% of the time, Pallas kernels for 10%

profile of v1, /device:TPU:0, one launch (start us, length us, event | category | flops | bytes accessed | tf_op | source)
XLA Modules:
  0.0 110.7 jit_solution(18269530670307304966)
XLA Ops:
  0.6 11.1 %shard_map.93 = (bf16[1024,4608]{1,0:T(8,128)(2,1)S(1)}, bf16[512,4608]{1,0:T(8,128)(2,1)S(1)}, f32[192,128]{1,0:T(8,128)S(1)}, f32[192,128]{1,0:T(8,128)S(1)}, ...) custom-call(bf16[1024,4608]{1,0:T(8,128)(2,1)} %bitcast.18, bf16[512,4608]{1,0:T(8,128)(2,1)} %bitcast.20, ...), custom_call_target="tpu_custom_call" | custom-call | flops 3623878656 | bytes 28311552 | tf_op jit(solution)/shard_map/pallas_call | solution.py:156
  11.8 3.0 %collective-permute-start = (f32[192,128]{1,0:T(8,128)S(1)}, f32[192,128]{1,0:T(8,128)S(1)}, u32[]{:S(2)}, u32[]{:S(2)}) collective-permute-start(f32[192,128]{1,0:T(8,128)S(1)} %get-tuple-element.52), channel_id=1, source_target_pairs={{0,4},{4,0},{8,12},{12,8},{16,20},{20,16},{24,28},{28,24},{1,5},{5... | collective-permute-start | bytes 294920 | tf_op jit(solution)/shard_map/ppermute | solution.py:71
  14.8 1.6 %collective-permute-start.1 = (f32[192,128]{1,0:T(8,128)S(1)}, f32[192,128]{1,0:T(8,128)S(1)}, u32[]{:S(2)}, u32[]{:S(2)}) collective-permute-start(f32[192,128]{1,0:T(8,128)S(1)} %get-tuple-element.54), channel_id=1, source_target_pairs={{0,8},{4,12},{8,0},{12,4},{16,24},{20,28},{24,16},{28,20},{1,9},{5... | collective-permute-start | bytes 294920 | tf_op jit(solution)/shard_map/ppermute | solution.py:71
  16.4 1.2 %collective-permute-done.refs_1_ = f32[192,128]{1,0:T(8,128)S(1)} collective-permute-done((f32[192,128]{1,0:T(8,128)S(1)}, f32[192,128]{1,0:T(8,128)S(1)}, u32[]{:S(2)}, u32[]{:S(2)}) %collective-permute-start) | collective-permute-done | bytes 98336 | tf_op jit(solution)/shard_map/ppermute | solution.py:71
  17.6 1.8 %collective-permute-done.1.refs_3_ = f32[192,128]{1,0:T(8,128)S(1)} collective-permute-done((f32[192,128]{1,0:T(8,128)S(1)}, f32[192,128]{1,0:T(8,128)S(1)}, u32[]{:S(2)}, u32[]{:S(2)}) %collective-permute-start.1) | collective-permute-done | bytes 98336 | tf_op jit(solution)/shard_map/ppermute | solution.py:71
  19.5 1.7 %collective-permute-start.2 = (f32[96,128]{1,0:T(8,128)S(1)}, f32[96,128]{1,0:T(8,128)S(1)}, u32[]{:S(2)}, u32[]{:S(2)}) collective-permute-start(f32[96,128]{1,0:T(8,128)S(1)} %get-tuple-element.56), channel_id=1, source_target_pairs={{0,8},{4,12},{8,0},{12,4},{16,24},{20,28},{24,16},{28,20},{1,9},{5... | collective-permute-start | bytes 147464 | tf_op jit(solution)/shard_map/ppermute | solution.py:71
  21.1 2.6 %collective-permute-start.3 = (f32[96,128]{1,0:T(8,128)S(1)}, f32[96,128]{1,0:T(8,128)S(1)}, u32[]{:S(2)}, u32[]{:S(2)}) collective-permute-start(f32[96,128]{1,0:T(8,128)S(1)} %get-tuple-element.58), channel_id=1, source_target_pairs={{0,16},{4,20},{8,24},{12,28},{16,0},{20,4},{24,8},{28,12},{1,17},{... | collective-permute-start | bytes 147464 | tf_op jit(solution)/shard_map/ppermute | solution.py:71
  23.9 2.7 %collective-permute-done.3.refs_3_ = f32[96,128]{1,0:T(8,128)S(1)} collective-permute-done((f32[96,128]{1,0:T(8,128)S(1)}, f32[96,128]{1,0:T(8,128)S(1)}, u32[]{:S(2)}, u32[]{:S(2)}) %collective-permute-start.3) | collective-permute-done | bytes 49184 | tf_op jit(solution)/shard_map/ppermute | solution.py:71
  26.7 2.1 %collective-permute-start.4 = (f32[48,128]{1,0:T(8,128)S(1)}, f32[48,128]{1,0:T(8,128)S(1)}, u32[]{:S(2)}, u32[]{:S(2)}) collective-permute-start(f32[48,128]{1,0:T(8,128)S(1)} %get-tuple-element.60), channel_id=1, source_target_pairs={{0,16},{4,20},{8,24},{12,28},{16,0},{20,4},{24,8},{28,12},{1,17},{... | collective-permute-start | bytes 73736 | tf_op jit(solution)/shard_map/ppermute | solution.py:71
  29.3 2.1 %collective-permute-done.4.refs_1_ = f32[48,128]{1,0:T(8,128)S(1)} collective-permute-done((f32[48,128]{1,0:T(8,128)S(1)}, f32[48,128]{1,0:T(8,128)S(1)}, u32[]{:S(2)}, u32[]{:S(2)}) %collective-permute-start.4) | collective-permute-done | bytes 24608 | tf_op jit(solution)/shard_map/ppermute | solution.py:71
  31.5 1.4 %collective-permute-done.5.refs_3_ = f32[48,128]{1,0:T(8,128)S(1)} collective-permute-done((f32[48,128]{1,0:T(8,128)S(1)}, f32[48,128]{1,0:T(8,128)S(1)}, u32[]{:S(2)}, u32[]{:S(2)}) %collective-permute-start.5) | collective-permute-done | bytes 24608 | tf_op jit(solution)/shard_map/ppermute | solution.py:71
  32.9 0.7 collective-permute-start.6
  34.1 3.6 %collective-permute-done.6.refs_1_ = f32[48,128]{1,0:T(8,128)S(1)} collective-permute-done((f32[48,128]{1,0:T(8,128)S(1)}, f32[48,128]{1,0:T(8,128)S(1)}, u32[]{:S(2)}, u32[]{:S(2)}) %collective-permute-start.6) | collective-permute-done | bytes 24608 | tf_op jit(solution)/shard_map/ppermute | solution.py:71
  38.1 2.0 %collective-permute-start.9 = (f32[96,128]{1,0:T(8,128)S(1)}, f32[96,128]{1,0:T(8,128)S(1)}, u32[]{:S(2)}, u32[]{:S(2)}) collective-permute-start(f32[96,128]{1,0:T(8,128)S(1)} %get-tuple-element.66.refs_2_), channel_id=1, source_target_pairs={{0,16},{4,20},{8,24},{12,28},{16,0},{20,4},{24,8},{28,12},{1,17},{... | collective-permute-start | bytes 147464 | tf_op jit(solution)/shard_map/ppermute | solution.py:71
  40.1 1.8 %collective-permute-done.8.refs_1_ = f32[96,128]{1,0:T(8,128)S(1)} collective-permute-done((f32[96,128]{1,0:T(8,128)S(1)}, f32[96,128]{1,0:T(8,128)S(1)}, u32[]{:S(2)}, u32[]{:S(2)}) %collective-permute-start.8) | collective-permute-done | bytes 49184 | tf_op jit(solution)/shard_map/ppermute | solution.py:71
  41.9 1.2 %collective-permute-done.9.refs_3_ = f32[96,128]{1,0:T(8,128)S(1)} collective-permute-done((f32[96,128]{1,0:T(8,128)S(1)}, f32[96,128]{1,0:T(8,128)S(1)}, u32[]{:S(2)}, u32[]{:S(2)}) %collective-permute-start.9) | collective-permute-done | bytes 49184 | tf_op jit(solution)/shard_map/ppermute | solution.py:71
  43.1 0.8 collective-permute-start.10
  43.9 1.9 %collective-permute-start.11 = (f32[192,128]{1,0:T(8,128)S(1)}, f32[192,128]{1,0:T(8,128)S(1)}, u32[]{:S(2)}, u32[]{:S(2)}) collective-permute-start(f32[192,128]{1,0:T(8,128)S(1)} %get-tuple-element.68.refs_2_), channel_id=1, source_target_pairs={{0,8},{4,12},{8,0},{12,4},{16,24},{20,28},{24,16},{28,20},{1,9},{5... | collective-permute-start | bytes 294920 | tf_op jit(solution)/shard_map/ppermute | solution.py:71
  45.9 1.9 %collective-permute-done.10.refs_1_ = f32[192,128]{1,0:T(8,128)S(1)} collective-permute-done((f32[192,128]{1,0:T(8,128)S(1)}, f32[192,128]{1,0:T(8,128)S(1)}, u32[]{:S(2)}, u32[]{:S(2)}) %collective-permute-start.10) | collective-permute-done | bytes 98336 | tf_op jit(solution)/shard_map/ppermute | solution.py:71
  47.8 0.8 collective-permute-done.11.refs_3_
  49.1 1.2 %shard_map.102 = bf16[2304,128]{1,0:T(8,128)(2,1)S(1)} custom-call(bf16[128,1024]{1,0:T(8,128)(2,1)S(1)} %get-tuple-element.70.refs_0_, bf16[128,512]{1,0:T(8,128)(2,1)S(1)} %get-tuple-element.71.refs_1_, bf16[1024,4608]{1,0:T(8,128)(2,1)S(1)} %get-tuple-element.72.refs_2_.refs_10_, bf16[512,4608]{1,0:T(8,128)(2,1)S(1)} %get-tuple-element.73.refs_3_.refs_11_), custom_call_target="tpu_custom_call" | custom-call | flops 1811939328 | bytes 14548992 | tf_op jit(solution)/shard_map/pallas_call | solution.py:36
  50.9 1.5 %collective-permute-done.12.refs_1_ = f32[64,128]{1,0:T(8,128)S(1)} collective-permute-done((f32[64,128]{1,0:T(8,128)S(1)}, f32[64,128]{1,0:T(8,128)S(1)}, u32[]{:S(2)}, u32[]{:S(2)}) %collective-permute-start.12) | collective-permute-done | bytes 32800 | tf_op jit(solution)/shard_map/ppermute | solution.py:71
  52.5 1.5 %collective-permute-start.13 = (f32[64,128]{1,0:T(8,128)S(1)}, f32[64,128]{1,0:T(8,128)S(1)}, u32[]{:S(2)}, u32[]{:S(2)}) collective-permute-start(f32[64,128]{1,0:T(8,128)S(1)} %shard_map.100.refs_0_), channel_id=1, source_target_pairs={{0,2},{1,3},{2,0},{3,1},{4,6},{5,7},{6,4},{7,5},{8,10},{9,11},{10,... | collective-permute-start | bytes 98312 | tf_op jit(solution)/shard_map/ppermute | solution.py:71
  54.0 1.2 %shard_map.101.refs_0_ = f32[2304,128]{1,0:T(8,128)S(1)} custom-call(bf16[128,1024]{1,0:T(8,128)(2,1)S(1)} %get-tuple-element.70.refs_0_, bf16[128,512]{1,0:T(8,128)(2,1)S(1)} %get-tuple-element.71.refs_1_, bf16[1024,4608]{1,0:T(8,128)(2,1)S(1)} %get-tuple-element.72.refs_2_.refs_10_, bf16[512,4608]{1,0:T(8,128)(2,1)S(1)} %get-tuple-element.73.refs_3_.refs_11_), custom_call_target="tpu_custom_call" | custom-call | flops 1811939328 | bytes 14548992 | tf_op jit(solution)/shard_map/pallas_call | solution.py:36
  56.1 1.3 %collective-permute-start.16 = (bf16[576,128]{1,0:T(8,128)(2,1)S(1)}, bf16[576,128]{1,0:T(8,128)(2,1)S(1)}, u32[]{:S(2)}, u32[]{:S(2)}) collective-permute-start(bf16[576,128]{1,0:T(8,128)(2,1)S(1)} %get-tuple-element.77), channel_id=1, source_target_pairs={{0,4},{4,0},{8,12},{12,8},{16,20},{20,16},{24,28},{28,24},{1,5},{5... | collective-permute-start | bytes 442376 | tf_op jit(solution)/shard_map/ppermute | solution.py:71
  57.3 8.8 %shard_map.104.refs_4_.refs_0_ = f32[128,128]{1,0:T(8,128)S(1)} custom-call(f32[64,128]{1,0:T(8,128)S(1)} %shard_map.100.refs_0_, f32[64,128]{1,0:T(8,128)S(1)} %collective-permute-done.13.refs_1_, f32[576,128]{1,0:T(8,128)S(1)} %get-tuple-element.74.refs_2_.refs_0_), custom_call_target="tpu_custom_call" | custom-call | flops 4294967296 | bytes 65536 | tf_op jit(solution)/shard_map/pallas_call | solution.py:36
  66.3 0.8 collective-permute-start.17
  67.1 1.5 %collective-permute-start.18 = (bf16[288,128]{1,0:T(8,128)(2,1)S(1)}, bf16[288,128]{1,0:T(8,128)(2,1)S(1)}, u32[]{:S(2)}, u32[]{:S(2)}) collective-permute-start(bf16[288,128]{1,0:T(8,128)(2,1)S(1)} %get-tuple-element.81), channel_id=1, source_target_pairs={{0,2},{1,3},{2,0},{3,1},{4,6},{5,7},{6,4},{7,5},{8,10},{9,11},{10,... | collective-permute-start | bytes 221192 | tf_op jit(solution)/shard_map/ppermute | solution.py:71
  68.6 2.1 %collective-permute-done.17.refs_1_ = bf16[288,128]{1,0:T(8,128)(2,1)S(1)} collective-permute-done((bf16[288,128]{1,0:T(8,128)(2,1)S(1)}, bf16[288,128]{1,0:T(8,128)(2,1)S(1)}, u32[]{:S(2)}, u32[]{:S(2)}) %collective-permute-start.17) | collective-permute-done | bytes 73760 | tf_op jit(solution)/shard_map/ppermute | solution.py:71
  70.7 0.8 collective-permute-done.18.refs_3_
  71.5 2.0 %collective-permute-start.19 = (bf16[144,128]{1,0:T(8,128)(2,1)S(1)}, bf16[144,128]{1,0:T(8,128)(2,1)S(1)}, u32[]{:S(2)}, u32[]{:S(2)}) collective-permute-start(bf16[144,128]{1,0:T(8,128)(2,1)S(1)} %get-tuple-element.83), channel_id=1, source_target_pairs={{0,8},{4,12},{8,0},{12,4},{16,24},{20,28},{24,16},{28,20},{1,9},{5... | collective-permute-start | bytes 110600 | tf_op jit(solution)/shard_map/ppermute | solution.py:71
  73.5 1.8 %collective-permute-start.20 = (bf16[144,128]{1,0:T(8,128)(2,1)S(1)}, bf16[144,128]{1,0:T(8,128)(2,1)S(1)}, u32[]{:S(2)}, u32[]{:S(2)}) collective-permute-start(bf16[144,128]{1,0:T(8,128)(2,1)S(1)} %get-tuple-element.84), channel_id=1, source_target_pairs={{0,16},{4,20},{8,24},{12,28},{16,0},{20,4},{24,8},{28,12},{1,17},{... | collective-permute-start | bytes 110600 | tf_op jit(solution)/shard_map/ppermute | solution.py:71
  75.3 0.7 collective-permute-start.21
  75.9 2.4 %collective-permute-done.20.refs_3_ = bf16[144,128]{1,0:T(8,128)(2,1)S(1)} collective-permute-done((bf16[144,128]{1,0:T(8,128)(2,1)S(1)}, bf16[144,128]{1,0:T(8,128)(2,1)S(1)}, u32[]{:S(2)}, u32[]{:S(2)}) %collective-permute-start.20) | collective-permute-done | bytes 36896 | tf_op jit(solution)/shard_map/ppermute | solution.py:71
  78.4 2.7 %collective-permute-done.21.refs_4_ = bf16[144,128]{1,0:T(8,128)(2,1)S(1)} collective-permute-done((bf16[144,128]{1,0:T(8,128)(2,1)S(1)}, bf16[144,128]{1,0:T(8,128)(2,1)S(1)}, u32[]{:S(2)}, u32[]{:S(2)}) %collective-permute-start.21) | collective-permute-done | bytes 36896 | tf_op jit(solution)/shard_map/ppermute | solution.py:71
  81.3 0.8 collective-permute-start.24
  82.1 3.7 %collective-permute-start.22 = (bf16[144,128]{1,0:T(8,128)(2,1)S(1)}, bf16[144,128]{1,0:T(8,128)(2,1)S(1)}, u32[]{:S(2)}, u32[]{:S(2)}) collective-permute-start(bf16[144,128]{1,0:T(8,128)(2,1)S(1)} %shard_map.107.refs_0_), channel_id=1, source_target_pairs={{0,8},{4,12},{8,0},{12,4},{16,24},{20,28},{24,16},{28,20},{1,9},{5... | collective-permute-start | bytes 110600 | tf_op jit(solution)/shard_map/ppermute | solution.py:71
  85.7 1.5 %collective-permute-done.24.refs_3_ = bf16[144,128]{1,0:T(8,128)(2,1)S(1)} collective-permute-done((bf16[144,128]{1,0:T(8,128)(2,1)S(1)}, bf16[144,128]{1,0:T(8,128)(2,1)S(1)}, u32[]{:S(2)}, u32[]{:S(2)}) %collective-permute-start.24) | collective-permute-done | bytes 36896 | tf_op jit(solution)/shard_map/ppermute | solution.py:71
  87.8 1.5 %collective-permute-start.25 = (bf16[288,128]{1,0:T(8,128)(2,1)S(1)}, bf16[288,128]{1,0:T(8,128)(2,1)S(1)}, u32[]{:S(2)}, u32[]{:S(2)}) collective-permute-start(bf16[288,128]{1,0:T(8,128)(2,1)S(1)} %get-tuple-element.86.refs_0_), channel_id=1, source_target_pairs={{0,4},{4,0},{8,12},{12,8},{16,20},{20,16},{24,28},{28,24},{1,5},{5... | collective-permute-start | bytes 221192 | tf_op jit(solution)/shard_map/ppermute | solution.py:71
  89.3 1.5 %collective-permute-start.26 = (bf16[288,128]{1,0:T(8,128)(2,1)S(1)}, bf16[288,128]{1,0:T(8,128)(2,1)S(1)}, u32[]{:S(2)}, u32[]{:S(2)}) collective-permute-start(bf16[288,128]{1,0:T(8,128)(2,1)S(1)} %get-tuple-element.87.refs_2_), channel_id=1, source_target_pairs={{0,2},{1,3},{2,0},{3,1},{4,6},{5,7},{6,4},{7,5},{8,10},{9,11},{10,... | collective-permute-start | bytes 221192 | tf_op jit(solution)/shard_map/ppermute | solution.py:71
  90.8 2.0 %collective-permute-done.25.refs_1_ = bf16[288,128]{1,0:T(8,128)(2,1)S(1)} collective-permute-done((bf16[288,128]{1,0:T(8,128)(2,1)S(1)}, bf16[288,128]{1,0:T(8,128)(2,1)S(1)}, u32[]{:S(2)}, u32[]{:S(2)}) %collective-permute-start.25) | collective-permute-done | bytes 73760 | tf_op jit(solution)/shard_map/ppermute | solution.py:71
  92.8 0.9 collective-permute-done.26.refs_3_
  93.7 1.6 %collective-permute-start.27 = (bf16[576,128]{1,0:T(8,128)(2,1)S(1)}, bf16[576,128]{1,0:T(8,128)(2,1)S(1)}, u32[]{:S(2)}, u32[]{:S(2)}) collective-permute-start(bf16[576,128]{1,0:T(8,128)(2,1)S(1)} %get-tuple-element.88.refs_0_), channel_id=1, source_target_pairs={{0,2},{1,3},{2,0},{3,1},{4,6},{5,7},{6,4},{7,5},{8,10},{9,11},{10,... | collective-permute-start | bytes 442376 | tf_op jit(solution)/shard_map/ppermute | solution.py:71
  95.3 0.6 collective-permute-start.28
  96.4 2.5 %collective-permute-done.27.refs_1_ = bf16[576,128]{1,0:T(8,128)(2,1)S(1)} collective-permute-done((bf16[576,128]{1,0:T(8,128)(2,1)S(1)}, bf16[576,128]{1,0:T(8,128)(2,1)S(1)}, u32[]{:S(2)}, u32[]{:S(2)}) %collective-permute-start.27) | collective-permute-done | bytes 147488 | tf_op jit(solution)/shard_map/ppermute | solution.py:71
  98.9 1.5 %collective-permute-done.28.refs_3_ = bf16[576,128]{1,0:T(8,128)(2,1)S(1)} collective-permute-done((bf16[576,128]{1,0:T(8,128)(2,1)S(1)}, bf16[576,128]{1,0:T(8,128)(2,1)S(1)}, u32[]{:S(2)}, u32[]{:S(2)}) %collective-permute-start.28) | collective-permute-done | bytes 147488 | tf_op jit(solution)/shard_map/ppermute | solution.py:71
  101.0 0.8 collective-permute-done.32.refs_7_
  101.8 9.0 %shard_map.111 = (bf16[1024,4608]{1,0:T(8,128)(2,1)}, bf16[512,4608]{1,0:T(8,128)(2,1)}, bf16[64,4608]{1,0:T(8,128)(2,1)}, bf16[64,4608]{1,0:T(8,128)(2,1)}) custom-call(bf16[576,128]{1,0:T(8,128)(2,1)S(1)} %get-tuple-element.88.refs_0_, bf16[576,128]{1,0:T(8,128)(2,1)S(1)} %collective-permute-done.27.refs_1_, ...), custom_call_target="tpu_custom_call" | custom-call | flops 3623878656 | bytes 28311552 | tf_op jit(solution)/shard_map/pallas_call | solution.py:436
  (37 shorter events, 5.8 us)
Async XLA Ops:
  11.8 5.8 %collective-permute-start = (f32[192,128]{1,0:T(8,128)S(1)}, f32[192,128]{1,0:T(8,128)S(1)}, u32[]{:S(2)}, u32[]{:S(2)}) collective-permute-start(f32[192,128]{1,0:T(8,128)S(1)} %get-tuple-element.52), channel_id=1, source_target_pairs={{0,4},{4,0},{8,12},{12,8},{16,20},{20,16},{24,28},{28,24},{1,5},{5... | collective-permute-start | bytes 294920 | tf_op jit(solution)/shard_map/ppermute | solution.py:71
  14.8 4.6 %collective-permute-start.1 = (f32[192,128]{1,0:T(8,128)S(1)}, f32[192,128]{1,0:T(8,128)S(1)}, u32[]{:S(2)}, u32[]{:S(2)}) collective-permute-start(f32[192,128]{1,0:T(8,128)S(1)} %get-tuple-element.54), channel_id=1, source_target_pairs={{0,8},{4,12},{8,0},{12,4},{16,24},{20,28},{24,16},{28,20},{1,9},{5... | collective-permute-start | bytes 294920 | tf_op jit(solution)/shard_map/ppermute | solution.py:71
  19.5 4.4 %collective-permute-start.2 = (f32[96,128]{1,0:T(8,128)S(1)}, f32[96,128]{1,0:T(8,128)S(1)}, u32[]{:S(2)}, u32[]{:S(2)}) collective-permute-start(f32[96,128]{1,0:T(8,128)S(1)} %get-tuple-element.56), channel_id=1, source_target_pairs={{0,8},{4,12},{8,0},{12,4},{16,24},{20,28},{24,16},{28,20},{1,9},{5... | collective-permute-start | bytes 147464 | tf_op jit(solution)/shard_map/ppermute | solution.py:71
  21.1 5.5 %collective-permute-start.3 = (f32[96,128]{1,0:T(8,128)S(1)}, f32[96,128]{1,0:T(8,128)S(1)}, u32[]{:S(2)}, u32[]{:S(2)}) collective-permute-start(f32[96,128]{1,0:T(8,128)S(1)} %get-tuple-element.58), channel_id=1, source_target_pairs={{0,16},{4,20},{8,24},{12,28},{16,0},{20,4},{24,8},{28,12},{1,17},{... | collective-permute-start | bytes 147464 | tf_op jit(solution)/shard_map/ppermute | solution.py:71
  26.7 4.8 %collective-permute-start.4 = (f32[48,128]{1,0:T(8,128)S(1)}, f32[48,128]{1,0:T(8,128)S(1)}, u32[]{:S(2)}, u32[]{:S(2)}) collective-permute-start(f32[48,128]{1,0:T(8,128)S(1)} %get-tuple-element.60), channel_id=1, source_target_pairs={{0,16},{4,20},{8,24},{12,28},{16,0},{20,4},{24,8},{28,12},{1,17},{... | collective-permute-start | bytes 73736 | tf_op jit(solution)/shard_map/ppermute | solution.py:71
  28.8 4.1 %collective-permute-start.5 = (f32[48,128]{1,0:T(8,128)S(1)}, f32[48,128]{1,0:T(8,128)S(1)}, u32[]{:S(2)}, u32[]{:S(2)}) collective-permute-start(f32[48,128]{1,0:T(8,128)S(1)} %get-tuple-element.62), channel_id=1, source_target_pairs={{0,4},{4,0},{8,12},{12,8},{16,20},{20,16},{24,28},{28,24},{1,5},{5... | collective-permute-start | bytes 73736 | tf_op jit(solution)/shard_map/ppermute | solution.py:71
  32.9 4.8 %collective-permute-start.6 = (f32[48,128]{1,0:T(8,128)S(1)}, f32[48,128]{1,0:T(8,128)S(1)}, u32[]{:S(2)}, u32[]{:S(2)}) collective-permute-start(f32[48,128]{1,0:T(8,128)S(1)} %get-tuple-element.63.refs_0_), channel_id=1, source_target_pairs={{0,16},{4,20},{8,24},{12,28},{16,0},{20,4},{24,8},{28,12},{1,17},{... | collective-permute-start | bytes 73736 | tf_op jit(solution)/shard_map/ppermute | solution.py:71
  33.6 4.1 %collective-permute-start.7 = (f32[48,128]{1,0:T(8,128)S(1)}, f32[48,128]{1,0:T(8,128)S(1)}, u32[]{:S(2)}, u32[]{:S(2)}) collective-permute-start(f32[48,128]{1,0:T(8,128)S(1)} %get-tuple-element.64.refs_2_), channel_id=1, source_target_pairs={{0,4},{4,0},{8,12},{12,8},{16,20},{20,16},{24,28},{28,24},{1,5},{5... | collective-permute-start | bytes 73736 | tf_op jit(solution)/shard_map/ppermute | solution.py:71
  37.7 4.2 %collective-permute-start.8 = (f32[96,128]{1,0:T(8,128)S(1)}, f32[96,128]{1,0:T(8,128)S(1)}, u32[]{:S(2)}, u32[]{:S(2)}) collective-permute-start(f32[96,128]{1,0:T(8,128)S(1)} %get-tuple-element.65.refs_0_), channel_id=1, source_target_pairs={{0,8},{4,12},{8,0},{12,4},{16,24},{20,28},{24,16},{28,20},{1,9},{5... | collective-permute-start | bytes 147464 | tf_op jit(solution)/shard_map/ppermute | solution.py:71
  38.1 5.0 %collective-permute-start.9 = (f32[96,128]{1,0:T(8,128)S(1)}, f32[96,128]{1,0:T(8,128)S(1)}, u32[]{:S(2)}, u32[]{:S(2)}) collective-permute-start(f32[96,128]{1,0:T(8,128)S(1)} %get-tuple-element.66.refs_2_), channel_id=1, source_target_pairs={{0,16},{4,20},{8,24},{12,28},{16,0},{20,4},{24,8},{28,12},{1,17},{... | collective-permute-start | bytes 147464 | tf_op jit(solution)/shard_map/ppermute | solution.py:71
  43.1 4.7 %collective-permute-start.10 = (f32[192,128]{1,0:T(8,128)S(1)}, f32[192,128]{1,0:T(8,128)S(1)}, u32[]{:S(2)}, u32[]{:S(2)}) collective-permute-start(f32[192,128]{1,0:T(8,128)S(1)} %get-tuple-element.67.refs_0_), channel_id=1, source_target_pairs={{0,4},{4,0},{8,12},{12,8},{16,20},{20,16},{24,28},{28,24},{1,5},{5... | collective-permute-start | bytes 294920 | tf_op jit(solution)/shard_map/ppermute | solution.py:71
  43.9 4.6 %collective-permute-start.11 = (f32[192,128]{1,0:T(8,128)S(1)}, f32[192,128]{1,0:T(8,128)S(1)}, u32[]{:S(2)}, u32[]{:S(2)}) collective-permute-start(f32[192,128]{1,0:T(8,128)S(1)} %get-tuple-element.68.refs_2_), channel_id=1, source_target_pairs={{0,8},{4,12},{8,0},{12,4},{16,24},{20,28},{24,16},{28,20},{1,9},{5... | collective-permute-start | bytes 294920 | tf_op jit(solution)/shard_map/ppermute | solution.py:71
  50.3 4.8 %collective-permute-start.14 = (bf16[2304,128]{1,0:T(8,128)(2,1)S(1)}, bf16[2304,128]{1,0:T(8,128)(2,1)S(1)}, u32[]{:S(2)}, u32[]{:S(2)}) collective-permute-start(bf16[2304,128]{1,0:T(8,128)(2,1)S(1)} %shard_map.102), channel_id=1, source_target_pairs={{0,1},{1,0},{2,3},{3,2},{4,5},{5,4},{6,7},{7,6},{8,9},{9,8},{10,11... | collective-permute-start | bytes 1769480 | tf_op jit(solution)/shard_map/ppermute | solution.py:71
  50.4 2.0 %collective-permute-start.12 = (f32[64,128]{1,0:T(8,128)S(1)}, f32[64,128]{1,0:T(8,128)S(1)}, u32[]{:S(2)}, u32[]{:S(2)}) collective-permute-start(f32[64,128]{1,0:T(8,128)S(1)} %get-tuple-element.69.refs_0_), channel_id=1, source_target_pairs={{0,1},{1,0},{2,3},{3,2},{4,5},{5,4},{6,7},{7,6},{8,9},{9,8},{10,11... | collective-permute-start | bytes 98312 | tf_op jit(solution)/shard_map/ppermute | solution.py:71
  52.5 4.9 %collective-permute-start.13 = (f32[64,128]{1,0:T(8,128)S(1)}, f32[64,128]{1,0:T(8,128)S(1)}, u32[]{:S(2)}, u32[]{:S(2)}) collective-permute-start(f32[64,128]{1,0:T(8,128)S(1)} %shard_map.100.refs_0_), channel_id=1, source_target_pairs={{0,2},{1,3},{2,0},{3,1},{4,6},{5,7},{6,4},{7,5},{8,10},{9,11},{10,... | collective-permute-start | bytes 98312 | tf_op jit(solution)/shard_map/ppermute | solution.py:71
  55.5 10.7 %collective-permute-start.15 = (bf16[576,128]{1,0:T(8,128)(2,1)S(1)}, bf16[576,128]{1,0:T(8,128)(2,1)S(1)}, u32[]{:S(2)}, u32[]{:S(2)}) collective-permute-start(bf16[576,128]{1,0:T(8,128)(2,1)S(1)} %get-tuple-element.75), channel_id=1, source_target_pairs={{0,2},{1,3},{2,0},{3,1},{4,6},{5,7},{6,4},{7,5},{8,10},{9,11},{10,... | collective-permute-start | bytes 442376 | tf_op jit(solution)/shard_map/ppermute | solution.py:71
  56.1 10.1 %collective-permute-start.16 = (bf16[576,128]{1,0:T(8,128)(2,1)S(1)}, bf16[576,128]{1,0:T(8,128)(2,1)S(1)}, u32[]{:S(2)}, u32[]{:S(2)}) collective-permute-start(bf16[576,128]{1,0:T(8,128)(2,1)S(1)} %get-tuple-element.77), channel_id=1, source_target_pairs={{0,4},{4,0},{8,12},{12,8},{16,20},{20,16},{24,28},{28,24},{1,5},{5... | collective-permute-start | bytes 442376 | tf_op jit(solution)/shard_map/ppermute | solution.py:71
  66.3 4.4 %collective-permute-start.17 = (bf16[288,128]{1,0:T(8,128)(2,1)S(1)}, bf16[288,128]{1,0:T(8,128)(2,1)S(1)}, u32[]{:S(2)}, u32[]{:S(2)}) collective-permute-start(bf16[288,128]{1,0:T(8,128)(2,1)S(1)} %get-tuple-element.79), channel_id=1, source_target_pairs={{0,4},{4,0},{8,12},{12,8},{16,20},{20,16},{24,28},{28,24},{1,5},{5... | collective-permute-start | bytes 221192 | tf_op jit(solution)/shard_map/ppermute | solution.py:71
  67.1 4.4 %collective-permute-start.18 = (bf16[288,128]{1,0:T(8,128)(2,1)S(1)}, bf16[288,128]{1,0:T(8,128)(2,1)S(1)}, u32[]{:S(2)}, u32[]{:S(2)}) collective-permute-start(bf16[288,128]{1,0:T(8,128)(2,1)S(1)} %get-tuple-element.81), channel_id=1, source_target_pairs={{0,2},{1,3},{2,0},{3,1},{4,6},{5,7},{6,4},{7,5},{8,10},{9,11},{10,... | collective-permute-start | bytes 221192 | tf_op jit(solution)/shard_map/ppermute | solution.py:71
  71.5 4.5 %collective-permute-start.19 = (bf16[144,128]{1,0:T(8,128)(2,1)S(1)}, bf16[144,128]{1,0:T(8,128)(2,1)S(1)}, u32[]{:S(2)}, u32[]{:S(2)}) collective-permute-start(bf16[144,128]{1,0:T(8,128)(2,1)S(1)} %get-tuple-element.83), channel_id=1, source_target_pairs={{0,8},{4,12},{8,0},{12,4},{16,24},{20,28},{24,16},{28,20},{1,9},{5... | collective-permute-start | bytes 110600 | tf_op jit(solution)/shard_map/ppermute | solution.py:71
  73.5 4.9 %collective-permute-start.20 = (bf16[144,128]{1,0:T(8,128)(2,1)S(1)}, bf16[144,128]{1,0:T(8,128)(2,1)S(1)}, u32[]{:S(2)}, u32[]{:S(2)}) collective-permute-start(bf16[144,128]{1,0:T(8,128)(2,1)S(1)} %get-tuple-element.84), channel_id=1, source_target_pairs={{0,16},{4,20},{8,24},{12,28},{16,0},{20,4},{24,8},{28,12},{1,17},{... | collective-permute-start | bytes 110600 | tf_op jit(solution)/shard_map/ppermute | solution.py:71
  75.3 5.8 %collective-permute-start.21 = (bf16[144,128]{1,0:T(8,128)(2,1)S(1)}, bf16[144,128]{1,0:T(8,128)(2,1)S(1)}, u32[]{:S(2)}, u32[]{:S(2)}) collective-permute-start(bf16[144,128]{1,0:T(8,128)(2,1)S(1)} %get-tuple-element.85), channel_id=1, source_target_pairs={{0,24},{4,28},{8,16},{12,20},{16,8},{20,12},{24,0},{28,4},{1,25},{... | collective-permute-start | bytes 110600 | tf_op jit(solution)/shard_map/ppermute | solution.py:71
  81.3 5.9 %collective-permute-start.24 = (bf16[144,128]{1,0:T(8,128)(2,1)S(1)}, bf16[144,128]{1,0:T(8,128)(2,1)S(1)}, u32[]{:S(2)}, u32[]{:S(2)}) collective-permute-start(bf16[144,128]{1,0:T(8,128)(2,1)S(1)} %shard_map.107.refs_0_), channel_id=1, source_target_pairs={{0,24},{4,28},{8,16},{12,20},{16,8},{20,12},{24,0},{28,4},{1,25},{... | collective-permute-start | bytes 110600 | tf_op jit(solution)/shard_map/ppermute | solution.py:71
  82.1 5.7 %collective-permute-start.23 = (bf16[144,128]{1,0:T(8,128)(2,1)S(1)}, bf16[144,128]{1,0:T(8,128)(2,1)S(1)}, u32[]{:S(2)}, u32[]{:S(2)}) collective-permute-start(bf16[144,128]{1,0:T(8,128)(2,1)S(1)} %shard_map.107.refs_0_), channel_id=1, source_target_pairs={{0,16},{4,20},{8,24},{12,28},{16,0},{20,4},{24,8},{28,12},{1,17},{... | collective-permute-start | bytes 110600 | tf_op jit(solution)/shard_map/ppermute | solution.py:71
  82.1 5.7 %collective-permute-start.22 = (bf16[144,128]{1,0:T(8,128)(2,1)S(1)}, bf16[144,128]{1,0:T(8,128)(2,1)S(1)}, u32[]{:S(2)}, u32[]{:S(2)}) collective-permute-start(bf16[144,128]{1,0:T(8,128)(2,1)S(1)} %shard_map.107.refs_0_), channel_id=1, source_target_pairs={{0,8},{4,12},{8,0},{12,4},{16,24},{20,28},{24,16},{28,20},{1,9},{5... | collective-permute-start | bytes 110600 | tf_op jit(solution)/shard_map/ppermute | solution.py:71
  87.8 4.9 %collective-permute-start.25 = (bf16[288,128]{1,0:T(8,128)(2,1)S(1)}, bf16[288,128]{1,0:T(8,128)(2,1)S(1)}, u32[]{:S(2)}, u32[]{:S(2)}) collective-permute-start(bf16[288,128]{1,0:T(8,128)(2,1)S(1)} %get-tuple-element.86.refs_0_), channel_id=1, source_target_pairs={{0,4},{4,0},{8,12},{12,8},{16,20},{20,16},{24,28},{28,24},{1,5},{5... | collective-permute-start | bytes 221192 | tf_op jit(solution)/shard_map/ppermute | solution.py:71
  89.3 4.4 %collective-permute-start.26 = (bf16[288,128]{1,0:T(8,128)(2,1)S(1)}, bf16[288,128]{1,0:T(8,128)(2,1)S(1)}, u32[]{:S(2)}, u32[]{:S(2)}) collective-permute-start(bf16[288,128]{1,0:T(8,128)(2,1)S(1)} %get-tuple-element.87.refs_2_), channel_id=1, source_target_pairs={{0,2},{1,3},{2,0},{3,1},{4,6},{5,7},{6,4},{7,5},{8,10},{9,11},{10,... | collective-permute-start | bytes 221192 | tf_op jit(solution)/shard_map/ppermute | solution.py:71
  93.7 5.2 %collective-permute-start.27 = (bf16[576,128]{1,0:T(8,128)(2,1)S(1)}, bf16[576,128]{1,0:T(8,128)(2,1)S(1)}, u32[]{:S(2)}, u32[]{:S(2)}) collective-permute-start(bf16[576,128]{1,0:T(8,128)(2,1)S(1)} %get-tuple-element.88.refs_0_), channel_id=1, source_target_pairs={{0,2},{1,3},{2,0},{3,1},{4,6},{5,7},{6,4},{7,5},{8,10},{9,11},{10,... | collective-permute-start | bytes 442376 | tf_op jit(solution)/shard_map/ppermute | solution.py:71
  95.3 5.1 %collective-permute-start.28 = (bf16[576,128]{1,0:T(8,128)(2,1)S(1)}, bf16[576,128]{1,0:T(8,128)(2,1)S(1)}, u32[]{:S(2)}, u32[]{:S(2)}) collective-permute-start(bf16[576,128]{1,0:T(8,128)(2,1)S(1)} %get-tuple-element.89.refs_2_), channel_id=1, source_target_pairs={{0,4},{4,0},{8,12},{12,8},{16,20},{20,16},{24,28},{28,24},{1,5},{5... | collective-permute-start | bytes 442376 | tf_op jit(solution)/shard_map/ppermute | solution.py:71
  95.9 5.1 %collective-permute-start.29 = (bf16[576,128]{1,0:T(8,128)(2,1)S(1)}, bf16[576,128]{1,0:T(8,128)(2,1)S(1)}, u32[]{:S(2)}, u32[]{:S(2)}) collective-permute-start(bf16[576,128]{1,0:T(8,128)(2,1)S(1)} %get-tuple-element.88.refs_0_), channel_id=1, source_target_pairs={{0,1},{1,0},{2,3},{3,2},{4,5},{5,4},{6,7},{7,6},{8,9},{9,8},{10,11... | collective-permute-start | bytes 442376 | tf_op jit(solution)/shard_map/ppermute | solution.py:71
  95.9 5.1 %collective-permute-start.31 = (bf16[576,128]{1,0:T(8,128)(2,1)S(1)}, bf16[576,128]{1,0:T(8,128)(2,1)S(1)}, u32[]{:S(2)}, u32[]{:S(2)}) collective-permute-start(bf16[576,128]{1,0:T(8,128)(2,1)S(1)} %get-tuple-element.89.refs_2_), channel_id=1, source_target_pairs={{0,1},{1,0},{2,3},{3,2},{4,5},{5,4},{6,7},{7,6},{8,9},{9,8},{10,11... | collective-permute-start | bytes 442376 | tf_op jit(solution)/shard_map/ppermute | solution.py:71
  98.9 2.1 %collective-permute-start.30 = (bf16[576,128]{1,0:T(8,128)(2,1)S(1)}, bf16[576,128]{1,0:T(8,128)(2,1)S(1)}, u32[]{:S(2)}, u32[]{:S(2)}) collective-permute-start(bf16[576,128]{1,0:T(8,128)(2,1)S(1)} %collective-permute-done.27.refs_1_), channel_id=1, source_target_pairs={{0,1},{1,0},{2,3},{3,2},{4,5},{5,4},{6,7},{7,6},{8,9},{9,8},{10,11... | collective-permute-start | bytes 442376 | tf_op jit(solution)/shard_map/ppermute | solution.py:71
  100.4 1.4 %collective-permute-start.32 = (bf16[576,128]{1,0:T(8,128)(2,1)S(1)}, bf16[576,128]{1,0:T(8,128)(2,1)S(1)}, u32[]{:S(2)}, u32[]{:S(2)}) collective-permute-start(bf16[576,128]{1,0:T(8,128)(2,1)S(1)} %collective-permute-done.28.refs_3_), channel_id=1, source_target_pairs={{0,1},{1,0},{2,3},{3,2},{4,5},{5,4},{6,7},{7,6},{8,9},{9,8},{10,11... | collective-permute-start | bytes 442376 | tf_op jit(solution)/shard_map/ppermute | solution.py:71

commit v2 on v1

v2 whole, which is shorter than its diff:
```python
import functools

import jax
import jax.numpy as jnp
from jax import lax
from jax.experimental import pallas as pl
from jax.experimental.pallas import tpu as pltpu
from jax.sharding import Mesh, PartitionSpec as P

F32, BF16 = jnp.float32, jnp.bfloat16
MIB = 1 << 20
AXES = ("z", "y", "x", "core")
EXACT = lax.Precision.HIGHEST
LANES = 128


def wide(a):
    return a.astype(F32)


def vmem(shape, dtype):
    return pltpu.VMEM(tuple(shape), dtype)


def whole():
    return pl.BlockSpec(memory_space=pltpu.VMEM)


def local(kernel, ins, outs, scratch=(), limit=8, flops=0, after=()):
    ins = [pltpu.with_memory_space_constraint(a, pltpu.VMEM) for a in ins]
    moved = sum(a.size * a.dtype.itemsize for a in ins)
    n_in, n_after = len(ins), len(after)

    def run(*refs):
        kernel(*refs[:n_in], *refs[n_in + n_after :])

    return pl.pallas_call(
        run,
        in_specs=[whole()] * n_in + [pl.BlockSpec(memory_space=pl.ANY)] * n_after,
        out_specs=[whole()] * len(outs),
        out_shape=list(outs),
        scratch_shapes=list(scratch),
        compiler_params=pltpu.CompilerParams(vmem_limit_bytes=limit * MIB),
        cost_estimate=pl.CostEstimate(flops=flops, bytes_accessed=moved, transcendentals=0),
    )(*ins, *after)


class Group:
    def __init__(self, digits, count):
        self.digits, self.count = digits, count
        self.size = 1
        for _, size in digits:
            self.size *= size
        self.pairwise = self.size & (self.size - 1) == 0

    def place(self, index):
        p, weight = 0, 1
        for stride, size in self.digits:
            p = p + (index // stride) % size * weight
            weight *= size
        return p

    def pos(self):
        p, weight = 0, 1
        index = lax.axis_index(AXES)
        for stride, size in self.digits:
            p = p + lax.rem(lax.div(index, stride), size) * weight
            weight *= size
        return p

    def to(self, step):
        if self.pairwise:
            return lax.bitwise_xor(self.pos(), step)
        return lax.rem(self.pos() + step, self.size)

    def source(self, step):
        if self.pairwise:
            return lax.bitwise_xor(self.pos(), step)
        return lax.rem(self.pos() + (self.size - step), self.size)

    def send(self, x, step):
        pairs = []
        for src in range(self.count):
            p = self.place(src)
            q = p ^ step if self.pairwise else (p + step) % self.size
            dst, weight = src, 1
            for stride, size in self.digits:
                dst += ((q // weight) % size - (p // weight) % size) * stride
                weight *= size
            pairs.append((src, dst))
        return lax.ppermute(x, AXES, pairs)

    def scatter(self, parts):
        return [self.send(x, s + 1) for s, x in enumerate(parts)]

    def gather(self, x):
        return [self.send(x, s) for s in range(1, self.size)]


def rows_at(index, size, align):
    return pl.ds(pl.multiple_of(index * size, align), size)


def blocks_at(group, size, align):
    return [rows_at(group.source(s), size, align) for s in range(group.size)]


def cut_into(held, group, outs):
    size = held.shape[0] // group.size
    for s, out in enumerate(outs):
        out[...] = held[rows_at(group.to(s), size, 8)].astype(out.dtype)


def image_kernel(tile, depth, *refs):
    ins, outs, scratch = refs[:6], refs[6:9], refs[9:]
    grads, errors, factors = ins[0:2], ins[2:4], ins[4:6]
    merged, held = outs[:2], outs[2]
    arrived, flat_factors, natural, grad_sems, error_sems, factor_sems = scratch
    rank, d = flat_factors.shape[1:]
    tiles = [(m, i) for m in (0, 1) for i in range(grads[m].shape[0] // tile)]

    def copies(n):
        m, i = tiles[n]
        rows = pl.ds(i * tile, tile)
        return (
            pltpu.make_async_copy(grads[m].at[rows], merged[m].at[rows], grad_sems.at[n]),
            pltpu.make_async_copy(errors[m].at[rows], arrived.at[n], error_sems.at[n]),
        )

    def factor_copy(m):
        return pltpu.make_async_copy(factors[m], flat_factors.at[m], factor_sems.at[m])

    def start(n):
        for c in copies(n):
            c.start()

    factor_copy(0).start()
    for n in range(min(depth, len(tiles))):
        start(n)
        if n == 0:
            factor_copy(1).start()
    for m in range(2):
        factor_copy(m).wait()
        for t in range(0, d, LANES):
            natural[m, t : t + LANES] = wide(flat_factors[m, :, t : t + LANES]).T.astype(BF16)
    chunk = 512 if d % 512 == 0 else d
    for n, (m, i) in enumerate(tiles):
        for c in copies(n):
            c.wait()
        if n + depth < len(tiles):
            start(n + depth)
        rows = pl.ds(i * tile, tile)
        image = jnp.zeros((tile, rank), F32)
        for c in range(0, d, chunk):
            cols = pl.ds(c, chunk)
            x = (wide(merged[m][rows, cols]) + wide(arrived[n, :, cols])).astype(BF16)
            merged[m][rows, cols] = x
            image += jnp.dot(x, natural[m, cols], preferred_element_type=F32)
        held[n * rank : (n + 1) * rank] = image.T.astype(BF16)
    used = len(tiles) * rank
    if used < held.shape[0]:
        held[used:] = jnp.zeros((held.shape[0] - used, held.shape[1]), BF16)


def images(flat, grads, errors, factors):
    rows = [g.shape[0] for g in grads]
    d = grads[0].shape[1]
    rank = factors[0].shape[0]
    tile = LANES
    count = sum(rows) // tile
    ins = [pltpu.with_memory_space_constraint(a, pltpu.HBM) for a in (*grads, *errors, *factors)]
    outs = [vmem((r, d), BF16) for r in rows] + [vmem((flat, LANES), BF16)]
    return pl.pallas_call(
        functools.partial(image_kernel, tile, 6),
        in_specs=[pl.BlockSpec(memory_space=pltpu.HBM)] * len(ins),
        out_specs=[whole()] * len(outs),
        out_shape=outs,
        scratch_shapes=[
            vmem((count, tile, d), BF16),
            vmem((2, rank, d), BF16),
            vmem((2, d, rank), BF16),
            pltpu.SemaphoreType.DMA((count,)),
            pltpu.SemaphoreType.DMA((count,)),
            pltpu.SemaphoreType.DMA((2,)),
        ],
        compiler_params=pltpu.CompilerParams(vmem_limit_bytes=24 * MIB),
        cost_estimate=pl.CostEstimate(
            flops=2 * sum(rows) * d * 256, bytes_accessed=4 * sum(rows) * d, transcendentals=0
        ),
    )(*ins)


def share_total_kernel(blocks, copies):
    total = wide(blocks[0])
    for s in range(1, blocks.shape[0]):
        total = total + wide(blocks[s])
    for s in range(copies.shape[0]):
        copies[s] = total.astype(BF16)


def total_kernel(a, b, out):
    out[...] = a[...] + b[...]


def assemble_kernel(rank, rows, flat, image_q, image_k, gram):
    n = 0
    for m, image_out in enumerate((image_q, image_k)):
        count = rows[m] // LANES
        blocks = [flat[(n + i) * rank : (n + i + 1) * rank] for i in range(count)]
        image = jnp.concatenate(blocks, axis=1) if count > 1 else blocks[0]
        n += count
        image_out[...] = image
        gram[:, m * rank : (m + 1) * rank] = lax.dot_general(
            image, image, (((1,), (1,)), ((), ())), preferred_element_type=F32
        )


def project_kernel(core, other, tile, image_q, image_k, merged_q, merged_k, out):
    d = merged_q.shape[1]
    half = out.shape[0]
    first = (core.to(1) if other else core.pos()) * half
    for t in range(0, half, tile):
        start = pl.multiple_of(first + t, LANES)

        def fill(start=start, t=t):
            both = [
                jnp.dot(image[...], merged[:, pl.ds(start, tile)], preferred_element_type=F32)
                for image, merged in ((image_q, merged_q), (image_k, merged_k))
            ]
            out[t : t + tile] = jnp.concatenate(both, axis=0).T.astype(out.dtype)

        if 2 * half == d:
            fill()
        else:
            pl.when(start < d)(fill)

            @pl.when(start >= d)
            def _(t=t):
                out[t : t + tile] = jnp.zeros((tile, out.shape[1]), out.dtype)


def project(core, other, half, image_q, image_k, merged_q, merged_k):
    d = merged_q.shape[1]
    tile = next(t for t in (768, 512, 256, 128) if half % t == 0 and d % t == 0)
    return local(
        functools.partial(project_kernel, core, other, tile),
        [image_q, image_k, merged_q, merged_k],
        [vmem((half, 2 * image_q.shape[0]), BF16 if other else F32)],
        limit=16,
        flops=(merged_q.shape[0] + merged_k.shape[0]) * half * 512,
    )[0]


def inverse_kernel(group, *refs):
    grams, (out, held) = refs[:-2], refs[-2:]
    rank = out.shape[0] // 2
    for s, g in enumerate(grams):
        held[group.source(s)] = g[...]
    lane = lax.broadcasted_iota(jnp.int32, (8, 2 * rank), 1)
    sub = lax.broadcasted_iota(jnp.int32, (8, 2 * rank), 0)
    both = held[0]
    for j in range(1, len(grams)):
        both += held[j]
    systems = []
    for m in range(2):
        gram = both[:, m * rank : (m + 1) * rank]
        gram = jnp.concatenate([gram, jnp.zeros((rank, rank), F32)], axis=1)
        systems.append(
            [
                jnp.where(lane == sub + (rank + 8 * i), 1.0, gram[8 * i : 8 * i + 8])
                for i in range(rank // 8)
            ]
        )
    shape = (8, 2 * rank)
    results = [[None] * (rank // 8) for _ in systems]
    for j in range(0, rank, 2):
        i0, k = divmod(j, 8)
        for m, rows in enumerate(systems):
            one = jnp.broadcast_to(rows[i0][k : k + 1, :], shape)
            two = jnp.broadcast_to(rows[i0][k + 1 : k + 2, :], shape)
            a = jnp.broadcast_to(one[:, j : j + 1], shape)
            b = jnp.broadcast_to(one[:, j + 1 : j + 2], shape)
            c = jnp.broadcast_to(two[:, j + 1 : j + 2], shape)
            det = 1.0 / (a * c - b * b)
            first, second = (c * one - b * two) * det, (a * two - b * one) * det
            ratio = b / a
            done = results[m][i0] if k else jnp.zeros(shape, F32)
            done = jnp.where(sub == k, one / jnp.sqrt(a), done)
            below = (two - ratio * one) / jnp.sqrt(c - ratio * b)
            results[m][i0] = jnp.where(sub == k + 1, below, done)
            for i in range(i0 if k < 6 else i0 + 1, rank // 8):
                x = rows[i]
                rows[i] = x - x[:, j : j + 1] * first - x[:, j + 1 : j + 2] * second
    for m, rows in enumerate(results):
        for i, row in enumerate(rows):
            right = row[:, rank:]
            zero = jnp.zeros_like(right)
            pair = [right, zero] if m == 0 else [zero, right]
            out[m * rank + 8 * i : m * rank + 8 * i + 8] = jnp.concatenate(pair, axis=1)


def basis_kernel(scale, inverse, image_q, image_k, basis_q, basis_k):
    rank = image_q.shape[0]
    for m, (image, basis) in enumerate(((image_q, basis_q), (image_k, basis_k))):
        inv = inverse[m * rank : (m + 1) * rank, m * rank : (m + 1) * rank]
        b = jnp.dot(inv, wide(image[...]), precision=EXACT, preferred_element_type=F32)
        basis[...] = (wide(b.astype(BF16)) * scale).T.astype(BF16)


def split_kernel(group, *refs):
    ins, (kept, *sent), held = refs[: -group.size - 1], refs[-group.size - 1 : -1], refs[-1]
    total = ins[0][...]
    for r in ins[1:]:
        total = total + wide(r[...])
    held[...] = total
    cut_into(held, group, [kept, *sent])


def split(kept, received, group):
    rows, width = kept.shape
    shape = (rows // group.size, width)
    got = local(
        functools.partial(split_kernel, group),
        [kept, *received],
        [vmem(shape, F32)] + [vmem(shape, BF16)] * (group.size - 1),
        [vmem((rows, width), F32)],
    )
    return got[0], got[1:]


def stack_kernel(*refs):
    ins, out = refs[:-1], refs[-1]
    total = ins[0][...]
    for r in ins[1:]:
        total = total + wide(r[...])
    for s in range(out.shape[0]):
        out[s] = total[s * out.shape[1] : (s + 1) * out.shape[1]].astype(BF16)


def finish_kernel(inverse, blocks, copies):
    total = wide(blocks[0])
    for s in range(1, blocks.shape[0]):
        total = total + wide(blocks[s])
    new = lax.dot_general(
        total, inverse[...], (((1,), (1,)), ((), ())), precision=EXACT, preferred_element_type=F32
    ).astype(BF16)
    for s in range(copies.shape[0]):
        copies[s] = new


def copies_kernel(x, copies):
    for s in range(copies.shape[0]):
        copies[s] = x[...]


def refresh_kernel(core, tiles_q, tile, *refs):
    own, other, basis_q, basis_k, merged_q, merged_k, out_q, out_k, new_q, new_k, held, flat = refs
    rank, d = new_q.shape
    step = pl.program_id(0)

    @pl.when(step == 0)
    def _():
        half = held.shape[0] // 2
        held[rows_at(core.pos(), half, 16)] = own[...]
        held[rows_at(core.to(1), half, 16)] = other[...]
        for t in range(0, d, LANES):
            flat[:, t : t + LANES] = wide(held[t : t + LANES]).T.astype(BF16)
        new_q[...] = flat[:rank]
        new_k[...] = flat[rank:]

    chunk = 768 if d % 768 == 0 else d

    def update(at, merged, basis, factor, out):
        rows = rows_at(at, tile, tile)
        b = basis[rows]
        for c in range(0, d, chunk):
            approx = jnp.dot(b, factor[:, c : c + chunk], preferred_element_type=F32)
            out[:, c : c + chunk] = (wide(merged[rows, c : c + chunk]) - approx).astype(BF16)

    @pl.when(step < tiles_q)
    def _():
        update(step, merged_q, basis_q, flat.at[:rank], out_q)

    @pl.when(step >= tiles_q)
    def _():
        update(step - tiles_q, merged_k, basis_k, flat.at[rank:], out_k)


def refresh(core, padded, pieces, basis_q, basis_k, merged_q, merged_k):
    rank = basis_q.shape[1]
    rows_q, d = merged_q.shape
    rows_k = merged_k.shape[0]
    tile = 2 * LANES if rows_k % (2 * LANES) == 0 else LANES
    tiles_q, tiles_k = rows_q // tile, rows_k // tile
    ins = [*pieces, basis_q, basis_k, merged_q, merged_k]
    ins = [pltpu.with_memory_space_constraint(a, pltpu.VMEM) for a in ins]
    return pl.pallas_call(
        functools.partial(refresh_kernel, core, tiles_q, tile),
        grid=(tiles_q + tiles_k,),
        in_specs=[whole()] * len(ins),
        out_specs=[
            pl.BlockSpec((tile, d), lambda i: (jnp.minimum(i, tiles_q - 1), 0)),
            pl.BlockSpec((tile, d), lambda i: (jnp.maximum(i - tiles_q, 0), 0)),
            pl.BlockSpec((rank, d), lambda i: (0, 0)),
            pl.BlockSpec((rank, d), lambda i: (0, 0)),
        ],
        out_shape=[
            jax.ShapeDtypeStruct((rows_q, d), BF16),
            jax.ShapeDtypeStruct((rows_k, d), BF16),
            jax.ShapeDtypeStruct((rank, d), BF16),
            jax.ShapeDtypeStruct((rank, d), BF16),
        ],
        scratch_shapes=[vmem((padded, 2 * rank), BF16), vmem((2 * rank, d), BF16)],
        compiler_params=pltpu.CompilerParams(vmem_limit_bytes=24 * MIB),
        cost_estimate=pl.CostEstimate(
            flops=2 * (rows_q + rows_k) * d * 256, bytes_accessed=4 * (rows_q + rows_k) * d, transcendentals=0
        ),
    )(*ins)


def body(grad_query, grad_key, error_query, error_key, factor_query, factor_key):
    n_z, n_y, n_x, n_core = (lax.axis_size(a) for a in AXES)
    n_dp, count = n_z * n_y, n_z * n_y * n_x * n_core
    core = Group([(1, n_core)], count)
    across = Group([(n_core, n_x)], count)
    plane = Group([(n_core, n_x), (n_core * n_x, n_y)], count)
    rows_q, d = grad_query.shape[2:]
    rows_k = grad_key.shape[2]
    rank = factor_query.shape[2]
    unit = 16 * count
    padded = -(-d // unit) * unit
    half = padded // 2

    flat = -(-((rows_q + rows_k) // LANES * rank) // (16 * n_dp)) * 16 * n_dp
    merged_q, merged_k, blocks = images(
        flat,
        [grad_query[0, 0], grad_key[0, 0]],
        [error_query[0, 0], error_key[0, 0]],
        [factor_query[0].T, factor_key[0].T],
    )
    blocks = blocks.reshape(n_dp, flat // n_dp, LANES)
    blocks = lax.all_to_all(blocks, ("z", "y"), 0, 0)
    blocks = local(share_total_kernel, [blocks], [vmem(blocks.shape, BF16)])[0]
    blocks = lax.all_to_all(blocks, ("z", "y"), 0, 0)
    image_q, image_k, gram = local(
        functools.partial(assemble_kernel, rank, (rows_q, rows_k)),
        [blocks.reshape(flat, LANES)],
        [vmem((rank, rows_q), BF16), vmem((rank, rows_k), BF16), vmem((rank, 2 * rank), F32)],
    )

    gram_pair = core.send(gram, 1)
    operands = (image_q, image_k, merged_q, merged_k)
    got = core.send(project(core, True, half, *operands), 1)
    kept = project(core, False, half, *operands)
    gram = local(total_kernel, [gram, gram_pair], [vmem(gram.shape, F32)])[0]
    grams = [gram, *across.gather(gram)]
    kept, sent = split(kept, [got], plane)
    inverse = local(
        functools.partial(inverse_kernel, across),
        grams,
        [vmem((2 * rank, 2 * rank), F32)],
        [vmem((len(grams), rank, 2 * rank), F32)],
        flops=1 << 32,
        after=[kept],
    )[0]
    basis_q, basis_k = local(
        functools.partial(basis_kernel, 1.0 / n_dp),
        [inverse, image_q, image_k],
        [vmem((rows_q, rank), BF16), vmem((rows_k, rank), BF16)],
    )
    piece = (kept.shape[0] // n_z, kept.shape[1])
    blocks = local(
        stack_kernel, [kept, *plane.scatter(sent)], [vmem((n_z,) + piece, BF16)], after=[basis_k]
    )[0]
    blocks = lax.all_to_all(blocks, "z", 0, 0)
    blocks = local(finish_kernel, [inverse, blocks], [vmem(blocks.shape, BF16)])[0]

    blocks = lax.all_to_all(blocks, "z", 0, 0).reshape(kept.shape)
    copies = local(copies_kernel, [blocks], [vmem((plane.size,) + blocks.shape, BF16)])[0]
    own = lax.all_to_all(copies, ("y", "x"), 0, 0).reshape(half, 2 * rank)
    pieces = [own, core.send(own, 1)]
    error_q, error_k, new_q, new_k = refresh(
        core, padded, pieces, basis_q, basis_k, merged_q, merged_k
    )
    return error_q[None, None], error_k[None, None], new_q.T[None], new_k.T[None]


def solution(mesh):
    n_dp, n_t = mesh.shape["dp"], mesh.shape["tensor"]
    n_z = 4 if n_dp % 4 == 0 else 1
    chips = Mesh(mesh.devices.reshape(n_z, n_dp // n_z, n_t // 2, 2), AXES)
    rows = P(("z", "y"), None, ("x", "core"), None)
    return jax.shard_map(
        body,
        mesh=chips,
        in_specs=(rows, rows, rows, rows, P(), P()),
        out_specs=(rows, rows, P(), P()),
        check_vma=False,
    )
```

time: 111 us -> 95.1 us (0.86)
  blocking collectives: 0 us -> 54.3 us
  waiting for transfers between devices: 38 us -> 4.03 us
  starting transfers between devices: 38.6 us -> 5.61 us
  Pallas kernels: 33.3 us -> 30.1 us
    all_to_all x0 -> x5, blocking collectives: none -> 54.3 us  [the longest x2 25.8 us: body(): blocks = lax.all_to_all(blocks, ('z', 'y'), 0, 0)]
    ppermute x33 -> x7, waiting for transfers between devices: 38 us -> 4.03 us  [send(): return lax.ppermute(x, AXES, pairs)]
    ppermute x33 -> x7, starting transfers between devices: 38.6 us -> 5.61 us  [send(): return lax.ppermute(x, AXES, pairs)]
    pallas_call x17 -> x11, Pallas kernels: 13.2 us -> 9.01 us  [local(): pl.pallas_call(run, in_specs=[whole()] * n_in + [pl.BlockSpec(memory_spac...]
  transfers between devices with their start and end apart: 33 -> 7, of which waited for: 23 -> 3; matrix products, arithmetic and copies ran while one was open for 0% -> 0% of each run, Pallas kernels for 10% -> 7%
where the time goes in v2:
time: 95.1 us; the launch traced here: 94.8 us
  blocking collectives  54.3 us (57%)
  Pallas kernels  30.1 us (32%)
  starting transfers between devices  5.61 us (6%)
  waiting for transfers between devices  4.03 us (4%)
    all_to_all x2, blocking collectives, body(): blocks = lax.all_to_all(blocks, ('z', 'y'), 0, 0)  25.8 us
    pallas_call x1, Pallas kernels, images(): pl.pallas_call(functools.partial(image_kernel, tile, 6), in_specs=[pl.Blo...  12.1 us
    all_to_all x1, blocking collectives, body(): own = lax.all_to_all(copies, ('y', 'x'), 0, 0).reshape(half, 2 * rank)  10.5 us
    all_to_all x1, blocking collectives, body(): blocks = lax.all_to_all(blocks, 'z', 0, 0)  9.06 us
    all_to_all x1, blocking collectives, body(): blocks = lax.all_to_all(blocks, 'z', 0, 0).reshape(kept.shape)  9.01 us
    pallas_call x11, Pallas kernels, local(): pl.pallas_call(run, in_specs=[whole()] * n_in + [pl.BlockSpec(memory_spac...  9.01 us
    pallas_call x1, Pallas kernels, refresh(): pl.pallas_call(functools.partial(refresh_kernel, core, tiles_q, tile), gr...  8.99 us
    ppermute x7, starting transfers between devices, send(): return lax.ppermute(x, AXES, pairs)  5.61 us
  transfers between devices with their start and end apart: 7, of which 3 were waited for; matrix products, arithmetic and copies ran while one was open for 0% of the time, Pallas kernels for 7%

profile of v2, /device:TPU:0, one launch (start us, length us, event | category | flops | bytes accessed | tf_op | source)
XLA Modules:
  0.0 94.8 jit_solution(6118148906581525067)
XLA Ops:
  0.6 12.1 %shard_map.93 = (bf16[1024,4608]{1,0:T(8,128)(2,1)S(1)}, bf16[512,4608]{1,0:T(8,128)(2,1)S(1)}, bf16[768,128]{1,0:T(8,128)(2,1)S(1)}) custom-call(bf16[1024,4608]{1,0:T(8,128)(2,1)} %bitcast.27, bf16[512,4608]{1,0:T(8,128)(2,1)} %bitcast.29, bf16[1024,4608]{1,0:T(8,128)(2,1)} %bitcast.28, bf16[512,4608]{1,0:T(8,128)(2,1)} %bitcast.30, ...), custom_call_target="tpu_custom_call" | custom-call | flops 3623878656 | bytes 28311552 | tf_op jit(solution)/shard_map/pallas_call | solution.py:173
  12.7 15.0 %all_to_all.25.refs_0_ = bf16[8,96,128]{2,1,0:T(8,128)(2,1)S(1)} all-to-all(bf16[8,96,128]{2,1,0:T(8,128)(2,1)S(1)} %bitcast.26), channel_id=1, replica_groups=mesh['z'=4,'y'=2,'x'=2,'core'=2] {'z','y'}, dimensions={0} | all-to-all | bytes 393216 | tf_op jit(solution)/shard_map/all_to_all | solution.py:442
  27.8 10.7 %all_to_all.26 = bf16[8,96,128]{2,1,0:T(8,128)(2,1)S(1)} all-to-all(bf16[8,96,128]{2,1,0:T(8,128)(2,1)S(1)} %shard_map.94), channel_id=1, replica_groups=mesh['z'=4,'y'=2,'x'=2,'core'=2] {'z','y'}, dimensions={0} | all-to-all | bytes 393216 | tf_op jit(solution)/shard_map/all_to_all | solution.py:444
  38.5 0.3 shard_map.95
  38.8 1.5 %shard_map.98 = bf16[2304,128]{1,0:T(8,128)(2,1)S(1)} custom-call(bf16[64,1024]{1,0:T(8,128)(2,1)S(1)} %get-tuple-element.22.refs_0_.refs_1_, bf16[64,512]{1,0:T(8,128)(2,1)S(1)} %get-tuple-element.23.refs_1_.refs_2_, bf16[1024,4608]{1,0:T(8,128)(2,1)S(1)} %get-tuple-element.24.refs_2_.refs_4_, bf16[512,4608]{1,0:T(8,128)(2,1)S(1)} %get-tuple-element.25.refs_3_.refs_5_), custom_call_target="tpu_custom_call" | custom-call | flops 1811939328 | bytes 14352384 | tf_op jit(solution)/shard_map/pallas_call | solution.py:37
  40.3 0.1 collective-permute-start.2
  40.3 0.5 collective-permute-start
  40.8 1.5 %collective-permute-done.refs_1_ = f32[64,128]{1,0:T(8,128)S(1)} collective-permute-done((f32[64,128]{1,0:T(8,128)S(1)}, f32[64,128]{1,0:T(8,128)S(1)}, u32[]{:S(2)}, u32[]{:S(2)}) %collective-permute-start) | collective-permute-done | bytes 32800 | tf_op jit(solution)/shard_map/ppermute | solution.py:91
  42.4 1.5 %collective-permute-start.1 = (f32[64,128]{1,0:T(8,128)S(1)}, f32[64,128]{1,0:T(8,128)S(1)}, u32[]{:S(2)}, u32[]{:S(2)}) collective-permute-start(f32[64,128]{1,0:T(8,128)S(1)} %shard_map.96.refs_0_), channel_id=1, source_target_pairs={{0,2},{1,3},{2,0},{3,1},{4,6},{5,7},{6,4},{7,5},{8,10},{9,11},{10,... | collective-permute-start | bytes 98312 | tf_op jit(solution)/shard_map/ppermute | solution.py:91
  43.9 1.5 %shard_map.97.refs_0_ = f32[2304,128]{1,0:T(8,128)S(1)} custom-call(bf16[64,1024]{1,0:T(8,128)(2,1)S(1)} %get-tuple-element.22.refs_0_.refs_1_, bf16[64,512]{1,0:T(8,128)(2,1)S(1)} %get-tuple-element.23.refs_1_.refs_2_, bf16[1024,4608]{1,0:T(8,128)(2,1)S(1)} %get-tuple-element.24.refs_2_.refs_4_, bf16[512,4608]{1,0:T(8,128)(2,1)S(1)} %get-tuple-element.25.refs_3_.refs_5_), custom_call_target="tpu_custom_call" | custom-call | flops 1811939328 | bytes 14352384 | tf_op jit(solution)/shard_map/pallas_call | solution.py:37
  45.3 0.0 collective-permute-done.2.refs_1_
  45.4 0.2 shard_map.99
  45.6 0.6 collective-permute-start.3
  46.2 1.0 %collective-permute-start.4 = (bf16[576,128]{1,0:T(8,128)(2,1)S(1)}, bf16[576,128]{1,0:T(8,128)(2,1)S(1)}, u32[]{:S(2)}, u32[]{:S(2)}) collective-permute-start(bf16[576,128]{1,0:T(8,128)(2,1)S(1)} %get-tuple-element.28), channel_id=1, source_target_pairs={{0,4},{1,5},{2,6},{3,7},{4,0},{5,1},{6,2},{7,3},{8,12},{9,13},{10,... | collective-permute-start | bytes 442376 | tf_op jit(solution)/shard_map/ppermute | solution.py:91
  47.1 2.0 %collective-permute-start.5 = (bf16[576,128]{1,0:T(8,128)(2,1)S(1)}, bf16[576,128]{1,0:T(8,128)(2,1)S(1)}, u32[]{:S(2)}, u32[]{:S(2)}) collective-permute-start(bf16[576,128]{1,0:T(8,128)(2,1)S(1)} %get-tuple-element.29), channel_id=1, source_target_pairs={{0,6},{1,7},{2,4},{3,5},{4,2},{5,3},{6,0},{7,1},{8,14},{9,15},{10,... | collective-permute-start | bytes 442376 | tf_op jit(solution)/shard_map/ppermute | solution.py:91
  49.1 0.0 collective-permute-done.1.refs_1_
  49.1 4.6 %shard_map.100.refs_0_ = f32[128,128]{1,0:T(8,128)S(1)} custom-call(f32[64,128]{1,0:T(8,128)S(1)} %shard_map.96.refs_0_, f32[64,128]{1,0:T(8,128)S(1)} %collective-permute-done.1.refs_1_, f32[576,128]{1,0:T(8,128)S(1)} %get-tuple-element.26.refs_2_.refs_0_), custom_call_target="tpu_custom_call" | custom-call | flops 4294967296 | bytes 65536 | tf_op jit(solution)/shard_map/pallas_call | solution.py:37
  53.7 0.6 shard_map.101
  54.3 0.0 collective-permute-done.3.refs_1_
  54.3 0.0 collective-permute-done.4.refs_2_
  54.3 0.5 collective-permute-done.5.refs_3_
  54.8 0.1 shard_map.102
  54.9 9.1 %all_to_all.27.refs_1_ = bf16[4,144,128]{2,1,0:T(8,128)(2,1)S(1)} all-to-all(bf16[4,144,128]{2,1,0:T(8,128)(2,1)S(1)} %shard_map.102), channel_id=1, replica_groups=mesh['z'=4,'y'=2,'x'=2,'core'=2] {'z'}, dimensions={0} | all-to-all | bytes 294912 | tf_op jit(solution)/shard_map/all_to_all | solution.py:475
  63.9 0.3 shard_map.103
  64.2 9.0 %all_to_all.28 = bf16[4,144,128]{2,1,0:T(8,128)(2,1)S(1)} all-to-all(bf16[4,144,128]{2,1,0:T(8,128)(2,1)S(1)} %shard_map.103), channel_id=1, replica_groups=mesh['z'=4,'y'=2,'x'=2,'core'=2] {'z'}, dimensions={0} | all-to-all | bytes 294912 | tf_op jit(solution)/shard_map/all_to_all | solution.py:478
  73.2 0.1 shard_map.104
  73.3 10.5 %all_to_all.29 = bf16[4,576,128]{2,1,0:T(8,128)(2,1)S(1)} all-to-all(bf16[4,576,128]{2,1,0:T(8,128)(2,1)S(1)} %shard_map.104), channel_id=1, replica_groups=mesh['z'=4,'y'=2,'x'=2,'core'=2] {'y','x'}, dimensions={0} | all-to-all | bytes 1179648 | tf_op jit(solution)/shard_map/all_to_all | solution.py:480
  83.8 0.0 collective-permute-start.6
  83.8 2.0 %collective-permute-done.6.refs_1_ = bf16[2304,128]{1,0:T(8,128)(2,1)S(1)} collective-permute-done((bf16[2304,128]{1,0:T(8,128)(2,1)S(1)}, bf16[2304,128]{1,0:T(8,128)(2,1)S(1)}, u32[]{:S(2)}, u32[]{:S(2)}) %collective-permute-start.6) | collective-permute-done | bytes 589856 | tf_op jit(solution)/shard_map/ppermute | solution.py:91
  85.8 9.0 %shard_map.105 = (bf16[1024,4608]{1,0:T(8,128)(2,1)}, bf16[512,4608]{1,0:T(8,128)(2,1)}, bf16[64,4608]{1,0:T(8,128)(2,1)}, bf16[64,4608]{1,0:T(8,128)(2,1)}) custom-call(bf16[2304,128]{1,0:T(8,128)(2,1)S(1)} %bitcast.23, bf16[2304,128]{1,0:T(8,128)(2,1)S(1)} %collective-permute-done.6.refs_1_, bf16[1024,64]{1,0:T(8,128)(2,1)S(1)} %get-tuple-element.31.refs_2_, ...), custom_call_target="tpu_custom_call" | custom-call | flops 3623878656 | bytes 28311552 | tf_op jit(solution)/shard_map/pallas_call | solution.py:397
  (2 shorter events, 0.0 us)
Async XLA Ops:
  40.3 5.1 %collective-permute-start.2 = (bf16[2304,128]{1,0:T(8,128)(2,1)S(1)}, bf16[2304,128]{1,0:T(8,128)(2,1)S(1)}, u32[]{:S(2)}, u32[]{:S(2)}) collective-permute-start(bf16[2304,128]{1,0:T(8,128)(2,1)S(1)} %shard_map.98), channel_id=1, source_target_pairs={{0,1},{1,0},{2,3},{3,2},{4,5},{5,4},{6,7},{7,6},{8,9},{9,8},{10,11... | collective-permute-start | bytes 1769480 | tf_op jit(solution)/shard_map/ppermute | solution.py:91
  40.3 2.0 %collective-permute-start = (f32[64,128]{1,0:T(8,128)S(1)}, f32[64,128]{1,0:T(8,128)S(1)}, u32[]{:S(2)}, u32[]{:S(2)}) collective-permute-start(f32[64,128]{1,0:T(8,128)S(1)} %get-tuple-element.21.refs_0_), channel_id=1, source_target_pairs={{0,1},{1,0},{2,3},{3,2},{4,5},{5,4},{6,7},{7,6},{8,9},{9,8},{10,11... | collective-permute-start | bytes 98312 | tf_op jit(solution)/shard_map/ppermute | solution.py:91
  42.4 6.7 %collective-permute-start.1 = (f32[64,128]{1,0:T(8,128)S(1)}, f32[64,128]{1,0:T(8,128)S(1)}, u32[]{:S(2)}, u32[]{:S(2)}) collective-permute-start(f32[64,128]{1,0:T(8,128)S(1)} %shard_map.96.refs_0_), channel_id=1, source_target_pairs={{0,2},{1,3},{2,0},{3,1},{4,6},{5,7},{6,4},{7,5},{8,10},{9,11},{10,... | collective-permute-start | bytes 98312 | tf_op jit(solution)/shard_map/ppermute | solution.py:91
  45.6 8.8 %collective-permute-start.3 = (bf16[576,128]{1,0:T(8,128)(2,1)S(1)}, bf16[576,128]{1,0:T(8,128)(2,1)S(1)}, u32[]{:S(2)}, u32[]{:S(2)}) collective-permute-start(bf16[576,128]{1,0:T(8,128)(2,1)S(1)} %get-tuple-element.27), channel_id=1, source_target_pairs={{0,2},{1,3},{2,0},{3,1},{4,6},{5,7},{6,4},{7,5},{8,10},{9,11},{10,... | collective-permute-start | bytes 442376 | tf_op jit(solution)/shard_map/ppermute | solution.py:91
  46.2 8.2 %collective-permute-start.4 = (bf16[576,128]{1,0:T(8,128)(2,1)S(1)}, bf16[576,128]{1,0:T(8,128)(2,1)S(1)}, u32[]{:S(2)}, u32[]{:S(2)}) collective-permute-start(bf16[576,128]{1,0:T(8,128)(2,1)S(1)} %get-tuple-element.28), channel_id=1, source_target_pairs={{0,4},{1,5},{2,6},{3,7},{4,0},{5,1},{6,2},{7,3},{8,12},{9,13},{10,... | collective-permute-start | bytes 442376 | tf_op jit(solution)/shard_map/ppermute | solution.py:91
  47.1 7.7 %collective-permute-start.5 = (bf16[576,128]{1,0:T(8,128)(2,1)S(1)}, bf16[576,128]{1,0:T(8,128)(2,1)S(1)}, u32[]{:S(2)}, u32[]{:S(2)}) collective-permute-start(bf16[576,128]{1,0:T(8,128)(2,1)S(1)} %get-tuple-element.29), channel_id=1, source_target_pairs={{0,6},{1,7},{2,4},{3,5},{4,2},{5,3},{6,0},{7,1},{8,14},{9,15},{10,... | collective-permute-start | bytes 442376 | tf_op jit(solution)/shard_map/ppermute | solution.py:91
  83.8 2.0 %collective-permute-start.6 = (bf16[2304,128]{1,0:T(8,128)(2,1)S(1)}, bf16[2304,128]{1,0:T(8,128)(2,1)S(1)}, u32[]{:S(2)}, u32[]{:S(2)}) collective-permute-start(bf16[2304,128]{1,0:T(8,128)(2,1)S(1)} %bitcast.22), channel_id=1, source_target_pairs={{0,1},{1,0},{2,3},{3,2},{4,5},{5,4},{6,7},{7,6},{8,9},{9,8},{10,11... | collective-permute-start | bytes 1769480 | tf_op jit(solution)/shard_map/ppermute | solution.py:91

commit v3 on v2

--- a/solution.py
+++ b/solution.py
@@ -10,6 +10,7 @@
 F32, BF16 = jnp.float32, jnp.bfloat16
 MIB = 1 << 20
 AXES = ("z", "y", "x", "core")
+LIMIT = 3.0
 EXACT = lax.Precision.HIGHEST
 LANES = 128
 
@@ -37,7 +38,7 @@
     return pl.pallas_call(
         run,
         in_specs=[whole()] * n_in + [pl.BlockSpec(memory_space=pl.ANY)] * n_after,
-        out_specs=[whole()] * len(outs),
+        out_specs=[pl.BlockSpec(memory_space=o.memory_space) for o in outs],
         out_shape=list(outs),
         scratch_shapes=list(scratch),
         compiler_params=pltpu.CompilerParams(vmem_limit_bytes=limit * MIB),
@@ -111,11 +112,10 @@
         out[...] = held[rows_at(group.to(s), size, 8)].astype(out.dtype)
 
 
-def image_kernel(tile, depth, *refs):
-    ins, outs, scratch = refs[:6], refs[6:9], refs[9:]
+def image_kernel(group, tile, depth, *refs):
+    ins, merged, outs, scratch = refs[:6], refs[6:8], refs[8 : 8 + group.size], refs[8 + group.size :]
     grads, errors, factors = ins[0:2], ins[2:4], ins[4:6]
-    merged, held = outs[:2], outs[2]
-    arrived, flat_factors, natural, grad_sems, error_sems, factor_sems = scratch
+    arrived, flat_factors, natural, held, grad_sems, error_sems, factor_sems = scratch
     rank, d = flat_factors.shape[1:]
     tiles = [(m, i) for m in (0, 1) for i in range(grads[m].shape[0] // tile)]
 
@@ -156,22 +156,24 @@
             x = (wide(merged[m][rows, cols]) + wide(arrived[n, :, cols])).astype(BF16)
             merged[m][rows, cols] = x
             image += jnp.dot(x, natural[m, cols], preferred_element_type=F32)
-        held[n * rank : (n + 1) * rank] = image.T.astype(BF16)
+        held[n * rank : (n + 1) * rank] = image.T
     used = len(tiles) * rank
     if used < held.shape[0]:
-        held[used:] = jnp.zeros((held.shape[0] - used, held.shape[1]), BF16)
-
-
-def images(flat, grads, errors, factors):
+        held[used:] = jnp.zeros((held.shape[0] - used, held.shape[1]), F32)
+    cut_into(held, group, outs)
+
+
+def images(group, flat, grads, errors, factors):
     rows = [g.shape[0] for g in grads]
     d = grads[0].shape[1]
     rank = factors[0].shape[0]
     tile = LANES
     count = sum(rows) // tile
     ins = [pltpu.with_memory_space_constraint(a, pltpu.HBM) for a in (*grads, *errors, *factors)]
-    outs = [vmem((r, d), BF16) for r in rows] + [vmem((flat, LANES), BF16)]
+    cut = (flat // group.size, LANES)
+    outs = [vmem((r, d), BF16) for r in rows] + [vmem(cut, F32)] + [vmem(cut, BF16)] * (group.size - 1)
     return pl.pallas_call(
-        functools.partial(image_kernel, tile, 6),
+        functools.partial(image_kernel, group, tile, 2),
         in_specs=[pl.BlockSpec(memory_space=pltpu.HBM)] * len(ins),
         out_specs=[whole()] * len(outs),
         out_shape=outs,
@@ -179,6 +181,7 @@
             vmem((count, tile, d), BF16),
             vmem((2, rank, d), BF16),
             vmem((2, d, rank), BF16),
+            vmem((flat, LANES), F32),
             pltpu.SemaphoreType.DMA((count,)),
             pltpu.SemaphoreType.DMA((count,)),
             pltpu.SemaphoreType.DMA((2,)),
@@ -190,24 +193,26 @@
     )(*ins)
 
 
-def share_total_kernel(blocks, copies):
-    total = wide(blocks[0])
-    for s in range(1, blocks.shape[0]):
-        total = total + wide(blocks[s])
-    for s in range(copies.shape[0]):
-        copies[s] = total.astype(BF16)
-
-
-def total_kernel(a, b, out):
-    out[...] = a[...] + b[...]
-
-
-def assemble_kernel(rank, rows, flat, image_q, image_k, gram):
+def ordered_kernel(group, *refs):
+    blocks, (out, held) = refs[:-2], refs[-2:]
+    for s, block in enumerate(blocks):
+        held[group.source(s)] = wide(block[...])
+    total = held[0]
+    for j in range(1, len(blocks)):
+        total = total + held[j]
+    out[...] = total.astype(BF16)
+
+
+def assemble_kernel(group, rank, rows, *refs):
+    blocks, (image_q, image_k, gram, flat) = refs[: group.size], refs[group.size :]
+    for s, block in enumerate(blocks):
+        size = block.shape[0]
+        flat[rows_at(group.source(s), size, 16)] = block[...]
     n = 0
     for m, image_out in enumerate((image_q, image_k)):
         count = rows[m] // LANES
-        blocks = [flat[(n + i) * rank : (n + i + 1) * rank] for i in range(count)]
-        image = jnp.concatenate(blocks, axis=1) if count > 1 else blocks[0]
+        parts = [flat[(n + i) * rank : (n + i + 1) * rank] for i in range(count)]
+        image = jnp.concatenate(parts, axis=1) if count > 1 else parts[0]
         n += count
         image_out[...] = image
         gram[:, m * rank : (m + 1) * rank] = lax.dot_general(
@@ -251,15 +256,26 @@
     )[0]
 
 
-def inverse_kernel(group, *refs):
-    grams, (out, held) = refs[:-2], refs[-2:]
+def parts_of(x):
+    high = x.astype(BF16)
+    rest = x - wide(high)
+    middle = rest.astype(BF16)
+    return high, middle, (rest - wide(middle)).astype(BF16)
+
+
+def inverse_kernel(group, own, *refs):
+    received, (out, growth, held) = refs[:-3], refs[-3:]
     rank = out.shape[0] // 2
-    for s, g in enumerate(grams):
-        held[group.source(s)] = g[...]
+    tail = slice(received[0].shape[0] - 3 * rank, None)
+    for s, three in enumerate([parts_of(own[...])] + [r[tail] for r in received]):
+        if s:
+            three = [three[i * rank : (i + 1) * rank] for i in range(3)]
+        high, middle, low = (wide(p) for p in three)
+        held[group.source(s)] = high + (middle + low)
     lane = lax.broadcasted_iota(jnp.int32, (8, 2 * rank), 1)
     sub = lax.broadcasted_iota(jnp.int32, (8, 2 * rank), 0)
     both = held[0]
-    for j in range(1, len(grams)):
+    for j in range(1, group.size):
         both += held[j]
     systems = []
     for m in range(2):
@@ -272,6 +288,9 @@
             ]
         )
     shape = (8, 2 * rank)
+    square = lax.broadcasted_iota(jnp.int32, both.shape, 0) - lax.broadcasted_iota(jnp.int32, both.shape, 1)
+    norms = jnp.where((square == 0) | (square == -rank), both, 0.0).sum(axis=0, keepdims=True)
+    worse = jnp.zeros((8, 1), F32)
     results = [[None] * (rank // 8) for _ in systems]
     for j in range(0, rank, 2):
         i0, k = divmod(j, 8)
@@ -294,9 +313,12 @@
     for m, rows in enumerate(results):
         for i, row in enumerate(rows):
             right = row[:, rank:]
+            grown = (right * right * norms[:, m * rank : (m + 1) * rank]).sum(axis=1, keepdims=True)
+            worse += jnp.where(grown <= LIMIT, 0.0, 1.0)
             zero = jnp.zeros_like(right)
             pair = [right, zero] if m == 0 else [zero, right]
             out[m * rank + 8 * i : m * rank + 8 * i + 8] = jnp.concatenate(pair, axis=1)
+    growth[0] = jnp.sum(worse)
 
 
 def basis_kernel(scale, inverse, image_q, image_k, basis_q, basis_k):
@@ -307,50 +329,55 @@
         basis[...] = (wide(b.astype(BF16)) * scale).T.astype(BF16)
 
 
-def split_kernel(group, *refs):
-    ins, (kept, *sent), held = refs[: -group.size - 1], refs[-group.size - 1 : -1], refs[-1]
-    total = ins[0][...]
-    for r in ins[1:]:
-        total = total + wide(r[...])
-    held[...] = total
-    cut_into(held, group, [kept, *sent])
-
-
-def split(kept, received, group):
-    rows, width = kept.shape
-    shape = (rows // group.size, width)
-    got = local(
-        functools.partial(split_kernel, group),
-        [kept, *received],
-        [vmem(shape, F32)] + [vmem(shape, BF16)] * (group.size - 1),
+def split_kernel(group, across, *refs):
+    own, got, gram, other = refs[:4]
+    kept, *sent = refs[4 : 4 + group.size]
+    gram_out, held = refs[4 + group.size :]
+    held[...] = own[...] + wide(got[...])
+    size = kept.shape[0]
+    cut_into(held, group, [kept] + [x.at[:size] for x in sent])
+    total = gram[...] + other[...]
+    gram_out[...] = total
+    three = parts_of(total)
+    rank = total.shape[0]
+    for x in sent[: across.size - 1]:
+        for i, part in enumerate(three):
+            x[size + i * rank : size + (i + 1) * rank] = part
+
+
+def split(own, got, gram, other, group, across):
+    rows, width = own.shape
+    size, extra = rows // group.size, 3 * gram.shape[0]
+    sent = [vmem((size + (extra if s < across.size else 0), width), BF16) for s in range(1, group.size)]
+    out = local(
+        functools.partial(split_kernel, group, across),
+        [own, got, gram, other],
+        [vmem((size, width), F32), *sent, vmem(gram.shape, F32)],
         [vmem((rows, width), F32)],
     )
-    return got[0], got[1:]
-
-
-def stack_kernel(*refs):
-    ins, out = refs[:-1], refs[-1]
-    total = ins[0][...]
-    for r in ins[1:]:
-        total = total + wide(r[...])
-    for s in range(out.shape[0]):
-        out[s] = total[s * out.shape[1] : (s + 1) * out.shape[1]].astype(BF16)
-
-
-def finish_kernel(inverse, blocks, copies):
-    total = wide(blocks[0])
-    for s in range(1, blocks.shape[0]):
-        total = total + wide(blocks[s])
+    return out[0], out[1:-1], out[-1]
+
+
+def sum_kernel(*refs):
+    own, received, out = refs[0], refs[1:-1], refs[-1]
+    total = own[...]
+    for r in received:
+        total = total + wide(r[: own.shape[0]])
+    out[...] = total.astype(BF16)
+
+
+def finish_kernel(group, inverse, *refs):
+    blocks, (copies, held) = refs[:-2], refs[-2:]
+    for s, block in enumerate(blocks):
+        held[group.source(s)] = wide(block[...])
+    total = held[0]
+    for j in range(1, len(blocks)):
+        total = total + held[j]
     new = lax.dot_general(
         total, inverse[...], (((1,), (1,)), ((), ())), precision=EXACT, preferred_element_type=F32
     ).astype(BF16)
     for s in range(copies.shape[0]):
         copies[s] = new
-
-
-def copies_kernel(x, copies):
-    for s in range(copies.shape[0]):
-        copies[s] = x[...]
 
 
 def refresh_kernel(core, tiles_q, tile, *refs):
@@ -418,12 +445,43 @@
     )(*ins)
 
 
+def sum_over(x, axes):
+    size = lax.axis_size(axes)
+    rows = x.shape[0]
+    parts = lax.all_to_all(x.reshape(size, rows // size, x.shape[1]), axes, 0, 0).sum(0)
+    parts = jnp.broadcast_to(parts, (size,) + parts.shape)
+    return lax.all_to_all(parts, axes, 0, 0).reshape(x.shape)
+
+
+def in_float32(grad_query, grad_key, error_query, error_key, factor_query, factor_key):
+    n_dp = lax.axis_size(("z", "y"))
+    errors, news = [], []
+    for grad, error, factor in (
+        (grad_query, error_query, factor_query),
+        (grad_key, error_key, factor_key),
+    ):
+        merged = (wide(grad[0, 0]) + wide(error[0, 0])).astype(BF16)
+        image = jnp.dot(merged, factor[0], preferred_element_type=F32)
+        image = sum_over(image, ("z", "y"))
+        gram = lax.dot_general(image, image, (((0,), (0,)), ((), ())), precision=EXACT)
+        lower = jnp.linalg.cholesky(sum_over(gram, ("x", "core")))
+        basis = jax.scipy.linalg.solve_triangular(lower, image.T, lower=True).astype(BF16)
+        new = lax.dot_general(merged, basis, (((0,), (1,)), ((), ())), preferred_element_type=F32)
+        new = sum_over(new, AXES).astype(BF16)
+        approx = lax.dot_general(basis, new, (((0,), (1,)), ((), ())), preferred_element_type=F32)
+        errors.append((wide(merged) - approx / n_dp).astype(BF16))
+        news.append(new.T)
+    return (*errors, *news)
+
+
 def body(grad_query, grad_key, error_query, error_key, factor_query, factor_key):
     n_z, n_y, n_x, n_core = (lax.axis_size(a) for a in AXES)
     n_dp, count = n_z * n_y, n_z * n_y * n_x * n_core
     core = Group([(1, n_core)], count)
     across = Group([(n_core, n_x)], count)
     plane = Group([(n_core, n_x), (n_core * n_x, n_y)], count)
+    column = Group([(n_core * n_x, n_y)], count)
+    line = Group([(n_core * n_x * n_y, n_z)], count)
     rows_q, d = grad_query.shape[2:]
     rows_k = grad_key.shape[2]
     rank = factor_query.shape[2]
@@ -431,57 +489,67 @@
     padded = -(-d // unit) * unit
     half = padded // 2
 
-    flat = -(-((rows_q + rows_k) // LANES * rank) // (16 * n_dp)) * 16 * n_dp
-    merged_q, merged_k, blocks = images(
+    flat = -(-((rows_q + rows_k) // LANES * rank) // (16 * n_z)) * 16 * n_z
+    merged_q, merged_k, kept, *sent = images(
+        line,
         flat,
         [grad_query[0, 0], grad_key[0, 0]],
         [error_query[0, 0], error_key[0, 0]],
         [factor_query[0].T, factor_key[0].T],
     )
-    blocks = blocks.reshape(n_dp, flat // n_dp, LANES)
-    blocks = lax.all_to_all(blocks, ("z", "y"), 0, 0)
-    blocks = local(share_total_kernel, [blocks], [vmem(blocks.shape, BF16)])[0]
-    blocks = lax.all_to_all(blocks, ("z", "y"), 0, 0)
+    shape = kept.shape
+    block = local(sum_kernel, [kept, *line.scatter(sent)], [vmem(shape, BF16)])[0]
+    block = local(
+        functools.partial(ordered_kernel, column),
+        [block, *column.gather(block)],
+        [vmem(shape, BF16)],
+        [vmem((n_y,) + shape, F32)],
+    )[0]
     image_q, image_k, gram = local(
-        functools.partial(assemble_kernel, rank, (rows_q, rows_k)),
-        [blocks.reshape(flat, LANES)],
+        functools.partial(assemble_kernel, line, rank, (rows_q, rows_k)),
+        [block, *line.gather(block)],
         [vmem((rank, rows_q), BF16), vmem((rank, rows_k), BF16), vmem((rank, 2 * rank), F32)],
+        [vmem((flat, LANES), BF16)],
     )
 
     gram_pair = core.send(gram, 1)
     operands = (image_q, image_k, merged_q, merged_k)
     got = core.send(project(core, True, half, *operands), 1)
     kept = project(core, False, half, *operands)
-    gram = local(total_kernel, [gram, gram_pair], [vmem(gram.shape, F32)])[0]
-    grams = [gram, *across.gather(gram)]
-    kept, sent = split(kept, [got], plane)
-    inverse = local(
+    kept, sent, gram = split(kept, got, gram, gram_pair, plane, across)
+    received = plane.scatter(sent)
+    block = local(sum_kernel, [kept, *received], [vmem(kept.shape, BF16)])[0]
+    blocks = [block, *line.gather(block)]
+    inverse, growth = local(
         functools.partial(inverse_kernel, across),
-        grams,
-        [vmem((2 * rank, 2 * rank), F32)],
-        [vmem((len(grams), rank, 2 * rank), F32)],
+        [gram, *received[: n_x - 1]],
+        [vmem((2 * rank, 2 * rank), F32), pltpu.SMEM((1,), F32)],
+        [vmem((n_x, rank, 2 * rank), F32)],
         flops=1 << 32,
-        after=[kept],
-    )[0]
+        after=[block],
+    )
     basis_q, basis_k = local(
         functools.partial(basis_kernel, 1.0 / n_dp),
         [inverse, image_q, image_k],
         [vmem((rows_q, rank), BF16), vmem((rows_k, rank), BF16)],
     )
-    piece = (kept.shape[0] // n_z, kept.shape[1])
-    blocks = local(
-        stack_kernel, [kept, *plane.scatter(sent)], [vmem((n_z,) + piece, BF16)], after=[basis_k]
+
+    copies = local(
+        functools.partial(finish_kernel, line),
+        [inverse, *blocks],
+        [vmem((plane.size,) + block.shape, BF16)],
+        [vmem((n_z,) + block.shape, F32)],
     )[0]
-    blocks = lax.all_to_all(blocks, "z", 0, 0)
-    blocks = local(finish_kernel, [inverse, blocks], [vmem(blocks.shape, BF16)])[0]
-
-    blocks = lax.all_to_all(blocks, "z", 0, 0).reshape(kept.shape)
-    copies = local(copies_kernel, [blocks], [vmem((plane.size,) + blocks.shape, BF16)])[0]
+
     own = lax.all_to_all(copies, ("y", "x"), 0, 0).reshape(half, 2 * rank)
     pieces = [own, core.send(own, 1)]
-    error_q, error_k, new_q, new_k = refresh(
-        core, padded, pieces, basis_q, basis_k, merged_q, merged_k
-    )
+    results = refresh(core, padded, pieces, basis_q, basis_k, merged_q, merged_k)
+
+    def careful(_):
+        return in_float32(grad_query, grad_key, error_query, error_key, factor_query, factor_key)
+
+    fine = growth[0] == 0.0
+    error_q, error_k, new_q, new_k = lax.cond(fine, tuple, careful, results)
     return error_q[None, None], error_k[None, None], new_q.T[None], new_k.T[None]
 
 

time: 95.1 us -> 90.8 us (0.955)
  blocking collectives: 54.3 us -> 11.5 us
  waiting for transfers between devices: 4.03 us -> 25.9 us
  starting transfers between devices: 5.61 us -> 20.3 us
  Pallas kernels: 30.1 us -> 31.6 us
    all_to_all x4 -> x0, blocking collectives: 43.8 us -> none  [the longest x2 25.8 us: body(): blocks = lax.all_to_all(blocks, ('z', 'y'), 0, 0)]
    ppermute x7 -> x16, waiting for transfers between devices: 4.03 us -> 25.9 us  [send(): return lax.ppermute(x, AXES, pairs)]
    ppermute x7 -> x16, starting transfers between devices: 5.61 us -> 20.3 us  [send(): return lax.ppermute(x, AXES, pairs)]
    all_to_all x1, blocking collectives: 10.5 us -> 11.5 us  [body(): own = lax.all_to_all(copies, ('y', 'x'), 0, 0).reshape(half, 2 * rank)]
    pallas_call x11 -> x10, Pallas kernels: 9.01 us -> 9.8 us  [local(): pl.pallas_call(run, in_specs=[whole()] * n_in + [pl.BlockSpec(memory_spac...]
  transfers between devices with their start and end apart: 7 -> 16, of which waited for: 3 -> 10; matrix products, arithmetic and copies ran while one was open for 0% -> 0% of each run, Pallas kernels for 7% -> 8%
where the time goes in v3:
time: 90.8 us; the launch traced here: 90.6 us
  Pallas kernels  31.6 us (35%)
  waiting for transfers between devices  25.9 us (29%)
  starting transfers between devices  20.3 us (22%)
  blocking collectives  11.5 us (13%)
  between operations  1.02 us (1%)
    ppermute x16, waiting for transfers between devices, send(): return lax.ppermute(x, AXES, pairs)  25.9 us
    ppermute x16, starting transfers between devices, send(): return lax.ppermute(x, AXES, pairs)  20.3 us
    pallas_call x1, Pallas kernels, images(): pl.pallas_call(functools.partial(image_kernel, group, tile, 2), in_specs=...  12.7 us
    all_to_all x1, blocking collectives, body(): own = lax.all_to_all(copies, ('y', 'x'), 0, 0).reshape(half, 2 * rank)  11.5 us
    pallas_call x10, Pallas kernels, local(): pl.pallas_call(run, in_specs=[whole()] * n_in + [pl.BlockSpec(memory_spac...  9.8 us
    pallas_call x1, Pallas kernels, refresh(): pl.pallas_call(functools.partial(refresh_kernel, core, tiles_q, tile), gr...  9.04 us
  transfers between devices with their start and end apart: 16, of which 10 were waited for; matrix products, arithmetic and copies ran while one was open for 0% of the time, Pallas kernels for 8%

profile of v3, /device:TPU:0, one launch (start us, length us, event | category | flops | bytes accessed | tf_op | source)
XLA Modules:
  0.0 90.6 jit_solution(10111317910873216327)
XLA Ops:
  0.6 12.7 %shard_map.93 = (bf16[1024,4608]{1,0:T(8,128)(2,1)S(1)}, bf16[512,4608]{1,0:T(8,128)(2,1)S(1)}, f32[192,128]{1,0:T(8,128)S(1)}, bf16[192,128]{1,0:T(8,128)(2,1)S...) custom-call(bf16[1024,4608]{1,0:T(8,128)(2,1)} %bitcast.124, bf16[512,4608]{1,0:T(8,128)(2,1)} %bitcast.126, ...), custom_call_target="tpu_custom_call" | custom-call | flops 3623878656 | bytes 28311552 | tf_op jit(solution)/shard_map/pallas_call | solution.py:175
  13.4 3.1 %collective-permute-start = (bf16[192,128]{1,0:T(8,128)(2,1)S(1)}, bf16[192,128]{1,0:T(8,128)(2,1)S(1)}, u32[]{:S(2)}, u32[]{:S(2)}) collective-permute-start(bf16[192,128]{1,0:T(8,128)(2,1)S(1)} %get-tuple-element.64), channel_id=1, source_target_pairs={{0,8},{1,9},{2,10},{3,11},{4,12},{5,13},{6,14},{7,15},{8,0},{9,1},... | collective-permute-start | bytes 147464 | tf_op jit(solution)/shard_map/ppermute | solution.py:92
  16.4 2.6 %collective-permute-start.1 = (bf16[192,128]{1,0:T(8,128)(2,1)S(1)}, bf16[192,128]{1,0:T(8,128)(2,1)S(1)}, u32[]{:S(2)}, u32[]{:S(2)}) collective-permute-start(bf16[192,128]{1,0:T(8,128)(2,1)S(1)} %get-tuple-element.65), channel_id=1, source_target_pairs={{0,16},{1,17},{2,18},{3,19},{4,20},{5,21},{6,22},{7,23},{8,24},{9,... | collective-permute-start | bytes 147464 | tf_op jit(solution)/shard_map/ppermute | solution.py:92
  19.0 0.0 collective-permute-start.2
  19.0 0.0 collective-permute-done.refs_1_
  19.1 3.3 %collective-permute-done.1.refs_2_ = bf16[192,128]{1,0:T(8,128)(2,1)S(1)} collective-permute-done((bf16[192,128]{1,0:T(8,128)(2,1)S(1)}, bf16[192,128]{1,0:T(8,128)(2,1)S(1)}, u32[]{:S(2)}, u32[]{:S(2)}) %collective-permute-start.1) | collective-permute-done | bytes 49184 | tf_op jit(solution)/shard_map/ppermute | solution.py:92
  22.4 2.6 %collective-permute-done.2.refs_3_ = bf16[192,128]{1,0:T(8,128)(2,1)S(1)} collective-permute-done((bf16[192,128]{1,0:T(8,128)(2,1)S(1)}, bf16[192,128]{1,0:T(8,128)(2,1)S(1)}, u32[]{:S(2)}, u32[]{:S(2)}) %collective-permute-start.2) | collective-permute-done | bytes 49184 | tf_op jit(solution)/shard_map/ppermute | solution.py:92
  25.0 1.6 %collective-permute-start.3 = (bf16[192,128]{1,0:T(8,128)(2,1)S(1)}, bf16[192,128]{1,0:T(8,128)(2,1)S(1)}, u32[]{:S(2)}, u32[]{:S(2)}) collective-permute-start(bf16[192,128]{1,0:T(8,128)(2,1)S(1)} %shard_map.94.refs_0_), channel_id=1, source_target_pairs={{0,4},{1,5},{2,6},{3,7},{4,0},{5,1},{6,2},{7,3},{8,12},{9,13},{10,... | collective-permute-start | bytes 147464 | tf_op jit(solution)/shard_map/ppermute | solution.py:92
  26.5 2.6 %collective-permute-done.3.refs_1_ = bf16[192,128]{1,0:T(8,128)(2,1)S(1)} collective-permute-done((bf16[192,128]{1,0:T(8,128)(2,1)S(1)}, bf16[192,128]{1,0:T(8,128)(2,1)S(1)}, u32[]{:S(2)}, u32[]{:S(2)}) %collective-permute-start.3) | collective-permute-done | bytes 49184 | tf_op jit(solution)/shard_map/ppermute | solution.py:92
  29.2 0.8 collective-permute-start.6
  29.9 0.0 collective-permute-start.5
  29.9 3.7 %collective-permute-start.4 = (bf16[192,128]{1,0:T(8,128)(2,1)S(1)}, bf16[192,128]{1,0:T(8,128)(2,1)S(1)}, u32[]{:S(2)}, u32[]{:S(2)}) collective-permute-start(bf16[192,128]{1,0:T(8,128)(2,1)S(1)} %shard_map.95.refs_0_), channel_id=1, source_target_pairs={{0,8},{1,9},{2,10},{3,11},{4,12},{5,13},{6,14},{7,15},{8,0},{9,1},... | collective-permute-start | bytes 147464 | tf_op jit(solution)/shard_map/ppermute | solution.py:92
  33.6 1.6 %collective-permute-done.6.refs_3_ = bf16[192,128]{1,0:T(8,128)(2,1)S(1)} collective-permute-done((bf16[192,128]{1,0:T(8,128)(2,1)S(1)}, bf16[192,128]{1,0:T(8,128)(2,1)S(1)}, u32[]{:S(2)}, u32[]{:S(2)}) %collective-permute-start.6) | collective-permute-done | bytes 49184 | tf_op jit(solution)/shard_map/ppermute | solution.py:92
  35.2 0.8 collective-permute-done.5.refs_2_
  36.0 0.0 collective-permute-done.4.refs_1_
  36.0 0.3 shard_map.96
  36.3 1.5 %shard_map.98 = bf16[2304,128]{1,0:T(8,128)(2,1)S(1)} custom-call(bf16[64,1024]{1,0:T(8,128)(2,1)S(1)} %get-tuple-element.67.refs_0_.refs_1_, bf16[64,512]{1,0:T(8,128)(2,1)S(1)} %get-tuple-element.68.refs_1_.refs_2_, bf16[1024,4608]{1,0:T(8,128)(2,1)S(1)} %get-tuple-element.69.refs_2_.refs_4_, bf16[512,4608]{1,0:T(8,128)(2,1)S(1)} %get-tuple-element.70.refs_3_.refs_5_), custom_call_target="tpu_custom_call" | custom-call | flops 1811939328 | bytes 14352384 | tf_op jit(solution)/shard_map/pallas_call | solution.py:38
  37.7 0.1 collective-permute-start.7
  37.8 0.5 collective-permute-start.8
  38.3 1.5 %shard_map.97.refs_0_ = f32[2304,128]{1,0:T(8,128)S(1)} custom-call(bf16[64,1024]{1,0:T(8,128)(2,1)S(1)} %get-tuple-element.67.refs_0_.refs_1_, bf16[64,512]{1,0:T(8,128)(2,1)S(1)} %get-tuple-element.68.refs_1_.refs_2_, bf16[1024,4608]{1,0:T(8,128)(2,1)S(1)} %get-tuple-element.69.refs_2_.refs_4_, bf16[512,4608]{1,0:T(8,128)(2,1)S(1)} %get-tuple-element.70.refs_3_.refs_5_), custom_call_target="tpu_custom_call" | custom-call | flops 1811939328 | bytes 14352384 | tf_op jit(solution)/shard_map/pallas_call | solution.py:38
  39.8 0.1 collective-permute-done.8.refs_3_
  39.9 0.0 collective-permute-done.7.refs_1_
  39.9 0.2 shard_map.99
  40.1 1.6 %collective-permute-start.9 = (bf16[768,128]{1,0:T(8,128)(2,1)S(1)}, bf16[768,128]{1,0:T(8,128)(2,1)S(1)}, u32[]{:S(2)}, u32[]{:S(2)}) collective-permute-start(bf16[768,128]{1,0:T(8,128)(2,1)S(1)} %get-tuple-element.73), channel_id=1, source_target_pairs={{0,2},{1,3},{2,0},{3,1},{4,6},{5,7},{6,4},{7,5},{8,10},{9,11},{10,... | collective-permute-start | bytes 589832 | tf_op jit(solution)/shard_map/ppermute | solution.py:92
  41.6 1.5 %collective-permute-start.10 = (bf16[576,128]{1,0:T(8,128)(2,1)S(1)}, bf16[576,128]{1,0:T(8,128)(2,1)S(1)}, u32[]{:S(2)}, u32[]{:S(2)}) collective-permute-start(bf16[576,128]{1,0:T(8,128)(2,1)S(1)} %get-tuple-element.75), channel_id=1, source_target_pairs={{0,4},{1,5},{2,6},{3,7},{4,0},{5,1},{6,2},{7,3},{8,12},{9,13},{10,... | collective-permute-start | bytes 442376 | tf_op jit(solution)/shard_map/ppermute | solution.py:92
  43.2 0.5 collective-permute-start.11
  43.6 3.6 %collective-permute-done.10.refs_2_ = bf16[576,128]{1,0:T(8,128)(2,1)S(1)} collective-permute-done((bf16[576,128]{1,0:T(8,128)(2,1)S(1)}, bf16[576,128]{1,0:T(8,128)(2,1)S(1)}, u32[]{:S(2)}, u32[]{:S(2)}) %collective-permute-start.10) | collective-permute-done | bytes 147488 | tf_op jit(solution)/shard_map/ppermute | solution.py:92
  47.3 4.0 %collective-permute-done.11.refs_3_ = bf16[576,128]{1,0:T(8,128)(2,1)S(1)} collective-permute-done((bf16[576,128]{1,0:T(8,128)(2,1)S(1)}, bf16[576,128]{1,0:T(8,128)(2,1)S(1)}, u32[]{:S(2)}, u32[]{:S(2)}) %collective-permute-start.11) | collective-permute-done | bytes 147488 | tf_op jit(solution)/shard_map/ppermute | solution.py:92
  51.2 0.0 collective-permute-done.9.refs_1_
  51.2 0.1 shard_map.100.refs_2_.refs_1_
  51.3 2.1 %collective-permute-start.14 = (bf16[576,128]{1,0:T(8,128)(2,1)S(1)}, bf16[576,128]{1,0:T(8,128)(2,1)S(1)}, u32[]{:S(2)}, u32[]{:S(2)}) collective-permute-start(bf16[576,128]{1,0:T(8,128)(2,1)S(1)} %shard_map.100.refs_2_.refs_1_), channel_id=1, source_target_pairs={{0,24},{1,25},{2,26},{3,27},{4,28},{5,29},{6,30},{7,31},{8,16},{9,... | collective-permute-start | bytes 442376 | tf_op jit(solution)/shard_map/ppermute | solution.py:92
  53.4 1.1 %collective-permute-start.13 = (bf16[576,128]{1,0:T(8,128)(2,1)S(1)}, bf16[576,128]{1,0:T(8,128)(2,1)S(1)}, u32[]{:S(2)}, u32[]{:S(2)}) collective-permute-start(bf16[576,128]{1,0:T(8,128)(2,1)S(1)} %shard_map.100.refs_2_.refs_1_), channel_id=1, source_target_pairs={{0,16},{1,17},{2,18},{3,19},{4,20},{5,21},{6,22},{7,23},{8,24},{9,... | collective-permute-start | bytes 442376 | tf_op jit(solution)/shard_map/ppermute | solution.py:92
  54.5 1.2 %collective-permute-start.12 = (bf16[576,128]{1,0:T(8,128)(2,1)S(1)}, bf16[576,128]{1,0:T(8,128)(2,1)S(1)}, u32[]{:S(2)}, u32[]{:S(2)}) collective-permute-start(bf16[576,128]{1,0:T(8,128)(2,1)S(1)} %shard_map.100.refs_2_.refs_1_), channel_id=1, source_target_pairs={{0,8},{1,9},{2,10},{3,11},{4,12},{5,13},{6,14},{7,15},{8,0},{9,1},... | collective-permute-start | bytes 442376 | tf_op jit(solution)/shard_map/ppermute | solution.py:92
  55.7 5.2 %shard_map.101 = (f32[128,128]{1,0:T(8,128)S(1)}, f32[1]{0:T(128)S(4)}) custom-call(f32[64,128]{1,0:T(8,128)S(1)} %get-tuple-element.72.refs_0_, bf16[768,128]{1,0:T(8,128)(2,1)S(1)} %collective-permute-done.9.refs_1_, bf16[576,128]{1,0:T(8,128)(2,1)S(1)} %shard_map.100.refs_2_.refs_1_), custom_call_target="tpu_custom_call" | custom-call | flops 4294967296 | bytes 229376 | tf_op jit(solution)/shard_map/pallas_call | solution.py:38
  61.0 0.0 slice-start
  61.0 0.0 slice-start.2
  61.0 0.0 copy-start.1
  61.0 0.0 copy-start.4
  61.0 0.0 collective-permute-done.14.refs_4_
  61.0 6.0 %collective-permute-done.13.refs_3_ = bf16[576,128]{1,0:T(8,128)(2,1)S(1)} collective-permute-done((bf16[576,128]{1,0:T(8,128)(2,1)S(1)}, bf16[576,128]{1,0:T(8,128)(2,1)S(1)}, u32[]{:S(2)}, u32[]{:S(2)}) %collective-permute-start.13) | collective-permute-done | bytes 147488 | tf_op jit(solution)/shard_map/ppermute | solution.py:92
  67.0 0.0 collective-permute-done.12.refs_2_
  67.0 0.5 shard_map.102
  67.5 11.5 %all_to_all.54 = bf16[4,576,128]{2,1,0:T(8,128)(2,1)S(1)} all-to-all(bf16[4,576,128]{2,1,0:T(8,128)(2,1)S(1)} %shard_map.102), channel_id=1, replica_groups=mesh['z'=4,'y'=2,'x'=2,'core'=2] {'y','x'}, dimensions={0} | all-to-all | bytes 1179648 | tf_op jit(solution)/shard_map/all_to_all | solution.py:544
  79.0 0.0 collective-permute-start.15
  79.1 0.6 shard_map.103
  79.6 1.4 %collective-permute-done.15.refs_1_ = bf16[2304,128]{1,0:T(8,128)(2,1)S(1)} collective-permute-done((bf16[2304,128]{1,0:T(8,128)(2,1)S(1)}, bf16[2304,128]{1,0:T(8,128)(2,1)S(1)}, u32[]{:S(2)}, u32[]{:S(2)}) %collective-permute-start.15) | collective-permute-done | bytes 589856 | tf_op jit(solution)/shard_map/ppermute | solution.py:92
  81.1 9.0 %shard_map.104 = (bf16[1024,4608]{1,0:T(8,128)(2,1)}, bf16[512,4608]{1,0:T(8,128)(2,1)}, bf16[64,4608]{1,0:T(8,128)(2,1)}, bf16[64,4608]{1,0:T(8,128)(2,1)}) custom-call(bf16[2304,128]{1,0:T(8,128)(2,1)S(1)} %bitcast.118, bf16[2304,128]{1,0:T(8,128)(2,1)S(1)} %collective-permute-done.15.refs_1_, bf16[1024,64]{1,0:T(8,128)(2,1)S(1)} %get-tuple-element.79.refs_2_, ...), custom_call_target="tpu_custom_call" | custom-call | flops 3623878656 | bytes 28311552 | tf_op jit(solution)/shard_map/pallas_call | solution.py:424
  90.2 0.3 conditional.1
  (12 shorter events, 0.1 us)
Async XLA Ops:
  13.4 5.7 %collective-permute-start = (bf16[192,128]{1,0:T(8,128)(2,1)S(1)}, bf16[192,128]{1,0:T(8,128)(2,1)S(1)}, u32[]{:S(2)}, u32[]{:S(2)}) collective-permute-start(bf16[192,128]{1,0:T(8,128)(2,1)S(1)} %get-tuple-element.64), channel_id=1, source_target_pairs={{0,8},{1,9},{2,10},{3,11},{4,12},{5,13},{6,14},{7,15},{8,0},{9,1},... | collective-permute-start | bytes 147464 | tf_op jit(solution)/shard_map/ppermute | solution.py:92
  16.4 5.9 %collective-permute-start.1 = (bf16[192,128]{1,0:T(8,128)(2,1)S(1)}, bf16[192,128]{1,0:T(8,128)(2,1)S(1)}, u32[]{:S(2)}, u32[]{:S(2)}) collective-permute-start(bf16[192,128]{1,0:T(8,128)(2,1)S(1)} %get-tuple-element.65), channel_id=1, source_target_pairs={{0,16},{1,17},{2,18},{3,19},{4,20},{5,21},{6,22},{7,23},{8,24},{9,... | collective-permute-start | bytes 147464 | tf_op jit(solution)/shard_map/ppermute | solution.py:92
  19.0 5.9 %collective-permute-start.2 = (bf16[192,128]{1,0:T(8,128)(2,1)S(1)}, bf16[192,128]{1,0:T(8,128)(2,1)S(1)}, u32[]{:S(2)}, u32[]{:S(2)}) collective-permute-start(bf16[192,128]{1,0:T(8,128)(2,1)S(1)} %get-tuple-element.66), channel_id=1, source_target_pairs={{0,24},{1,25},{2,26},{3,27},{4,28},{5,29},{6,30},{7,31},{8,16},{9,... | collective-permute-start | bytes 147464 | tf_op jit(solution)/shard_map/ppermute | solution.py:92
  25.0 4.2 %collective-permute-start.3 = (bf16[192,128]{1,0:T(8,128)(2,1)S(1)}, bf16[192,128]{1,0:T(8,128)(2,1)S(1)}, u32[]{:S(2)}, u32[]{:S(2)}) collective-permute-start(bf16[192,128]{1,0:T(8,128)(2,1)S(1)} %shard_map.94.refs_0_), channel_id=1, source_target_pairs={{0,4},{1,5},{2,6},{3,7},{4,0},{5,1},{6,2},{7,3},{8,12},{9,13},{10,... | collective-permute-start | bytes 147464 | tf_op jit(solution)/shard_map/ppermute | solution.py:92
  29.2 6.1 %collective-permute-start.6 = (bf16[192,128]{1,0:T(8,128)(2,1)S(1)}, bf16[192,128]{1,0:T(8,128)(2,1)S(1)}, u32[]{:S(2)}, u32[]{:S(2)}) collective-permute-start(bf16[192,128]{1,0:T(8,128)(2,1)S(1)} %shard_map.95.refs_0_), channel_id=1, source_target_pairs={{0,24},{1,25},{2,26},{3,27},{4,28},{5,29},{6,30},{7,31},{8,16},{9,... | collective-permute-start | bytes 147464 | tf_op jit(solution)/shard_map/ppermute | solution.py:92
  29.9 6.0 %collective-permute-start.5 = (bf16[192,128]{1,0:T(8,128)(2,1)S(1)}, bf16[192,128]{1,0:T(8,128)(2,1)S(1)}, u32[]{:S(2)}, u32[]{:S(2)}) collective-permute-start(bf16[192,128]{1,0:T(8,128)(2,1)S(1)} %shard_map.95.refs_0_), channel_id=1, source_target_pairs={{0,16},{1,17},{2,18},{3,19},{4,20},{5,21},{6,22},{7,23},{8,24},{9,... | collective-permute-start | bytes 147464 | tf_op jit(solution)/shard_map/ppermute | solution.py:92
  29.9 6.0 %collective-permute-start.4 = (bf16[192,128]{1,0:T(8,128)(2,1)S(1)}, bf16[192,128]{1,0:T(8,128)(2,1)S(1)}, u32[]{:S(2)}, u32[]{:S(2)}) collective-permute-start(bf16[192,128]{1,0:T(8,128)(2,1)S(1)} %shard_map.95.refs_0_), channel_id=1, source_target_pairs={{0,8},{1,9},{2,10},{3,11},{4,12},{5,13},{6,14},{7,15},{8,0},{9,1},... | collective-permute-start | bytes 147464 | tf_op jit(solution)/shard_map/ppermute | solution.py:92
  37.7 2.1 %collective-permute-start.7 = (bf16[2304,128]{1,0:T(8,128)(2,1)S(1)}, bf16[2304,128]{1,0:T(8,128)(2,1)S(1)}, u32[]{:S(2)}, u32[]{:S(2)}) collective-permute-start(bf16[2304,128]{1,0:T(8,128)(2,1)S(1)} %shard_map.98), channel_id=1, source_target_pairs={{0,1},{1,0},{2,3},{3,2},{4,5},{5,4},{6,7},{7,6},{8,9},{9,8},{10,11... | collective-permute-start | bytes 1769480 | tf_op jit(solution)/shard_map/ppermute | solution.py:92
  37.8 2.0 %collective-permute-start.8 = (f32[64,128]{1,0:T(8,128)S(1)}, f32[64,128]{1,0:T(8,128)S(1)}, u32[]{:S(2)}, u32[]{:S(2)}) collective-permute-start(f32[64,128]{1,0:T(8,128)S(1)} %get-tuple-element.71.refs_2_), channel_id=1, source_target_pairs={{0,1},{1,0},{2,3},{3,2},{4,5},{5,4},{6,7},{7,6},{8,9},{9,8},{10,11... | collective-permute-start | bytes 98312 | tf_op jit(solution)/shard_map/ppermute | solution.py:92
  40.1 11.1 %collective-permute-start.9 = (bf16[768,128]{1,0:T(8,128)(2,1)S(1)}, bf16[768,128]{1,0:T(8,128)(2,1)S(1)}, u32[]{:S(2)}, u32[]{:S(2)}) collective-permute-start(bf16[768,128]{1,0:T(8,128)(2,1)S(1)} %get-tuple-element.73), channel_id=1, source_target_pairs={{0,2},{1,3},{2,0},{3,1},{4,6},{5,7},{6,4},{7,5},{8,10},{9,11},{10,... | collective-permute-start | bytes 589832 | tf_op jit(solution)/shard_map/ppermute | solution.py:92
  41.6 5.6 %collective-permute-start.10 = (bf16[576,128]{1,0:T(8,128)(2,1)S(1)}, bf16[576,128]{1,0:T(8,128)(2,1)S(1)}, u32[]{:S(2)}, u32[]{:S(2)}) collective-permute-start(bf16[576,128]{1,0:T(8,128)(2,1)S(1)} %get-tuple-element.75), channel_id=1, source_target_pairs={{0,4},{1,5},{2,6},{3,7},{4,0},{5,1},{6,2},{7,3},{8,12},{9,13},{10,... | collective-permute-start | bytes 442376 | tf_op jit(solution)/shard_map/ppermute | solution.py:92
  43.2 8.0 %collective-permute-start.11 = (bf16[576,128]{1,0:T(8,128)(2,1)S(1)}, bf16[576,128]{1,0:T(8,128)(2,1)S(1)}, u32[]{:S(2)}, u32[]{:S(2)}) collective-permute-start(bf16[576,128]{1,0:T(8,128)(2,1)S(1)} %get-tuple-element.76), channel_id=1, source_target_pairs={{0,6},{1,7},{2,4},{3,5},{4,2},{5,3},{6,0},{7,1},{8,14},{9,15},{10,... | collective-permute-start | bytes 442376 | tf_op jit(solution)/shard_map/ppermute | solution.py:92
  51.3 9.7 %collective-permute-start.14 = (bf16[576,128]{1,0:T(8,128)(2,1)S(1)}, bf16[576,128]{1,0:T(8,128)(2,1)S(1)}, u32[]{:S(2)}, u32[]{:S(2)}) collective-permute-start(bf16[576,128]{1,0:T(8,128)(2,1)S(1)} %shard_map.100.refs_2_.refs_1_), channel_id=1, source_target_pairs={{0,24},{1,25},{2,26},{3,27},{4,28},{5,29},{6,30},{7,31},{8,16},{9,... | collective-permute-start | bytes 442376 | tf_op jit(solution)/shard_map/ppermute | solution.py:92
  53.4 13.6 %collective-permute-start.13 = (bf16[576,128]{1,0:T(8,128)(2,1)S(1)}, bf16[576,128]{1,0:T(8,128)(2,1)S(1)}, u32[]{:S(2)}, u32[]{:S(2)}) collective-permute-start(bf16[576,128]{1,0:T(8,128)(2,1)S(1)} %shard_map.100.refs_2_.refs_1_), channel_id=1, source_target_pairs={{0,16},{1,17},{2,18},{3,19},{4,20},{5,21},{6,22},{7,23},{8,24},{9,... | collective-permute-start | bytes 442376 | tf_op jit(solution)/shard_map/ppermute | solution.py:92
  54.5 12.5 %collective-permute-start.12 = (bf16[576,128]{1,0:T(8,128)(2,1)S(1)}, bf16[576,128]{1,0:T(8,128)(2,1)S(1)}, u32[]{:S(2)}, u32[]{:S(2)}) collective-permute-start(bf16[576,128]{1,0:T(8,128)(2,1)S(1)} %shard_map.100.refs_2_.refs_1_), channel_id=1, source_target_pairs={{0,8},{1,9},{2,10},{3,11},{4,12},{5,13},{6,14},{7,15},{8,0},{9,1},... | collective-permute-start | bytes 442376 | tf_op jit(solution)/shard_map/ppermute | solution.py:92
  61.0 29.1 %slice-start = ((s8[4718592]{0:T(1024)(128)(4,1)}), s8[4194304]{0:T(1024)(128)(4,1)S(1)}, s32[]{:S(2)}) async-start(s8[4718592]{0:T(1024)(128)(4,1)} %bitcast.127), calls=%async_computation.13 | async-start | bytes 8388608
  61.0 29.1 %slice-start.2 = ((s8[4718592]{0:T(1024)(128)(4,1)}), s8[4194304]{0:T(1024)(128)(4,1)S(1)}, s32[]{:S(2)}) async-start(s8[4718592]{0:T(1024)(128)(4,1)} %bitcast.130), calls=%async_computation.15 | async-start | bytes 8388608
  61.0 29.1 %copy-start.1 = (bf16[1,4608,64]{1,2,0:T(8,128)(2,1)S(1)}, bf16[1,4608,64]{1,2,0:T(8,128)(2,1)}, u32[]{:S(2)}) copy-start(bf16[1,4608,64]{1,2,0:T(8,128)(2,1)} %param.13) | copy-start | bytes 1769476
  61.0 29.1 %copy-start.4 = (bf16[1,4608,64]{1,2,0:T(8,128)(2,1)S(1)}, bf16[1,4608,64]{1,2,0:T(8,128)(2,1)}, u32[]{:S(2)}) copy-start(bf16[1,4608,64]{1,2,0:T(8,128)(2,1)} %param.14) | copy-start | bytes 1769476
  79.0 2.0 %collective-permute-start.15 = (bf16[2304,128]{1,0:T(8,128)(2,1)S(1)}, bf16[2304,128]{1,0:T(8,128)(2,1)S(1)}, u32[]{:S(2)}, u32[]{:S(2)}) collective-permute-start(bf16[2304,128]{1,0:T(8,128)(2,1)S(1)} %bitcast.117), channel_id=1, source_target_pairs={{0,1},{1,0},{2,3},{3,2},{4,5},{5,4},{6,7},{7,6},{8,9},{9,8},{10,11... | collective-permute-start | bytes 1769480 | tf_op jit(solution)/shard_map/ppermute | solution.py:92
  81.1 9.1 %slice-start.1 = ((s8[4718592]{0:T(1024)(128)(4,1)}), s8[524288]{0:T(1024)(128)(4,1)S(1)}, s32[]{:S(2)}) async-start(s8[4718592]{0:T(1024)(128)(4,1)} %bitcast.127), calls=%async_computation.14 | async-start | bytes 1048576
  81.1 9.1 %slice-start.3 = ((s8[4718592]{0:T(1024)(128)(4,1)}), s8[524288]{0:T(1024)(128)(4,1)S(1)}, s32[]{:S(2)}) async-start(s8[4718592]{0:T(1024)(128)(4,1)} %bitcast.130), calls=%async_computation.16 | async-start | bytes 1048576

commit v4 on v3

--- a/solution.py
+++ b/solution.py
@@ -173,7 +173,7 @@
     cut = (flat // group.size, LANES)
     outs = [vmem((r, d), BF16) for r in rows] + [vmem(cut, F32)] + [vmem(cut, BF16)] * (group.size - 1)
     return pl.pallas_call(
-        functools.partial(image_kernel, group, tile, 2),
+        functools.partial(image_kernel, group, tile, 4),
         in_specs=[pl.BlockSpec(memory_space=pltpu.HBM)] * len(ins),
         out_specs=[whole()] * len(outs),
         out_shape=outs,
@@ -367,29 +367,30 @@
 
 
 def finish_kernel(group, inverse, *refs):
-    blocks, (copies, held) = refs[:-2], refs[-2:]
+    blocks, (out, held) = refs[:-2], refs[-2:]
     for s, block in enumerate(blocks):
         held[group.source(s)] = wide(block[...])
     total = held[0]
     for j in range(1, len(blocks)):
         total = total + held[j]
-    new = lax.dot_general(
+    out[...] = lax.dot_general(
         total, inverse[...], (((1,), (1,)), ((), ())), precision=EXACT, preferred_element_type=F32
     ).astype(BF16)
-    for s in range(copies.shape[0]):
-        copies[s] = new
-
-
-def refresh_kernel(core, tiles_q, tile, *refs):
-    own, other, basis_q, basis_k, merged_q, merged_k, out_q, out_k, new_q, new_k, held, flat = refs
+
+
+def refresh_kernel(core, plane, tiles_q, tile, *refs):
+    pieces, refs = refs[: 2 * plane.size], refs[2 * plane.size :]
+    basis_q, basis_k, merged_q, merged_k, out_q, out_k, new_q, new_k, held, flat = refs
     rank, d = new_q.shape
     step = pl.program_id(0)
 
     @pl.when(step == 0)
     def _():
         half = held.shape[0] // 2
-        held[rows_at(core.pos(), half, 16)] = own[...]
-        held[rows_at(core.to(1), half, 16)] = other[...]
+        size = half // plane.size
+        for i, piece in enumerate(pieces):
+            first = core.to(i // plane.size) * half + plane.source(i % plane.size) * size
+            held[pl.ds(pl.multiple_of(first, 16), size)] = piece[...]
         for t in range(0, d, LANES):
             flat[:, t : t + LANES] = wide(held[t : t + LANES]).T.astype(BF16)
         new_q[...] = flat[:rank]
@@ -413,7 +414,7 @@
         update(step - tiles_q, merged_k, basis_k, flat.at[rank:], out_k)
 
 
-def refresh(core, padded, pieces, basis_q, basis_k, merged_q, merged_k):
+def refresh(core, plane, padded, pieces, basis_q, basis_k, merged_q, merged_k):
     rank = basis_q.shape[1]
     rows_q, d = merged_q.shape
     rows_k = merged_k.shape[0]
@@ -422,7 +423,7 @@
     ins = [*pieces, basis_q, basis_k, merged_q, merged_k]
     ins = [pltpu.with_memory_space_constraint(a, pltpu.VMEM) for a in ins]
     return pl.pallas_call(
-        functools.partial(refresh_kernel, core, tiles_q, tile),
+        functools.partial(refresh_kernel, core, plane, tiles_q, tile),
         grid=(tiles_q + tiles_k,),
         in_specs=[whole()] * len(ins),
         out_specs=[
@@ -534,16 +535,16 @@
         [vmem((rows_q, rank), BF16), vmem((rows_k, rank), BF16)],
     )
 
-    copies = local(
+    new = local(
         functools.partial(finish_kernel, line),
         [inverse, *blocks],
-        [vmem((plane.size,) + block.shape, BF16)],
+        [vmem(block.shape, BF16)],
         [vmem((n_z,) + block.shape, F32)],
     )[0]
 
-    own = lax.all_to_all(copies, ("y", "x"), 0, 0).reshape(half, 2 * rank)
-    pieces = [own, core.send(own, 1)]
-    results = refresh(core, padded, pieces, basis_q, basis_k, merged_q, merged_k)
+    pieces = [new, *plane.gather(new)]
+    pieces += [core.send(p, 1) for p in pieces]
+    results = refresh(core, plane, padded, pieces, basis_q, basis_k, merged_q, merged_k)
 
     def careful(_):
         return in_float32(grad_query, grad_key, error_query, error_key, factor_query, factor_key)

time: 90.8 us -> 86.5 us (0.953)
  blocking collectives: 11.5 us -> 0 us
  waiting for transfers between devices: 25.9 us -> 30.6 us
  starting transfers between devices: 20.3 us -> 24.4 us
  Pallas kernels: 31.6 us -> 30 us
    all_to_all x1 -> x0, blocking collectives: 11.5 us -> none  [body(): own = lax.all_to_all(copies, ('y', 'x'), 0, 0).reshape(half, 2 * rank)]
    ppermute x16 -> x22, waiting for transfers between devices: 25.9 us -> 30.6 us  [send(): return lax.ppermute(x, AXES, pairs)]
    ppermute x16 -> x22, starting transfers between devices: 20.3 us -> 24.4 us  [send(): return lax.ppermute(x, AXES, pairs)]
    pallas_call x2, Pallas kernels: 21.8 us -> 20.2 us  [the longest x1 11.1 us: images(): pl.pallas_call(functools.partial(image_kernel, group, tile, 4), in_specs=...]
  transfers between devices with their start and end apart: 16 -> 22, of which waited for: 10 -> 13; matrix products, arithmetic and copies ran while one was open for 0% -> 0% of each run, Pallas kernels for 8% -> 8%
where the time goes in v4:
time: 86.5 us; the launch traced here: 86.3 us
  waiting for transfers between devices  30.6 us (35%)
  Pallas kernels  30 us (35%)
  starting transfers between devices  24.4 us (28%)
  between operations  1.04 us (1%)
    ppermute x22, waiting for transfers between devices, send(): return lax.ppermute(x, AXES, pairs)  30.6 us
    ppermute x22, starting transfers between devices, send(): return lax.ppermute(x, AXES, pairs)  24.4 us
    pallas_call x1, Pallas kernels, images(): pl.pallas_call(functools.partial(image_kernel, group, tile, 4), in_specs=...  11.1 us
    pallas_call x10, Pallas kernels, local(): pl.pallas_call(run, in_specs=[whole()] * n_in + [pl.BlockSpec(memory_spac...  9.78 us
    pallas_call x1, Pallas kernels, refresh(): pl.pallas_call(functools.partial(refresh_kernel, core, plane, tiles_q, ti...  9.04 us
  transfers between devices with their start and end apart: 22, of which 13 were waited for; matrix products, arithmetic and copies ran while one was open for 0% of the time, Pallas kernels for 8%

profile of v4, /device:TPU:0, one launch (start us, length us, event | category | flops | bytes accessed | tf_op | source)
XLA Modules:
  0.0 86.3 jit_solution(11434501847692548645)
XLA Ops:
  0.6 11.1 %shard_map.93 = (bf16[1024,4608]{1,0:T(8,128)(2,1)S(1)}, bf16[512,4608]{1,0:T(8,128)(2,1)S(1)}, f32[192,128]{1,0:T(8,128)S(1)}, bf16[192,128]{1,0:T(8,128)(2,1)S...) custom-call(bf16[1024,4608]{1,0:T(8,128)(2,1)} %bitcast.119, bf16[512,4608]{1,0:T(8,128)(2,1)} %bitcast.121, ...), custom_call_target="tpu_custom_call" | custom-call | flops 3623878656 | bytes 28311552 | tf_op jit(solution)/shard_map/pallas_call | solution.py:175
  11.8 3.1 %collective-permute-start = (bf16[192,128]{1,0:T(8,128)(2,1)S(1)}, bf16[192,128]{1,0:T(8,128)(2,1)S(1)}, u32[]{:S(2)}, u32[]{:S(2)}) collective-permute-start(bf16[192,128]{1,0:T(8,128)(2,1)S(1)} %get-tuple-element.64), channel_id=1, source_target_pairs={{0,8},{1,9},{2,10},{3,11},{4,12},{5,13},{6,14},{7,15},{8,0},{9,1},... | collective-permute-start | bytes 147464 | tf_op jit(solution)/shard_map/ppermute | solution.py:92
  14.9 2.6 %collective-permute-start.1 = (bf16[192,128]{1,0:T(8,128)(2,1)S(1)}, bf16[192,128]{1,0:T(8,128)(2,1)S(1)}, u32[]{:S(2)}, u32[]{:S(2)}) collective-permute-start(bf16[192,128]{1,0:T(8,128)(2,1)S(1)} %get-tuple-element.65), channel_id=1, source_target_pairs={{0,16},{1,17},{2,18},{3,19},{4,20},{5,21},{6,22},{7,23},{8,24},{9,... | collective-permute-start | bytes 147464 | tf_op jit(solution)/shard_map/ppermute | solution.py:92
  17.5 0.0 collective-permute-start.2
  17.5 0.0 collective-permute-done.refs_1_
  17.5 3.3 %collective-permute-done.1.refs_2_ = bf16[192,128]{1,0:T(8,128)(2,1)S(1)} collective-permute-done((bf16[192,128]{1,0:T(8,128)(2,1)S(1)}, bf16[192,128]{1,0:T(8,128)(2,1)S(1)}, u32[]{:S(2)}, u32[]{:S(2)}) %collective-permute-start.1) | collective-permute-done | bytes 49184 | tf_op jit(solution)/shard_map/ppermute | solution.py:92
  20.8 2.6 %collective-permute-done.2.refs_3_ = bf16[192,128]{1,0:T(8,128)(2,1)S(1)} collective-permute-done((bf16[192,128]{1,0:T(8,128)(2,1)S(1)}, bf16[192,128]{1,0:T(8,128)(2,1)S(1)}, u32[]{:S(2)}, u32[]{:S(2)}) %collective-permute-start.2) | collective-permute-done | bytes 49184 | tf_op jit(solution)/shard_map/ppermute | solution.py:92
  23.4 1.6 %collective-permute-start.3 = (bf16[192,128]{1,0:T(8,128)(2,1)S(1)}, bf16[192,128]{1,0:T(8,128)(2,1)S(1)}, u32[]{:S(2)}, u32[]{:S(2)}) collective-permute-start(bf16[192,128]{1,0:T(8,128)(2,1)S(1)} %shard_map.94.refs_0_), channel_id=1, source_target_pairs={{0,4},{1,5},{2,6},{3,7},{4,0},{5,1},{6,2},{7,3},{8,12},{9,13},{10,... | collective-permute-start | bytes 147464 | tf_op jit(solution)/shard_map/ppermute | solution.py:92
  25.0 2.6 %collective-permute-done.3.refs_1_ = bf16[192,128]{1,0:T(8,128)(2,1)S(1)} collective-permute-done((bf16[192,128]{1,0:T(8,128)(2,1)S(1)}, bf16[192,128]{1,0:T(8,128)(2,1)S(1)}, u32[]{:S(2)}, u32[]{:S(2)}) %collective-permute-start.3) | collective-permute-done | bytes 49184 | tf_op jit(solution)/shard_map/ppermute | solution.py:92
  27.6 0.8 collective-permute-start.6
  28.4 0.0 collective-permute-start.5
  28.4 3.7 %collective-permute-start.4 = (bf16[192,128]{1,0:T(8,128)(2,1)S(1)}, bf16[192,128]{1,0:T(8,128)(2,1)S(1)}, u32[]{:S(2)}, u32[]{:S(2)}) collective-permute-start(bf16[192,128]{1,0:T(8,128)(2,1)S(1)} %shard_map.95.refs_0_), channel_id=1, source_target_pairs={{0,8},{1,9},{2,10},{3,11},{4,12},{5,13},{6,14},{7,15},{8,0},{9,1},... | collective-permute-start | bytes 147464 | tf_op jit(solution)/shard_map/ppermute | solution.py:92
  32.0 1.6 %collective-permute-done.6.refs_3_ = bf16[192,128]{1,0:T(8,128)(2,1)S(1)} collective-permute-done((bf16[192,128]{1,0:T(8,128)(2,1)S(1)}, bf16[192,128]{1,0:T(8,128)(2,1)S(1)}, u32[]{:S(2)}, u32[]{:S(2)}) %collective-permute-start.6) | collective-permute-done | bytes 49184 | tf_op jit(solution)/shard_map/ppermute | solution.py:92
  33.6 0.8 collective-permute-done.5.refs_2_
  34.4 0.3 shard_map.96
  34.7 1.5 %shard_map.98 = bf16[2304,128]{1,0:T(8,128)(2,1)S(1)} custom-call(bf16[64,1024]{1,0:T(8,128)(2,1)S(1)} %get-tuple-element.67.refs_0_.refs_1_, bf16[64,512]{1,0:T(8,128)(2,1)S(1)} %get-tuple-element.68.refs_1_.refs_2_, bf16[1024,4608]{1,0:T(8,128)(2,1)S(1)} %get-tuple-element.69.refs_2_.refs_10_, bf16[512,4608]{1,0:T(8,128)(2,1)S(1)} %get-tuple-element.70.refs_3_.refs_11_), custom_call_target="tpu_custom_call" | custom-call | flops 1811939328 | bytes 14352384 | tf_op jit(solution)/shard_map/pallas_call | solution.py:38
  36.2 0.1 collective-permute-start.7
  36.2 0.5 collective-permute-start.8
  36.7 1.5 %shard_map.97.refs_0_ = f32[2304,128]{1,0:T(8,128)S(1)} custom-call(bf16[64,1024]{1,0:T(8,128)(2,1)S(1)} %get-tuple-element.67.refs_0_.refs_1_, bf16[64,512]{1,0:T(8,128)(2,1)S(1)} %get-tuple-element.68.refs_1_.refs_2_, bf16[1024,4608]{1,0:T(8,128)(2,1)S(1)} %get-tuple-element.69.refs_2_.refs_10_, bf16[512,4608]{1,0:T(8,128)(2,1)S(1)} %get-tuple-element.70.refs_3_.refs_11_), custom_call_target="tpu_custom_call" | custom-call | flops 1811939328 | bytes 14352384 | tf_op jit(solution)/shard_map/pallas_call | solution.py:38
  38.2 0.1 collective-permute-done.8.refs_3_
  38.3 0.2 shard_map.99
  38.5 1.6 %collective-permute-start.9 = (bf16[768,128]{1,0:T(8,128)(2,1)S(1)}, bf16[768,128]{1,0:T(8,128)(2,1)S(1)}, u32[]{:S(2)}, u32[]{:S(2)}) collective-permute-start(bf16[768,128]{1,0:T(8,128)(2,1)S(1)} %get-tuple-element.73), channel_id=1, source_target_pairs={{0,2},{1,3},{2,0},{3,1},{4,6},{5,7},{6,4},{7,5},{8,10},{9,11},{10,... | collective-permute-start | bytes 589832 | tf_op jit(solution)/shard_map/ppermute | solution.py:92
  40.1 1.5 %collective-permute-start.10 = (bf16[576,128]{1,0:T(8,128)(2,1)S(1)}, bf16[576,128]{1,0:T(8,128)(2,1)S(1)}, u32[]{:S(2)}, u32[]{:S(2)}) collective-permute-start(bf16[576,128]{1,0:T(8,128)(2,1)S(1)} %get-tuple-element.75), channel_id=1, source_target_pairs={{0,4},{1,5},{2,6},{3,7},{4,0},{5,1},{6,2},{7,3},{8,12},{9,13},{10,... | collective-permute-start | bytes 442376 | tf_op jit(solution)/shard_map/ppermute | solution.py:92
  41.6 0.5 collective-permute-start.11
  42.1 3.6 %collective-permute-done.10.refs_2_ = bf16[576,128]{1,0:T(8,128)(2,1)S(1)} collective-permute-done((bf16[576,128]{1,0:T(8,128)(2,1)S(1)}, bf16[576,128]{1,0:T(8,128)(2,1)S(1)}, u32[]{:S(2)}, u32[]{:S(2)}) %collective-permute-start.10) | collective-permute-done | bytes 147488 | tf_op jit(solution)/shard_map/ppermute | solution.py:92
  45.7 4.0 %collective-permute-done.11.refs_3_ = bf16[576,128]{1,0:T(8,128)(2,1)S(1)} collective-permute-done((bf16[576,128]{1,0:T(8,128)(2,1)S(1)}, bf16[576,128]{1,0:T(8,128)(2,1)S(1)}, u32[]{:S(2)}, u32[]{:S(2)}) %collective-permute-start.11) | collective-permute-done | bytes 147488 | tf_op jit(solution)/shard_map/ppermute | solution.py:92
  49.6 0.1 shard_map.100.refs_2_.refs_1_
  49.7 2.1 %collective-permute-start.14 = (bf16[576,128]{1,0:T(8,128)(2,1)S(1)}, bf16[576,128]{1,0:T(8,128)(2,1)S(1)}, u32[]{:S(2)}, u32[]{:S(2)}) collective-permute-start(bf16[576,128]{1,0:T(8,128)(2,1)S(1)} %shard_map.100.refs_2_.refs_1_), channel_id=1, source_target_pairs={{0,24},{1,25},{2,26},{3,27},{4,28},{5,29},{6,30},{7,31},{8,16},{9,... | collective-permute-start | bytes 442376 | tf_op jit(solution)/shard_map/ppermute | solution.py:92
  51.8 1.1 %collective-permute-start.13 = (bf16[576,128]{1,0:T(8,128)(2,1)S(1)}, bf16[576,128]{1,0:T(8,128)(2,1)S(1)}, u32[]{:S(2)}, u32[]{:S(2)}) collective-permute-start(bf16[576,128]{1,0:T(8,128)(2,1)S(1)} %shard_map.100.refs_2_.refs_1_), channel_id=1, source_target_pairs={{0,16},{1,17},{2,18},{3,19},{4,20},{5,21},{6,22},{7,23},{8,24},{9,... | collective-permute-start | bytes 442376 | tf_op jit(solution)/shard_map/ppermute | solution.py:92
  53.0 1.2 %collective-permute-start.12 = (bf16[576,128]{1,0:T(8,128)(2,1)S(1)}, bf16[576,128]{1,0:T(8,128)(2,1)S(1)}, u32[]{:S(2)}, u32[]{:S(2)}) collective-permute-start(bf16[576,128]{1,0:T(8,128)(2,1)S(1)} %shard_map.100.refs_2_.refs_1_), channel_id=1, source_target_pairs={{0,8},{1,9},{2,10},{3,11},{4,12},{5,13},{6,14},{7,15},{8,0},{9,1},... | collective-permute-start | bytes 442376 | tf_op jit(solution)/shard_map/ppermute | solution.py:92
  54.2 5.2 %shard_map.101 = (f32[128,128]{1,0:T(8,128)S(1)}, f32[1]{0:T(128)S(4)}) custom-call(f32[64,128]{1,0:T(8,128)S(1)} %get-tuple-element.72.refs_0_, bf16[768,128]{1,0:T(8,128)(2,1)S(1)} %collective-permute-done.9.refs_1_, bf16[576,128]{1,0:T(8,128)(2,1)S(1)} %shard_map.100.refs_2_.refs_1_), custom_call_target="tpu_custom_call" | custom-call | flops 4294967296 | bytes 229376 | tf_op jit(solution)/shard_map/pallas_call | solution.py:38
  59.4 0.0 slice-start
  59.4 0.0 slice-start.2
  59.4 0.0 copy-start
  59.4 0.0 copy-start.3
  59.4 6.0 %collective-permute-done.13.refs_3_ = bf16[576,128]{1,0:T(8,128)(2,1)S(1)} collective-permute-done((bf16[576,128]{1,0:T(8,128)(2,1)S(1)}, bf16[576,128]{1,0:T(8,128)(2,1)S(1)}, u32[]{:S(2)}, u32[]{:S(2)}) %collective-permute-start.13) | collective-permute-done | bytes 147488 | tf_op jit(solution)/shard_map/ppermute | solution.py:92
  65.5 0.5 shard_map.102.refs_0_
  66.0 1.5 %collective-permute-start.17 = (bf16[576,128]{1,0:T(8,128)(2,1)S(1)}, bf16[576,128]{1,0:T(8,128)(2,1)S(1)}, u32[]{:S(2)}, u32[]{:S(2)}) collective-permute-start(bf16[576,128]{1,0:T(8,128)(2,1)S(1)} %shard_map.102.refs_0_), channel_id=1, source_target_pairs={{0,6},{1,7},{2,4},{3,5},{4,2},{5,3},{6,0},{7,1},{8,14},{9,15},{10,... | collective-permute-start | bytes 442376 | tf_op jit(solution)/shard_map/ppermute | solution.py:92
  67.4 1.5 %collective-permute-start.16 = (bf16[576,128]{1,0:T(8,128)(2,1)S(1)}, bf16[576,128]{1,0:T(8,128)(2,1)S(1)}, u32[]{:S(2)}, u32[]{:S(2)}) collective-permute-start(bf16[576,128]{1,0:T(8,128)(2,1)S(1)} %shard_map.102.refs_0_), channel_id=1, source_target_pairs={{0,4},{1,5},{2,6},{3,7},{4,0},{5,1},{6,2},{7,3},{8,12},{9,13},{10,... | collective-permute-start | bytes 442376 | tf_op jit(solution)/shard_map/ppermute | solution.py:92
  69.0 0.5 collective-permute-start.15
  69.5 4.1 %collective-permute-done.17.refs_3_ = bf16[576,128]{1,0:T(8,128)(2,1)S(1)} collective-permute-done((bf16[576,128]{1,0:T(8,128)(2,1)S(1)}, bf16[576,128]{1,0:T(8,128)(2,1)S(1)}, u32[]{:S(2)}, u32[]{:S(2)}) %collective-permute-start.17) | collective-permute-done | bytes 147488 | tf_op jit(solution)/shard_map/ppermute | solution.py:92
  73.6 1.6 %collective-permute-done.16.refs_2_ = bf16[576,128]{1,0:T(8,128)(2,1)S(1)} collective-permute-done((bf16[576,128]{1,0:T(8,128)(2,1)S(1)}, bf16[576,128]{1,0:T(8,128)(2,1)S(1)}, u32[]{:S(2)}, u32[]{:S(2)}) %collective-permute-start.16) | collective-permute-done | bytes 147488 | tf_op jit(solution)/shard_map/ppermute | solution.py:92
  75.1 0.5 collective-permute-start.19
  75.6 0.6 shard_map.103
  76.2 0.3 collective-permute-done.20.refs_6_
  76.5 0.2 collective-permute-done.19.refs_5_
  76.7 9.0 %shard_map.104 = (bf16[1024,4608]{1,0:T(8,128)(2,1)}, bf16[512,4608]{1,0:T(8,128)(2,1)}, bf16[64,4608]{1,0:T(8,128)(2,1)}, bf16[64,4608]{1,0:T(8,128)(2,1)}) custom-call(bf16[576,128]{1,0:T(8,128)(2,1)S(1)} %shard_map.102.refs_0_, bf16[576,128]{1,0:T(8,128)(2,1)S(1)} %collective-permute-done.15.refs_1_, ...), custom_call_target="tpu_custom_call" | custom-call | flops 3623878656 | bytes 28311552 | tf_op jit(solution)/shard_map/pallas_call | solution.py:425
  85.8 0.3 conditional.1
  (23 shorter events, 0.1 us)
Async XLA Ops:
  11.8 5.7 %collective-permute-start = (bf16[192,128]{1,0:T(8,128)(2,1)S(1)}, bf16[192,128]{1,0:T(8,128)(2,1)S(1)}, u32[]{:S(2)}, u32[]{:S(2)}) collective-permute-start(bf16[192,128]{1,0:T(8,128)(2,1)S(1)} %get-tuple-element.64), channel_id=1, source_target_pairs={{0,8},{1,9},{2,10},{3,11},{4,12},{5,13},{6,14},{7,15},{8,0},{9,1},... | collective-permute-start | bytes 147464 | tf_op jit(solution)/shard_map/ppermute | solution.py:92
  14.9 5.9 %collective-permute-start.1 = (bf16[192,128]{1,0:T(8,128)(2,1)S(1)}, bf16[192,128]{1,0:T(8,128)(2,1)S(1)}, u32[]{:S(2)}, u32[]{:S(2)}) collective-permute-start(bf16[192,128]{1,0:T(8,128)(2,1)S(1)} %get-tuple-element.65), channel_id=1, source_target_pairs={{0,16},{1,17},{2,18},{3,19},{4,20},{5,21},{6,22},{7,23},{8,24},{9,... | collective-permute-start | bytes 147464 | tf_op jit(solution)/shard_map/ppermute | solution.py:92
  17.5 5.9 %collective-permute-start.2 = (bf16[192,128]{1,0:T(8,128)(2,1)S(1)}, bf16[192,128]{1,0:T(8,128)(2,1)S(1)}, u32[]{:S(2)}, u32[]{:S(2)}) collective-permute-start(bf16[192,128]{1,0:T(8,128)(2,1)S(1)} %get-tuple-element.66), channel_id=1, source_target_pairs={{0,24},{1,25},{2,26},{3,27},{4,28},{5,29},{6,30},{7,31},{8,16},{9,... | collective-permute-start | bytes 147464 | tf_op jit(solution)/shard_map/ppermute | solution.py:92
  23.4 4.2 %collective-permute-start.3 = (bf16[192,128]{1,0:T(8,128)(2,1)S(1)}, bf16[192,128]{1,0:T(8,128)(2,1)S(1)}, u32[]{:S(2)}, u32[]{:S(2)}) collective-permute-start(bf16[192,128]{1,0:T(8,128)(2,1)S(1)} %shard_map.94.refs_0_), channel_id=1, source_target_pairs={{0,4},{1,5},{2,6},{3,7},{4,0},{5,1},{6,2},{7,3},{8,12},{9,13},{10,... | collective-permute-start | bytes 147464 | tf_op jit(solution)/shard_map/ppermute | solution.py:92
  27.6 6.1 %collective-permute-start.6 = (bf16[192,128]{1,0:T(8,128)(2,1)S(1)}, bf16[192,128]{1,0:T(8,128)(2,1)S(1)}, u32[]{:S(2)}, u32[]{:S(2)}) collective-permute-start(bf16[192,128]{1,0:T(8,128)(2,1)S(1)} %shard_map.95.refs_0_), channel_id=1, source_target_pairs={{0,24},{1,25},{2,26},{3,27},{4,28},{5,29},{6,30},{7,31},{8,16},{9,... | collective-permute-start | bytes 147464 | tf_op jit(solution)/shard_map/ppermute | solution.py:92
  28.4 6.0 %collective-permute-start.5 = (bf16[192,128]{1,0:T(8,128)(2,1)S(1)}, bf16[192,128]{1,0:T(8,128)(2,1)S(1)}, u32[]{:S(2)}, u32[]{:S(2)}) collective-permute-start(bf16[192,128]{1,0:T(8,128)(2,1)S(1)} %shard_map.95.refs_0_), channel_id=1, source_target_pairs={{0,16},{1,17},{2,18},{3,19},{4,20},{5,21},{6,22},{7,23},{8,24},{9,... | collective-permute-start | bytes 147464 | tf_op jit(solution)/shard_map/ppermute | solution.py:92
  28.4 6.0 %collective-permute-start.4 = (bf16[192,128]{1,0:T(8,128)(2,1)S(1)}, bf16[192,128]{1,0:T(8,128)(2,1)S(1)}, u32[]{:S(2)}, u32[]{:S(2)}) collective-permute-start(bf16[192,128]{1,0:T(8,128)(2,1)S(1)} %shard_map.95.refs_0_), channel_id=1, source_target_pairs={{0,8},{1,9},{2,10},{3,11},{4,12},{5,13},{6,14},{7,15},{8,0},{9,1},... | collective-permute-start | bytes 147464 | tf_op jit(solution)/shard_map/ppermute | solution.py:92
  36.2 2.1 %collective-permute-start.7 = (bf16[2304,128]{1,0:T(8,128)(2,1)S(1)}, bf16[2304,128]{1,0:T(8,128)(2,1)S(1)}, u32[]{:S(2)}, u32[]{:S(2)}) collective-permute-start(bf16[2304,128]{1,0:T(8,128)(2,1)S(1)} %shard_map.98), channel_id=1, source_target_pairs={{0,1},{1,0},{2,3},{3,2},{4,5},{5,4},{6,7},{7,6},{8,9},{9,8},{10,11... | collective-permute-start | bytes 1769480 | tf_op jit(solution)/shard_map/ppermute | solution.py:92
  36.2 2.0 %collective-permute-start.8 = (f32[64,128]{1,0:T(8,128)S(1)}, f32[64,128]{1,0:T(8,128)S(1)}, u32[]{:S(2)}, u32[]{:S(2)}) collective-permute-start(f32[64,128]{1,0:T(8,128)S(1)} %get-tuple-element.71.refs_2_), channel_id=1, source_target_pairs={{0,1},{1,0},{2,3},{3,2},{4,5},{5,4},{6,7},{7,6},{8,9},{9,8},{10,11... | collective-permute-start | bytes 98312 | tf_op jit(solution)/shard_map/ppermute | solution.py:92
  38.5 11.1 %collective-permute-start.9 = (bf16[768,128]{1,0:T(8,128)(2,1)S(1)}, bf16[768,128]{1,0:T(8,128)(2,1)S(1)}, u32[]{:S(2)}, u32[]{:S(2)}) collective-permute-start(bf16[768,128]{1,0:T(8,128)(2,1)S(1)} %get-tuple-element.73), channel_id=1, source_target_pairs={{0,2},{1,3},{2,0},{3,1},{4,6},{5,7},{6,4},{7,5},{8,10},{9,11},{10,... | collective-permute-start | bytes 589832 | tf_op jit(solution)/shard_map/ppermute | solution.py:92
  40.1 5.6 %collective-permute-start.10 = (bf16[576,128]{1,0:T(8,128)(2,1)S(1)}, bf16[576,128]{1,0:T(8,128)(2,1)S(1)}, u32[]{:S(2)}, u32[]{:S(2)}) collective-permute-start(bf16[576,128]{1,0:T(8,128)(2,1)S(1)} %get-tuple-element.75), channel_id=1, source_target_pairs={{0,4},{1,5},{2,6},{3,7},{4,0},{5,1},{6,2},{7,3},{8,12},{9,13},{10,... | collective-permute-start | bytes 442376 | tf_op jit(solution)/shard_map/ppermute | solution.py:92
  41.6 8.0 %collective-permute-start.11 = (bf16[576,128]{1,0:T(8,128)(2,1)S(1)}, bf16[576,128]{1,0:T(8,128)(2,1)S(1)}, u32[]{:S(2)}, u32[]{:S(2)}) collective-permute-start(bf16[576,128]{1,0:T(8,128)(2,1)S(1)} %get-tuple-element.76), channel_id=1, source_target_pairs={{0,6},{1,7},{2,4},{3,5},{4,2},{5,3},{6,0},{7,1},{8,14},{9,15},{10,... | collective-permute-start | bytes 442376 | tf_op jit(solution)/shard_map/ppermute | solution.py:92
  49.7 9.7 %collective-permute-start.14 = (bf16[576,128]{1,0:T(8,128)(2,1)S(1)}, bf16[576,128]{1,0:T(8,128)(2,1)S(1)}, u32[]{:S(2)}, u32[]{:S(2)}) collective-permute-start(bf16[576,128]{1,0:T(8,128)(2,1)S(1)} %shard_map.100.refs_2_.refs_1_), channel_id=1, source_target_pairs={{0,24},{1,25},{2,26},{3,27},{4,28},{5,29},{6,30},{7,31},{8,16},{9,... | collective-permute-start | bytes 442376 | tf_op jit(solution)/shard_map/ppermute | solution.py:92
  51.8 13.6 %collective-permute-start.13 = (bf16[576,128]{1,0:T(8,128)(2,1)S(1)}, bf16[576,128]{1,0:T(8,128)(2,1)S(1)}, u32[]{:S(2)}, u32[]{:S(2)}) collective-permute-start(bf16[576,128]{1,0:T(8,128)(2,1)S(1)} %shard_map.100.refs_2_.refs_1_), channel_id=1, source_target_pairs={{0,16},{1,17},{2,18},{3,19},{4,20},{5,21},{6,22},{7,23},{8,24},{9,... | collective-permute-start | bytes 442376 | tf_op jit(solution)/shard_map/ppermute | solution.py:92
  53.0 12.5 %collective-permute-start.12 = (bf16[576,128]{1,0:T(8,128)(2,1)S(1)}, bf16[576,128]{1,0:T(8,128)(2,1)S(1)}, u32[]{:S(2)}, u32[]{:S(2)}) collective-permute-start(bf16[576,128]{1,0:T(8,128)(2,1)S(1)} %shard_map.100.refs_2_.refs_1_), channel_id=1, source_target_pairs={{0,8},{1,9},{2,10},{3,11},{4,12},{5,13},{6,14},{7,15},{8,0},{9,1},... | collective-permute-start | bytes 442376 | tf_op jit(solution)/shard_map/ppermute | solution.py:92
  59.4 26.4 %slice-start = ((s8[4718592]{0:T(1024)(128)(4,1)}), s8[4194304]{0:T(1024)(128)(4,1)S(1)}, s32[]{:S(2)}) async-start(s8[4718592]{0:T(1024)(128)(4,1)} %bitcast.122), calls=%async_computation.12 | async-start | bytes 8388608
  59.4 26.4 %slice-start.2 = ((s8[4718592]{0:T(1024)(128)(4,1)}), s8[4194304]{0:T(1024)(128)(4,1)S(1)}, s32[]{:S(2)}) async-start(s8[4718592]{0:T(1024)(128)(4,1)} %bitcast.125), calls=%async_computation.14 | async-start | bytes 8388608
  59.4 26.4 %copy-start = (bf16[1,4608,64]{1,2,0:T(8,128)(2,1)S(1)}, bf16[1,4608,64]{1,2,0:T(8,128)(2,1)}, u32[]{:S(2)}) copy-start(bf16[1,4608,64]{1,2,0:T(8,128)(2,1)} %param.13) | copy-start | bytes 1769476
  59.4 26.4 %copy-start.3 = (bf16[1,4608,64]{1,2,0:T(8,128)(2,1)S(1)}, bf16[1,4608,64]{1,2,0:T(8,128)(2,1)}, u32[]{:S(2)}) copy-start(bf16[1,4608,64]{1,2,0:T(8,128)(2,1)} %param.14) | copy-start | bytes 1769476
  66.0 7.6 %collective-permute-start.17 = (bf16[576,128]{1,0:T(8,128)(2,1)S(1)}, bf16[576,128]{1,0:T(8,128)(2,1)S(1)}, u32[]{:S(2)}, u32[]{:S(2)}) collective-permute-start(bf16[576,128]{1,0:T(8,128)(2,1)S(1)} %shard_map.102.refs_0_), channel_id=1, source_target_pairs={{0,6},{1,7},{2,4},{3,5},{4,2},{5,3},{6,0},{7,1},{8,14},{9,15},{10,... | collective-permute-start | bytes 442376 | tf_op jit(solution)/shard_map/ppermute | solution.py:92
  67.4 7.7 %collective-permute-start.16 = (bf16[576,128]{1,0:T(8,128)(2,1)S(1)}, bf16[576,128]{1,0:T(8,128)(2,1)S(1)}, u32[]{:S(2)}, u32[]{:S(2)}) collective-permute-start(bf16[576,128]{1,0:T(8,128)(2,1)S(1)} %shard_map.102.refs_0_), channel_id=1, source_target_pairs={{0,4},{1,5},{2,6},{3,7},{4,0},{5,1},{6,2},{7,3},{8,12},{9,13},{10,... | collective-permute-start | bytes 442376 | tf_op jit(solution)/shard_map/ppermute | solution.py:92
  69.0 6.2 %collective-permute-start.15 = (bf16[576,128]{1,0:T(8,128)(2,1)S(1)}, bf16[576,128]{1,0:T(8,128)(2,1)S(1)}, u32[]{:S(2)}, u32[]{:S(2)}) collective-permute-start(bf16[576,128]{1,0:T(8,128)(2,1)S(1)} %shard_map.102.refs_0_), channel_id=1, source_target_pairs={{0,2},{1,3},{2,0},{3,1},{4,6},{5,7},{6,4},{7,5},{8,10},{9,11},{10,... | collective-permute-start | bytes 442376 | tf_op jit(solution)/shard_map/ppermute | solution.py:92
  69.5 6.7 %collective-permute-start.18 = (bf16[576,128]{1,0:T(8,128)(2,1)S(1)}, bf16[576,128]{1,0:T(8,128)(2,1)S(1)}, u32[]{:S(2)}, u32[]{:S(2)}) collective-permute-start(bf16[576,128]{1,0:T(8,128)(2,1)S(1)} %shard_map.102.refs_0_), channel_id=1, source_target_pairs={{0,1},{1,0},{2,3},{3,2},{4,5},{5,4},{6,7},{7,6},{8,9},{9,8},{10,11... | collective-permute-start | bytes 442376 | tf_op jit(solution)/shard_map/ppermute | solution.py:92
  73.6 2.7 %collective-permute-start.21 = (bf16[576,128]{1,0:T(8,128)(2,1)S(1)}, bf16[576,128]{1,0:T(8,128)(2,1)S(1)}, u32[]{:S(2)}, u32[]{:S(2)}) collective-permute-start(bf16[576,128]{1,0:T(8,128)(2,1)S(1)} %collective-permute-done.17.refs_3_), channel_id=1, source_target_pairs={{0,1},{1,0},{2,3},{3,2},{4,5},{5,4},{6,7},{7,6},{8,9},{9,8},{10,11... | collective-permute-start | bytes 442376 | tf_op jit(solution)/shard_map/ppermute | solution.py:92
  75.1 1.4 %collective-permute-start.20 = (bf16[576,128]{1,0:T(8,128)(2,1)S(1)}, bf16[576,128]{1,0:T(8,128)(2,1)S(1)}, u32[]{:S(2)}, u32[]{:S(2)}) collective-permute-start(bf16[576,128]{1,0:T(8,128)(2,1)S(1)} %collective-permute-done.16.refs_2_), channel_id=1, source_target_pairs={{0,1},{1,0},{2,3},{3,2},{4,5},{5,4},{6,7},{7,6},{8,9},{9,8},{10,11... | collective-permute-start | bytes 442376 | tf_op jit(solution)/shard_map/ppermute | solution.py:92
  75.1 1.6 %collective-permute-start.19 = (bf16[576,128]{1,0:T(8,128)(2,1)S(1)}, bf16[576,128]{1,0:T(8,128)(2,1)S(1)}, u32[]{:S(2)}, u32[]{:S(2)}) collective-permute-start(bf16[576,128]{1,0:T(8,128)(2,1)S(1)} %collective-permute-done.15.refs_1_), channel_id=1, source_target_pairs={{0,1},{1,0},{2,3},{3,2},{4,5},{5,4},{6,7},{7,6},{8,9},{9,8},{10,11... | collective-permute-start | bytes 442376 | tf_op jit(solution)/shard_map/ppermute | solution.py:92
  76.7 9.1 %slice-start.1 = ((s8[4718592]{0:T(1024)(128)(4,1)}), s8[524288]{0:T(1024)(128)(4,1)S(1)}, s32[]{:S(2)}) async-start(s8[4718592]{0:T(1024)(128)(4,1)} %bitcast.122), calls=%async_computation.13 | async-start | bytes 1048576
  76.7 9.1 %slice-start.3 = ((s8[4718592]{0:T(1024)(128)(4,1)}), s8[524288]{0:T(1024)(128)(4,1)S(1)}, s32[]{:S(2)}) async-start(s8[4718592]{0:T(1024)(128)(4,1)} %bitcast.125), calls=%async_computation.15 | async-start | bytes 1048576
